TPU v7x, 32 devices: a whole 2x2x4 slice. The times are simulated.
32 devices in a mesh: fsdp: 4 (over z), context: 4 (over y, core), tensor: 2 (over x).
Axes of the slice: x: 2, y: 2, z: 4, core: 2. Of those that a mesh axis runs over, the one named last changes fastest.
Arguments:
- tokens: bfloat16 [4, 1024, 2048], P('fsdp', 'context', 'tensor'), may hold values from -6 to 6
- span_order: int32 [4, 2], replicated, may hold values from 0 to 7, as said below
- attn_gain: bfloat16 [2048], P('fsdp'), may hold values from 0.099609375 to 1.8984375
- w_query: bfloat16 [2048, 2048], P('fsdp', 'tensor'), may hold values from -0.125 to 0.125
- key_weight: bfloat16 [2048, 512], P('fsdp', 'tensor'), may hold values from -0.125 to 0.125
- value_weight: bfloat16 [2048, 512], P('fsdp', 'tensor'), may hold values from -0.125 to 0.125
- w_out: bfloat16 [2048, 2048], P('tensor', 'fsdp'), may hold values from -3 to 3
- mlp_gain: bfloat16 [2048], P('fsdp'), may hold values from 0.099609375 to 1.8984375
- w_gate: bfloat16 [2048, 8192], P('fsdp', 'tensor'), may hold values from -0.125 to 0.125
- w_up: bfloat16 [2048, 8192], P('fsdp', 'tensor'), may hold values from -0.125 to 0.125
- w_down: bfloat16 [8192, 2048], P('tensor', 'fsdp'), may hold values from -0.0625 to 0.0625
- out_grad: bfloat16 [4, 1024, 2048], P('fsdp', 'context', 'tensor'), may hold values from -6 to 6
Outputs:
- output: bfloat16 [4, 1024, 2048], P('fsdp', 'context', 'tensor')
- input_grad: bfloat16 [4, 1024, 2048], P('fsdp', 'context', 'tensor')
- attn_gain_grad: float32 [2048], P('fsdp')
- w_query_grad: float32 [2048, 2048], P('fsdp', 'tensor')
- w_key_grad: float32 [2048, 512], P('fsdp', 'tensor')
- w_value_grad: float32 [2048, 512], P('fsdp', 'tensor')
- w_out_grad: float32 [2048, 2048], P('tensor', 'fsdp')
- mlp_gain_grad: float32 [2048], P('fsdp')
- w_gate_grad: float32 [2048, 8192], P('fsdp', 'tensor')
- w_up_grad: float32 [2048, 8192], P('fsdp', 'tensor')
- w_down_grad: float32 [8192, 2048], P('tensor', 'fsdp')
Inputs may be any that keep to these rules, and one draw needn't show every extreme that they name: `span_order`: row c holds j and 2 * 4 - 1 - j for some j, in either order; the smaller entries of the rows are a permutation of 0 to 4 - 1.
All inputs are finite; a program needn't handle non-finite values.
Results may differ from a plain program's by a relative error of at most 0.019.
Values may be sent and summed in bfloat16 or wider, within the bound.
A program may use at most 384 MiB of HBM per device.

v0:
```python
import math

import jax
import jax.numpy as jnp
from jax import lax
from jax.sharding import PartitionSpec as P

HEAD_WIDTH = 64


EPS = 1e-05
NEG = -1e30


def rope_freqs(head_size):
    half_size = head_size // 2
    index = jnp.arange(half_size, dtype=jnp.float32)
    base_freq = jnp.exp(-(2.0 * index / head_size) * math.log(500000.0))
    wavelen = 2.0 * math.pi / base_freq
    smooth = (8192.0 / wavelen - 1.0) / 3.0
    blended = (1.0 - smooth) * base_freq / 32.0 + smooth * base_freq
    return jnp.where(
        wavelen > 8192.0, base_freq / 32.0, jnp.where(wavelen < 2048.0, base_freq, blended)
    )


def apply_rotary(values, cosine_table, sine_table):
    half_size = values.shape[-1] // 2
    first = values[..., :half_size]
    second = values[..., half_size:]
    return jnp.concatenate(
        [first * cosine_table - second * sine_table, second * cosine_table + first * sine_table], -1
    )


def unrotate(grads, cosine_table, sine_table):
    half_size = grads.shape[-1] // 2
    first = grads[..., :half_size]
    second = grads[..., half_size:]
    return jnp.concatenate(
        [first * cosine_table + second * sine_table, second * cosine_table - first * sine_table], -1
    )


def norm_forward(inputs, gain):
    scale_row = lax.rsqrt(jnp.mean(inputs * inputs, -1, keepdims=True) + EPS)
    normal = inputs * scale_row
    return (normal, scale_row, (normal * gain.astype(jnp.float32)).astype(jnp.bfloat16))


def norm_backward(grad_out, normal, scale_row, gain):
    scaled = grad_out * gain.astype(jnp.float32)
    gain_grad = jnp.sum(grad_out * normal, 0)
    inner = jnp.mean(scaled * normal, -1, keepdims=True)
    return (gain_grad, scale_row * (scaled - normal * inner))


def spread_grads(gain_grad, first_grad, second_grad, last_grad):
    pieces = (
        lax.psum_scatter(gain_grad, ("fsdp", "context"), scatter_dimension=0, tiled=True),
        lax.psum_scatter(first_grad, ("fsdp", "context"), scatter_dimension=0, tiled=True),
        lax.psum_scatter(second_grad, ("fsdp", "context"), scatter_dimension=0, tiled=True),
        lax.psum_scatter(last_grad, ("fsdp", "context"), scatter_dimension=1, tiled=True),
    )
    return (
        lax.all_gather(pieces[0].astype(jnp.bfloat16), "context", axis=0, tiled=True).astype(
            jnp.float32
        ),
        lax.all_gather(pieces[1].astype(jnp.bfloat16), "context", axis=0, tiled=True).astype(
            jnp.float32
        ),
        lax.all_gather(pieces[2].astype(jnp.bfloat16), "context", axis=0, tiled=True).astype(
            jnp.float32
        ),
        lax.all_gather(pieces[3].astype(jnp.bfloat16), "context", axis=1, tiled=True).astype(
            jnp.float32
        ),
    )


def shards(
    tokens,
    span_order,
    attn_gain,
    w_query,
    key_weight,
    value_weight,
    w_out,
    mlp_gain,
    w_gate,
    w_up,
    w_down,
    out_grad,
):
    whole_in, whole_cot = (
        lax.all_gather(tokens, "tensor", axis=2, tiled=True),
        lax.all_gather(out_grad, "tensor", axis=2, tiled=True),
    )
    resid_in = whole_in[0].astype(jnp.float32)
    tok_rows = resid_in.shape[0]
    feat_width = resid_in.shape[1]
    contexts = lax.axis_size("context")
    tensors = lax.axis_size("tensor")
    seq_len = tok_rows * contexts
    half_rows = tok_rows // 2
    slot_index = jnp.arange(seq_len, dtype=jnp.int32)
    owner_dev = slot_index // tok_rows
    inside = slot_index % tok_rows
    span_ids = span_order.reshape(-1)[owner_dev * 2 + inside // half_rows]
    pos_all = span_ids * half_rows + inside % half_rows
    pos_mine = lax.dynamic_slice_in_dim(pos_all, lax.axis_index("context") * tok_rows, tok_rows)
    allowed = pos_mine[:, None] >= pos_all[None, :]
    angles = pos_mine.astype(jnp.float32)[:, None] * rope_freqs(HEAD_WIDTH)[None, :]
    cosine_table = jnp.cos(angles)[:, None, :]
    sine_table = jnp.sin(angles)[:, None, :]
    factor = 1.0 / math.sqrt(HEAD_WIDTH)
    gain_one, query_w, key_matrix, value_matrix, out_w = (
        lax.all_gather(attn_gain, "fsdp", axis=0, tiled=True),
        lax.all_gather(w_query, "fsdp", axis=0, tiled=True),
        lax.all_gather(key_weight, "fsdp", axis=0, tiled=True),
        lax.all_gather(value_weight, "fsdp", axis=0, tiled=True),
        lax.all_gather(w_out, "fsdp", axis=1, tiled=True),
    )
    heads_q = query_w.shape[1] // HEAD_WIDTH
    heads_kv = key_matrix.shape[1] // HEAD_WIDTH
    group_size = heads_q // heads_kv
    normal_one, scale_one, first_normalized = norm_forward(resid_in, gain_one)
    query_lin = jnp.dot(first_normalized, query_w, preferred_element_type=jnp.float32)
    key_lin = jnp.dot(first_normalized, key_matrix, preferred_element_type=jnp.float32)
    query_rot = apply_rotary(
        query_lin.reshape(tok_rows, heads_q, HEAD_WIDTH), cosine_table, sine_table
    ).astype(jnp.bfloat16)
    key_rot = (
        apply_rotary(key_lin.reshape(tok_rows, heads_kv, HEAD_WIDTH), cosine_table, sine_table)
        .astype(jnp.bfloat16)
        .reshape(tok_rows, heads_kv * HEAD_WIDTH)
    )
    value_low = jnp.dot(first_normalized, value_matrix, preferred_element_type=jnp.float32).astype(
        jnp.bfloat16
    )
    keys_all, values_all = (
        lax.all_gather(key_rot, "context", axis=0, tiled=True),
        lax.all_gather(value_low, "context", axis=0, tiled=True),
    )
    query_heads = query_rot.reshape(tok_rows, heads_kv, group_size, HEAD_WIDTH).transpose(
        1, 2, 0, 3
    )
    heads_of_key = keys_all.reshape(seq_len, heads_kv, HEAD_WIDTH).transpose(1, 0, 2)
    heads_of_value = values_all.reshape(seq_len, heads_kv, HEAD_WIDTH).transpose(1, 0, 2)

    def scores_of(query_block, key_block):
        raw_scores = (
            jnp.einsum("gtd,ld->gtl", query_block, key_block, preferred_element_type=jnp.float32)
            * factor
        )
        return jnp.where(allowed[None], raw_scores, NEG)

    def attend(item):
        query_block, key_block, value_block = item
        scores = scores_of(query_block, key_block)
        top_score = jnp.max(scores, -1, keepdims=True)
        expo = jnp.exp(scores - top_score)
        total = jnp.sum(expo, -1, keepdims=True)
        weights = expo / total
        attended = jnp.einsum(
            "gtl,ld->gtd",
            weights.astype(jnp.bfloat16),
            value_block,
            preferred_element_type=jnp.float32,
        )
        return (attended, top_score + jnp.log(total))

    attended, log_sums = lax.map(attend, (query_heads, heads_of_key, heads_of_value))
    attn_low = (
        attended.transpose(2, 0, 1, 3).reshape(tok_rows, heads_q * HEAD_WIDTH).astype(jnp.bfloat16)
    )
    attn_sum = lax.psum(
        jnp.dot(attn_low, out_w, preferred_element_type=jnp.float32).astype(jnp.bfloat16), "tensor"
    ).astype(jnp.float32)
    resid_mid = resid_in + attn_sum
    gain_two, gate_w, up_w, down_w = (
        lax.all_gather(mlp_gain, "fsdp", axis=0, tiled=True),
        lax.all_gather(w_gate, "fsdp", axis=0, tiled=True),
        lax.all_gather(w_up, "fsdp", axis=0, tiled=True),
        lax.all_gather(w_down, "fsdp", axis=1, tiled=True),
    )
    normal_two, scale_two, normed_two = norm_forward(resid_mid, gain_two)
    gate_val = jnp.dot(normed_two, gate_w, preferred_element_type=jnp.float32)
    up_val = jnp.dot(normed_two, up_w, preferred_element_type=jnp.float32)
    sigmoid_gate = jax.nn.sigmoid(gate_val)
    hidden = (gate_val * sigmoid_gate * up_val).astype(jnp.bfloat16)
    mlp_sum = lax.psum(
        jnp.dot(hidden, down_w, preferred_element_type=jnp.float32).astype(jnp.bfloat16), "tensor"
    ).astype(jnp.float32)
    own_cols = feat_width // tensors
    col_start = lax.axis_index("tensor") * own_cols
    result = lax.dynamic_slice_in_dim(resid_mid + mlp_sum, col_start, own_cols, 1).astype(
        jnp.bfloat16
    )
    cot_low = whole_cot[0]
    cot_full = cot_low.astype(jnp.float32)
    down_grad = jnp.einsum("tf,td->fd", hidden, cot_low, preferred_element_type=jnp.float32)
    hidden_grad = jnp.einsum("td,fd->tf", cot_low, down_w, preferred_element_type=jnp.float32)
    gate_grad_low = (
        hidden_grad * up_val * sigmoid_gate * (1.0 + gate_val * (1.0 - sigmoid_gate))
    ).astype(jnp.bfloat16)
    up_grad_low = (hidden_grad * gate_val * sigmoid_gate).astype(jnp.bfloat16)
    gate_w_grad = jnp.einsum(
        "td,tf->df", normed_two, gate_grad_low, preferred_element_type=jnp.float32
    )
    up_w_grad = jnp.einsum("td,tf->df", normed_two, up_grad_low, preferred_element_type=jnp.float32)
    normed_two_part = jnp.einsum(
        "tf,df->td", gate_grad_low, gate_w, preferred_element_type=jnp.float32
    )
    normed_two_part = normed_two_part + jnp.einsum(
        "tf,df->td", up_grad_low, up_w, preferred_element_type=jnp.float32
    )
    normed_two_grad = lax.psum(normed_two_part.astype(jnp.bfloat16), "tensor").astype(jnp.float32)
    gain_two_grad, mid_from_norm = norm_backward(normed_two_grad, normal_two, scale_two, gain_two)
    resid_grad = cot_full + mid_from_norm
    mlp_parts = spread_grads(gain_two_grad, gate_w_grad, up_w_grad, down_grad)
    resid_grad_low = resid_grad.astype(jnp.bfloat16)
    out_w_grad = jnp.einsum(
        "th,td->hd", attn_low, resid_grad_low, preferred_element_type=jnp.float32
    )
    attn_grad_low = jnp.einsum(
        "td,hd->th", resid_grad_low, out_w, preferred_element_type=jnp.float32
    ).astype(jnp.bfloat16)
    attn_grad_heads = attn_grad_low.reshape(tok_rows, heads_kv, group_size, HEAD_WIDTH).transpose(
        1, 2, 0, 3
    )

    def attend_back(item):
        query_block, key_block, value_block, grad_block, log_block = item
        scores = scores_of(query_block, key_block)
        weights = jnp.exp(scores - log_block)
        weight_grad = jnp.einsum(
            "gtd,ld->gtl", grad_block, value_block, preferred_element_type=jnp.float32
        )
        value_grad = jnp.einsum(
            "gtl,gtd->ld",
            weights.astype(jnp.bfloat16),
            grad_block,
            preferred_element_type=jnp.float32,
        )
        inner = jnp.sum(weights * weight_grad, -1, keepdims=True)
        score_grad = (weights * (weight_grad - inner)).astype(jnp.bfloat16)
        query_grad = (
            jnp.einsum("gtl,ld->gtd", score_grad, key_block, preferred_element_type=jnp.float32)
            * factor
        )
        key_grad = (
            jnp.einsum("gtl,gtd->ld", score_grad, query_block, preferred_element_type=jnp.float32)
            * factor
        )
        return (query_grad, key_grad, value_grad)

    query_grad, key_grad, value_grad = lax.map(
        attend_back, (query_heads, heads_of_key, heads_of_value, attn_grad_heads, log_sums)
    )
    key_grad_all = key_grad.transpose(1, 0, 2).reshape(seq_len, heads_kv * HEAD_WIDTH)
    value_grad_all = value_grad.transpose(1, 0, 2).reshape(seq_len, heads_kv * HEAD_WIDTH)
    key_grad_mine, value_grad_mine = (
        lax.psum_scatter(
            key_grad_all.astype(jnp.bfloat16), "context", scatter_dimension=0, tiled=True
        ).astype(jnp.float32),
        lax.psum_scatter(
            value_grad_all.astype(jnp.bfloat16), "context", scatter_dimension=0, tiled=True
        ).astype(jnp.float32),
    )
    query_lin_grad = unrotate(
        query_grad.transpose(2, 0, 1, 3).reshape(tok_rows, heads_q, HEAD_WIDTH),
        cosine_table,
        sine_table,
    )
    query_lin_grad = query_lin_grad.reshape(tok_rows, heads_q * HEAD_WIDTH).astype(jnp.bfloat16)
    key_lin_grad = unrotate(
        key_grad_mine.reshape(tok_rows, heads_kv, HEAD_WIDTH), cosine_table, sine_table
    )
    key_lin_grad = key_lin_grad.reshape(tok_rows, heads_kv * HEAD_WIDTH).astype(jnp.bfloat16)
    value_lin_grad = value_grad_mine.astype(jnp.bfloat16)
    query_w_grad = jnp.einsum(
        "td,th->dh", first_normalized, query_lin_grad, preferred_element_type=jnp.float32
    )
    key_w_grad = jnp.einsum(
        "td,th->dh", first_normalized, key_lin_grad, preferred_element_type=jnp.float32
    )
    value_w_grad = jnp.einsum(
        "td,th->dh", first_normalized, value_lin_grad, preferred_element_type=jnp.float32
    )
    normed_one_part = jnp.einsum(
        "th,dh->td", query_lin_grad, query_w, preferred_element_type=jnp.float32
    )
    normed_one_part = normed_one_part + jnp.einsum(
        "th,dh->td", key_lin_grad, key_matrix, preferred_element_type=jnp.float32
    )
    normed_one_part = normed_one_part + jnp.einsum(
        "th,dh->td", value_lin_grad, value_matrix, preferred_element_type=jnp.float32
    )
    normed_one_grad = lax.psum(normed_one_part.astype(jnp.bfloat16), "tensor").astype(jnp.float32)
    gain_one_grad, in_from_norm = norm_backward(normed_one_grad, normal_one, scale_one, gain_one)
    input_full = resid_grad + in_from_norm
    input_result = lax.dynamic_slice_in_dim(input_full, col_start, own_cols, 1).astype(jnp.bfloat16)
    key_cols = key_matrix.shape[1]
    kv_w_grad = jnp.concatenate([key_w_grad, value_w_grad], 1)
    attn_parts = spread_grads(gain_one_grad, query_w_grad, kv_w_grad, out_w_grad)
    key_part = attn_parts[2][:, :key_cols]
    value_part = attn_parts[2][:, key_cols:]
    return (
        result[None],
        input_result[None],
        attn_parts[0],
        attn_parts[1],
        key_part,
        value_part,
        attn_parts[3],
        mlp_parts[0],
        mlp_parts[1],
        mlp_parts[2],
        mlp_parts[3],
    )


def solution(mesh):
    placed = (
        P("fsdp", "context", "tensor"),
        P(),
        P("fsdp"),
        P("fsdp", "tensor"),
        P("fsdp", "tensor"),
        P("fsdp", "tensor"),
        P("tensor", "fsdp"),
        P("fsdp"),
        P("fsdp", "tensor"),
        P("fsdp", "tensor"),
        P("tensor", "fsdp"),
        P("fsdp", "context", "tensor"),
    )
    return jax.shard_map(
        shards,
        mesh=mesh,
        in_specs=placed,
        out_specs=(
            P("fsdp", "context", "tensor"),
            P("fsdp", "context", "tensor"),
            P("fsdp"),
            P("fsdp", "tensor"),
            P("fsdp", "tensor"),
            P("fsdp", "tensor"),
            P("tensor", "fsdp"),
            P("fsdp"),
            P("fsdp", "tensor"),
            P("fsdp", "tensor"),
            P("tensor", "fsdp"),
        ),
        check_vma=False,
    )
```

profile of v0, /device:TPU:0, one launch (start us, length us, event | category | flops | bytes accessed | tf_op | source)
XLA Modules:
  0.0 2880.4 jit_solution(7994952283392840217)
XLA Ops:
  11.6 13.5 all-gather
  25.9 4.6 compare_select_fusion.1
  35.2 27.9 all-gather.23.cloned.1.call-done
  65.3 7.2 all_gather.67
  72.4 19.8 all-gather.25.cloned.1.call-done
  93.9 7.2 all_gather.69
  101.3 72.6 %all-gather.21.cloned.1.call-done = bf16[2048,1024]{1,0:T(8,128)(2,1)} async-done(((bf16[512,1024]{1,0:T(8,128)(2,1)}), bf16[2048,1024]{1,0:T(8,128)(2,1)}) %all-gather.21.cloned.1.call-update) | async-done | bytes 4194320 | tf_op jit(solution)/shard_map/all_gather | solution.py:119
  173.9 6.4 copy.37
  184.5 19.2 while.30
  203.7 50.9 %all-gather.27.cloned.1.call-done = bf16[1024,2048]{1,0:T(8,128)(2,1)} async-done(((bf16[1024,512]{1,0:T(8,128)(2,1)}), bf16[1024,2048]{1,0:T(8,128)(2,1)}) %all-gather.27.cloned.1.call-update) | async-done | bytes 4194320 | tf_op jit(solution)/shard_map/all_gather | solution.py:122
  254.6 4.6 convolution_convert_fusion.1
  262.2 12.1 all-gather.1
  274.3 23.7 all-reduce.8.cloned.1.call-done
  300.3 286.2 %all-gather.29.cloned.1.call-done = bf16[2048,4096]{1,0:T(8,128)(2,1)} async-done(((bf16[512,4096]{1,0:T(8,128)(2,1)}), bf16[2048,4096]{1,0:T(8,128)(2,1)}) %all-gather.29.cloned.1.call-update) | async-done | bytes 16777232 | tf_op jit(solution)/shard_map/all_gather | solution.py:183
  586.5 10.3 fusion.110
  596.8 276.3 %all-gather.31.cloned.1.call-done = bf16[2048,4096]{1,0:T(8,128)(2,1)} async-done(((bf16[512,4096]{1,0:T(8,128)(2,1)}), bf16[2048,4096]{1,0:T(8,128)(2,1)}) %all-gather.31.cloned.1.call-update) | async-done | bytes 16777232 | tf_op jit(solution)/shard_map/all_gather | solution.py:184
  873.1 10.2 fusion.111
  883.3 11.0 all-gather.35.cloned.1.call-done
  894.3 288.3 %all-gather.33.cloned.1.call-done = bf16[4096,2048]{1,0:T(8,128)(2,1)} async-done(((bf16[4096,512]{1,0:T(8,128)(2,1)}), bf16[4096,2048]{1,0:T(8,128)(2,1)}) %all-gather.33.cloned.1.call-update) | async-done | bytes 16777232 | tf_op jit(solution)/shard_map/all_gather | solution.py:185
  1182.6 13.8 multiply_convert_fusion.1
  1196.4 12.2 fusion.112
  1208.6 12.5 fusion.61
  1221.2 38.3 %all-reduce.10.cloned.1.call-done = bf16[256,2048]{1,0:T(8,128)(2,1)} async-done(((bf16[256,2048]{1,0:T(8,128)(2,1)}), bf16[256,2048]{1,0:T(8,128)(2,1)}) %all-reduce.10.cloned.1.call-update) | async-done | bytes 1048592 | tf_op jit(solution)/shard_map/psum | solution.py:218
  1269.3 35.4 %while.31 = (s32[]{:T(128)}, f32[4,4,256,64]{2,3,1,0:T(8,128)}, bf16[4,1024,64]{1,2,0:T(8,128)(2,1)}, bf16[4,1024,64]{1,2,0:T(8,128)(2,1)}, bf16[4,4,256,64]{2,3...) while((s32[]{:T(128)}, f32[4,4,256,64]{2,3,1,0:T(8,128)}, ...), condition=%wide.region_12.13_spmd.clone.clone, body=%wide.region_10.12_spmd.clone.sunk.clone | while | flops 687209472 | bytes 42637544 | solution.py:258
  1307.0 4.8 fusion.86
  1313.4 5.7 fusion.90
  1319.2 17.9 fusion.114
  1337.3 17.8 fusion.115
  1355.2 21.1 fusion.76
  1376.6 12.3 convolution_convert_fusion
  1404.3 56.3 %reduce-scatter.13.cloned.1.call-done = f32[128,1024]{1,0:T(8,128)} async-done(((f32[2048,1024]{1,0:T(8,128)}), f32[128,1024]{1,0:T(8,128)}) %reduce-scatter.13.cloned.1.call-update) | async-done | bytes 524304 | tf_op jit(solution)/shard_map/reduce_scatter | solution.py:61
  1462.5 107.2 %reduce-scatter.17.cloned.1.call-done = f32[1024,128]{1,0:T(8,128)} async-done(((f32[1024,2048]{1,0:T(8,128)}), f32[1024,128]{1,0:T(8,128)}) %reduce-scatter.17.cloned.1.call-update) | async-done | bytes 524304 | tf_op jit(solution)/shard_map/reduce_scatter | solution.py:63
  1571.5 334.7 %reduce-scatter.19.cloned.1.call-done = f32[128,4096]{1,0:T(8,128)} async-done(((f32[2048,4096]{1,0:T(8,128)}), f32[128,4096]{1,0:T(8,128)}) %reduce-scatter.19.cloned.1.call-update) | async-done | bytes 2097168 | tf_op jit(solution)/shard_map/reduce_scatter | solution.py:61
  1909.0 333.2 %reduce-scatter.21.cloned.1.call-done = f32[128,4096]{1,0:T(8,128)} async-done(((f32[2048,4096]{1,0:T(8,128)}), f32[128,4096]{1,0:T(8,128)}) %reduce-scatter.21.cloned.1.call-update) | async-done | bytes 2097168 | tf_op jit(solution)/shard_map/reduce_scatter | solution.py:62
  2245.0 333.0 %reduce-scatter.23.cloned.1.call-done = f32[4096,128]{1,0:T(8,128)} async-done(((f32[4096,2048]{1,0:T(8,128)}), f32[4096,128]{1,0:T(8,128)}) %reduce-scatter.23.cloned.1.call-update) | async-done | bytes 2097168 | tf_op jit(solution)/shard_map/reduce_scatter | solution.py:63
  2582.0 61.2 %all-reduce.12.cloned.1.call-done = (bf16[256,2048]{1,0:T(8,128)(2,1)}, bf16[256,2048]{1,0:T(8,128)(2,1)}) async-done(((bf16[256,2048]{1,0:T(8,128)(2,1)}, bf16[256,2048]{1,0:T(8,128)(2,1)}), (bf16[256,2048]{1,0:T(8,128)(2,1)}, bf16[256,2048]{1,0:T(8,128)(2,1)})) %all-reduce.12.cloned.1.call-update) | async-done | bytes 2097168 | tf_op jit(solution)/shard_map/psum | solution.py:192
  2643.1 4.0 fusion.69
  2647.1 62.4 %all-reduce.2 = (bf16[2048]{0:T(1024)(128)(2,1)S(1)}, bf16[2048]{0:T(1024)(128)(2,1)S(1)}) all-reduce(f32[2048]{0:T(1024)S(1)} %get-tuple-element.189, f32[2048]{0:T(1024)S(1)} %copy-done.31), channel_id=4, replica_groups=mesh['fsdp'=4,'context'=4,'tensor'=2] {'fsdp','context'}, use_global_device_ids=true, to_apply=%region_18.19.clone | all-reduce | flops 4096 | bytes 24576
  2709.6 5.2 all-gather.2
  2715.4 5.0 all-gather.3
  2726.6 10.0 all_gather.78
  2743.2 13.6 all-gather.39.cloned.1.call-done
  2759.6 33.8 %all-gather.41.cloned.1.call-done = bf16[512,4096]{1,0:T(8,128)(2,1)} async-done(((bf16[128,4096]{1,0:T(8,128)(2,1)}), bf16[512,4096]{1,0:T(8,128)(2,1)}) %all-gather.41.cloned.1.call-update) | async-done | bytes 4194320 | tf_op jit(solution)/shard_map/all_gather | solution.py:69
  2793.4 6.7 convert_element_type.260
  2800.1 29.8 %all-gather.43.cloned.1.call-done = bf16[512,4096]{1,0:T(8,128)(2,1)} async-done(((bf16[128,4096]{1,0:T(8,128)(2,1)}), bf16[512,4096]{1,0:T(8,128)(2,1)}) %all-gather.43.cloned.1.call-update) | async-done | bytes 4194320 | tf_op jit(solution)/shard_map/all_gather | solution.py:72
  2829.9 6.7 convert_element_type.262
  2836.6 29.9 %all-gather.45.cloned.1.call-done = bf16[4096,512]{1,0:T(8,128)(2,1)} async-done(((bf16[4096,128]{1,0:T(8,128)(2,1)}), bf16[4096,512]{1,0:T(8,128)(2,1)}) %all-gather.45.cloned.1.call-update) | async-done | bytes 4194320 | tf_op jit(solution)/shard_map/all_gather | solution.py:75
  2866.6 6.8 convert_element_type.264
  (283 shorter events, 135.5 us)
Async XLA Ops:
  7.2 4.4 copy-start.32
  7.2 17.9 copy-start.33
  7.2 26.4 all-gather.19.cloned.1.call-start
  7.9 55.2 %all-gather.23.cloned.1.call-start = ((), (), s32[]{:S(2)}) async-start(), calls=%async_computation.10 | async-start | bytes 1310720 | tf_op jit(solution)/shard_map/all_gather | solution.py:120
  8.7 83.5 %all-gather.25.cloned.1.call-start = ((), (), s32[]{:S(2)}) async-start(), calls=%async_computation.11 | async-start | bytes 1310720 | tf_op jit(solution)/shard_map/all_gather | solution.py:121
  9.4 164.5 %all-gather.21.cloned.1.call-start = ((), (), s32[]{:S(2)}) async-start(), calls=%async_computation.9 | async-start | bytes 5242880 | tf_op jit(solution)/shard_map/all_gather | solution.py:119
  10.0 244.7 %all-gather.27.cloned.1.call-start = ((), (), s32[]{:S(2)}) async-start(), calls=%async_computation.12 | async-start | bytes 5242880 | tf_op jit(solution)/shard_map/all_gather | solution.py:122
  10.6 287.4 %all-reduce.8.cloned.1.call-start = ((), (), s32[]{:S(2)}) async-start(), calls=%async_computation.13 | async-start | bytes 2097152 | tf_op jit(solution)/shard_map/psum | solution.py:177
  25.1 155.2 %copy-start.27 = (f32[4,1,512]{2,1,0:T(1,128)}, f32[4,1,512]{2,1,0:T(1,128)S(1)}, u32[]{:S(2)}) copy-start(f32[4,1,512]{2,1,0:T(1,128)S(1)} %convert_element_type.266) | copy-start | bytes 24580
  31.4 152.9 %copy-start.18 = (f32[256,32]{0,1:T(8,128)}, f32[256,32]{0,1:T(8,128)S(1)}, u32[]{:S(2)}) copy-start(f32[256,32]{0,1:T(8,128)S(1)} %get-tuple-element.256) | copy-start | bytes 98308
  31.5 152.9 %copy-start.20 = (f32[256,32]{0,1:T(8,128)}, f32[256,32]{0,1:T(8,128)S(1)}, u32[]{:S(2)}) copy-start(f32[256,32]{0,1:T(8,128)S(1)} %get-tuple-element.257) | copy-start | bytes 98308
  33.6 31.0 %copy-start = (bf16[1,256,2048]{2,1,0:T(8,128)(2,1)S(1)}, bf16[1,256,2048]{2,1,0:T(8,128)(2,1)}, u32[]{:S(2)}) copy-start(bf16[1,256,2048]{2,1,0:T(8,128)(2,1)} %all-gather.19.cloned.1.call-done) | copy-start | bytes 3145732
  35.2 145.1 %copy-start.29 = (f32[256]{0:T(256)}, f32[256]{0:T(256)S(1)}, u32[]{:S(2)}) copy-start(f32[256]{0:T(256)S(1)} %add_rsqrt_fusion.1) | copy-start | bytes 3076
  203.7 55.5 %copy-start.5 = (bf16[4,1024,64]{1,2,0:T(8,128)(2,1)}, bf16[4,1024,64]{1,2,0:T(8,128)(2,1)S(1)}, u32[]{:S(2)}) copy-start(bf16[4,1024,64]{1,2,0:T(8,128)(2,1)S(1)} %get-tuple-element.535) | copy-start | bytes 1572868
  203.7 55.5 %copy-start.7 = (bf16[4,4,256,64]{2,3,1,0:T(8,128)(2,1)}, bf16[4,4,256,64]{2,3,1,0:T(8,128)(2,1)S(1)}, u32[]{:S(2)}) copy-start(bf16[4,4,256,64]{2,3,1,0:T(8,128)(2,1)S(1)} %get-tuple-element.536) | copy-start | bytes 1572868
  203.7 55.5 %copy-start.13 = (bf16[4,1024,64]{1,2,0:T(8,128)(2,1)}, bf16[4,1024,64]{1,2,0:T(8,128)(2,1)S(1)}, u32[]{:S(2)}) copy-start(bf16[4,1024,64]{1,2,0:T(8,128)(2,1)S(1)} %get-tuple-element.558) | copy-start | bytes 1572868
  259.3 327.2 %all-gather.29.cloned.1.call-start = ((), (), s32[]{:S(2)}) async-start(), calls=%async_computation.14 | async-start | bytes 20971520 | tf_op jit(solution)/shard_map/all_gather | solution.py:183
  260.0 613.1 %all-gather.31.cloned.1.call-start = ((), (), s32[]{:S(2)}) async-start(), calls=%async_computation.15 | async-start | bytes 20971520 | tf_op jit(solution)/shard_map/all_gather | solution.py:184
  260.8 633.5 %all-gather.35.cloned.1.call-start = ((), (), s32[]{:S(2)}) async-start(), calls=%async_computation.17 | async-start | bytes 1572864 | tf_op jit(solution)/shard_map/all_gather | solution.py:97
  261.5 921.0 %all-gather.33.cloned.1.call-start = ((), (), s32[]{:S(2)}) async-start(), calls=%async_computation.16 | async-start | bytes 20971520 | tf_op jit(solution)/shard_map/all_gather | solution.py:185
  262.1 997.4 %all-reduce.10.cloned.1.call-start = ((), (), s32[]{:S(2)}) async-start(), calls=%async_computation.18 | async-start | bytes 2097152 | tf_op jit(solution)/shard_map/psum | solution.py:218
  300.3 572.8 %copy-start.4 = (bf16[256,2048]{1,0:T(8,128)(2,1)}, bf16[256,2048]{1,0:T(8,128)(2,1)S(1)}, u32[]{:S(2)}) copy-start(bf16[256,2048]{1,0:T(8,128)(2,1)S(1)} %multiply_convert_fusion.4) | copy-start | bytes 3145732
  1221.1 41.3 %copy-start.11 = (bf16[1,256,2048]{2,1,0:T(8,128)(2,1)S(1)}, bf16[1,256,2048]{2,1,0:T(8,128)(2,1)}, u32[]{:S(2)}) copy-start(bf16[1,256,2048]{2,1,0:T(8,128)(2,1)} %all-gather.35.cloned.1.call-done) | copy-start | bytes 3145732
  1221.1 170.4 %reduce-scatter.9.cloned.1.call-start = ((), (), s32[]{:S(2)}) async-start(), calls=%async_computation.19 | async-start | bytes 655360 | tf_op jit(solution)/shard_map/reduce_scatter | solution.py:264
  1262.3 3.6 copy-start.35
  1265.9 3.4 copy-start.6
  1265.9 3.4 copy-start.8
  1269.3 36.2 %copy-start.19 = (f32[256,32]{0,1:T(8,128)S(1)}, f32[256,32]{0,1:T(8,128)}, u32[]{:S(2)}) copy-start(f32[256,32]{0,1:T(8,128)} %copy-done.18) | copy-start | bytes 98308
  1269.3 36.2 %copy-start.21 = (f32[256,32]{0,1:T(8,128)S(1)}, f32[256,32]{0,1:T(8,128)}, u32[]{:S(2)}) copy-start(f32[256,32]{0,1:T(8,128)} %copy-done.20) | copy-start | bytes 98308
  1304.7 91.6 %reduce-scatter.11.cloned.1.call-start = ((), (), s32[]{:S(2)}) async-start(), calls=%async_computation.20 | async-start | bytes 655360 | tf_op jit(solution)/shard_map/reduce_scatter | solution.py:267
  1305.5 155.1 %reduce-scatter.13.cloned.1.call-start = ((), (), s32[]{:S(2)}) async-start(), calls=%async_computation.21 | async-start | bytes 8912896 | tf_op jit(solution)/shard_map/reduce_scatter | solution.py:61
  1306.9 4.8 copy-start.16
  1311.8 257.9 %reduce-scatter.17.cloned.1.call-start = ((), (), s32[]{:S(2)}) async-start(), calls=%async_computation.24 | async-start | bytes 8912896 | tf_op jit(solution)/shard_map/reduce_scatter | solution.py:63
  1319.1 587.2 %reduce-scatter.19.cloned.1.call-start = ((), (), s32[]{:S(2)}) async-start(), calls=%async_computation.26 | async-start | bytes 35651584 | tf_op jit(solution)/shard_map/reduce_scatter | solution.py:61
  1337.1 905.2 %reduce-scatter.21.cloned.1.call-start = ((), (), s32[]{:S(2)}) async-start(), calls=%async_computation.28 | async-start | bytes 35651584 | tf_op jit(solution)/shard_map/reduce_scatter | solution.py:62
  1355.1 1222.9 %reduce-scatter.23.cloned.1.call-start = ((), (), s32[]{:S(2)}) async-start(), calls=%async_computation.30 | async-start | bytes 35651584 | tf_op jit(solution)/shard_map/reduce_scatter | solution.py:63
  1376.3 1266.8 %all-reduce.12.cloned.1.call-start = ((), (), s32[]{:S(2)}) async-start(), calls=%async_computation.32 | async-start | bytes 4194304 | tf_op jit(solution)/shard_map/psum | solution.py:192
  1376.6 12.3 copy-start.10
  1376.6 12.3 copy-start.17
  1399.7 1325.9 %reduce-scatter.15.cloned.1.call-start = ((), (), s32[]{:S(2)}) async-start(), calls=%async_computation.23 | async-start | bytes 4456448 | tf_op jit(solution)/shard_map/reduce_scatter | solution.py:62
  1404.3 1336.1 %all-gather.37.cloned.1.call-start = ((), (), s32[]{:S(2)}) async-start(), calls=%async_computation.22 | async-start | bytes 1310720 | tf_op jit(solution)/shard_map/all_gather | solution.py:69
  1462.4 1294.4 %all-gather.39.cloned.1.call-start = ((), (), s32[]{:S(2)}) async-start(), calls=%async_computation.25 | async-start | bytes 1310720 | tf_op jit(solution)/shard_map/all_gather | solution.py:75
  1571.5 1221.9 %all-gather.41.cloned.1.call-start = ((), (), s32[]{:S(2)}) async-start(), calls=%async_computation.27 | async-start | bytes 5242880 | tf_op jit(solution)/shard_map/all_gather | solution.py:69
  1909.0 920.9 %all-gather.43.cloned.1.call-start = ((), (), s32[]{:S(2)}) async-start(), calls=%async_computation.29 | async-start | bytes 5242880 | tf_op jit(solution)/shard_map/all_gather | solution.py:72
  2245.0 335.7 %copy-start.36 = (u32[32]{0:T(128)S(1)}, u32[32]{0:T(128)}, u32[]{:S(2)}) copy-start(u32[32]{0:T(128)} %constant.173) | copy-start | bytes 388
  2245.0 621.6 %all-gather.45.cloned.1.call-start = ((), (), s32[]{:S(2)}) async-start(), calls=%async_computation.31 | async-start | bytes 5242880 | tf_op jit(solution)/shard_map/all_gather | solution.py:75
  2643.1 4.0 copy-start.31
  2709.5 13.8 copy-start.9
  (32 other events, 44.2 us)
Sparse Core Ops, SparseCore 0:
  9.6 23.9 all-gather.18
  35.2 27.9 all-gather.22
  64.7 27.4 all-gather.24
  93.6 80.2 all-gather.20
  175.3 79.2 all-gather.26
  259.4 38.5 all-reduce.7
  299.6 286.7 all-gather.28
  588.1 284.9 all-gather.30
  874.7 19.4 all-gather.34
  895.7 286.7 all-gather.32
  1221.2 38.2 all-reduce.9
  1304.8 21.6 reduce-scatter.8
  1329.7 21.6 reduce-scatter.10
  1355.9 104.6 reduce-scatter.12
  1465.1 104.5 reduce-scatter.16
  1573.8 332.4 reduce-scatter.18
  1910.4 331.8 reduce-scatter.20
  2246.4 331.5 reduce-scatter.22
  2580.9 62.1 all-reduce.11
  2647.9 72.9 reduce-scatter.14
  2722.5 17.8 all-gather.36
  2741.9 14.7 all-gather.38
  2758.9 34.4 all-gather.40
  2795.4 34.4 all-gather.42
  2831.5 35.0 all-gather.44
where the time goes:
time: 2890 us; the launch traced here: 2880 us
  waiting for transfers between devices  2440 us (84%)
  matrix products  198 us (7%)
  blocking collectives  122 us (4%)
  other arithmetic  80.4 us (3%)
    reduce_scatter x2, waiting for transfers between devices, spread_grads(): lax.psum_scatter(last_grad, ('fsdp', 'context'), scatter_dimension=1, til...  440 us
    reduce_scatter x2, waiting for transfers between devices, spread_grads(): lax.psum_scatter(first_grad, ('fsdp', 'context'), scatter_dimension=0, ti...  391 us
    reduce_scatter x2, waiting for transfers between devices, spread_grads(): lax.psum_scatter(second_grad, ('fsdp', 'context'), scatter_dimension=0, t...  333 us
    all_gather x1, waiting for transfers between devices, shards(): lax.all_gather(w_down, 'fsdp', axis=1, tiled=True)  288 us
    all_gather x1, waiting for transfers between devices, shards(): lax.all_gather(w_gate, 'fsdp', axis=0, tiled=True)  286 us
    all_gather x1, waiting for transfers between devices, shards(): lax.all_gather(w_up, 'fsdp', axis=0, tiled=True)  276 us
    all_gather x1, waiting for transfers between devices, shards(): lax.all_gather(w_query, 'fsdp', axis=0, tiled=True)  72.6 us
    unnamed x1, blocking collectives  62.4 us
  transfers between devices with their start and end apart: 25, of which 22 were waited for; matrix products, arithmetic and copies ran while one was open for 7% of the time, Pallas kernels for 0%

commit v1 on v0

v1 whole, which is shorter than its diff:
```python
import math

import jax
import jax.numpy as jnp
from jax import lax
from jax.sharding import PartitionSpec as P

HEAD_WIDTH = 64
EPS = 1e-05
NEG = -1e30
BF = jnp.bfloat16
F32 = jnp.float32


def rope_freqs(head_size):
    half_size = head_size // 2
    index = jnp.arange(half_size, dtype=jnp.float32)
    base_freq = jnp.exp(-(2.0 * index / head_size) * math.log(500000.0))
    wavelen = 2.0 * math.pi / base_freq
    smooth = (8192.0 / wavelen - 1.0) / 3.0
    blended = (1.0 - smooth) * base_freq / 32.0 + smooth * base_freq
    return jnp.where(
        wavelen > 8192.0, base_freq / 32.0, jnp.where(wavelen < 2048.0, base_freq, blended)
    )


def apply_rotary(values, cosine_table, sine_table):
    half_size = values.shape[-1] // 2
    first = values[..., :half_size]
    second = values[..., half_size:]
    return jnp.concatenate(
        [first * cosine_table - second * sine_table, second * cosine_table + first * sine_table], -1
    )


def dot(left, right):
    return jnp.dot(left, right, preferred_element_type=F32)


def dot_t(left, right):
    return lax.dot_general(left, right, (((1,), (1,)), ((), ())), preferred_element_type=F32)


def t_dot(left, right):
    return lax.dot_general(left, right, (((0,), (0,)), ((), ())), preferred_element_type=F32)


def pick(blocks, index, axis=0):
    return lax.dynamic_index_in_dim(blocks, index, axis, keepdims=False)


def place(whole, block, starts):
    return lax.dynamic_update_slice(whole, block, starts)


def shards(
    tokens,
    span_order,
    attn_gain,
    w_query,
    key_weight,
    value_weight,
    w_out,
    mlp_gain,
    w_gate,
    w_up,
    w_down,
    out_grad,
):
    planes = lax.axis_size("fsdp")
    contexts = lax.axis_size("context")
    z = lax.axis_index("fsdp")
    c = lax.axis_index("context")
    t = lax.axis_index("tensor")
    outers = contexts // 2
    o, k = c // 2, c % 2

    def swap_t(v):
        return lax.ppermute(v, "tensor", [(0, 1), (1, 0)])

    def swap_k(v):
        return lax.ppermute(v, "context", [(i, i ^ 1) for i in range(contexts)])

    def shift_o(v, by):
        return lax.ppermute(
            v,
            "context",
            [(i, ((i // 2 + by) % outers) * 2 + i % 2) for i in range(contexts)],
        )

    def shift_z(v, by):
        return lax.ppermute(v, "fsdp", [(i, (i + by) % planes) for i in range(planes)])

    def gather_context(piece):
        column = [piece] + [shift_o(piece, by) for by in range(1, outers)]
        other = swap_k(jnp.stack(column))
        found = []
        for by in range(outers):
            home = (o - by + outers) % outers
            found.append((home * 2 + k, column[by]))
            found.append((home * 2 + 1 - k, other[by]))
        return found

    def sum_context(part):
        shape = part.shape
        part = part.reshape(shape[0], outers, 2, *shape[2:])
        got = swap_k(pick(part, 1 - k, 2).astype(BF))
        total = pick(part, k, 2) + got.astype(F32)
        sums = pick(total, o, 1)
        for by in range(1, outers):
            sums = sums + shift_o(pick(total, (o + by) % outers, 1).astype(BF), by).astype(F32)
        return sums

    tok_own, cot_own = tokens[0], out_grad[0]
    rows, own_cols = tok_own.shape
    width = own_cols * 2
    depth = width // planes
    strip = depth // contexts
    units = w_gate.shape[1] // planes
    unit_strip = units // contexts

    def whole_cols(mine, theirs):
        return jnp.concatenate(
            [jnp.where(t == 0, mine, theirs), jnp.where(t == 0, theirs, mine)], -1
        )

    def own_half(v):
        return lax.dynamic_slice_in_dim(v, t * own_cols, own_cols, v.ndim - 1)

    def other_half(v):
        return lax.dynamic_slice_in_dim(v, (1 - t) * own_cols, own_cols, v.ndim - 1)

    resid_in = whole_cols(tok_own, swap_t(tok_own)).astype(F32)
    own_in = tok_own.astype(F32)

    query_cols = w_query.shape[1]
    kv_cols = key_weight.shape[1]
    qkv_own = jnp.concatenate([w_query, key_weight, value_weight], 1)
    qkv_strip = lax.dynamic_slice_in_dim(qkv_own, c * strip, strip, 0)
    out_rows = w_out.shape[0]
    out_strip_rows = out_rows // contexts
    out_strip = lax.dynamic_slice_in_dim(w_out, c * out_strip_rows, out_strip_rows, 0)
    gains_own = jnp.stack([attn_gain, mlp_gain])
    gains = place(jnp.zeros((2, width), BF), gains_own, (0, z * depth))
    qkv_w = place(jnp.zeros((width, qkv_own.shape[1]), BF), qkv_own, (z * depth, 0))
    out_w = place(jnp.zeros((out_rows, width), BF), w_out, (0, z * depth))
    for by in range(1, planes):
        home = (z - by + planes) % planes
        gains = place(gains, shift_z(gains_own, by), (0, home * depth))
        for index, piece in gather_context(shift_z(qkv_strip, by)):
            qkv_w = place(qkv_w, piece, (home * depth + index * strip, 0))
    for by in range(1, planes):
        home = (z - by + planes) % planes
        for index, piece in gather_context(shift_z(out_strip, by)):
            out_w = place(out_w, piece, (index * out_strip_rows, home * depth))
    gain_one, gain_two = gains[0].astype(F32), gains[1].astype(F32)

    cot_blocks = []
    for by in range(planes):
        piece = cot_own if by == 0 else shift_z(cot_own, by)
        cot_blocks.append(whole_cols(piece, swap_t(piece)))

    def unit_cols(v, plane):
        return lax.dynamic_slice_in_dim(v, plane * units, units, 1)

    gate_up = jnp.concatenate([unit_cols(w_gate, z), unit_cols(w_up, z)], 1)
    gate_up_w = place(jnp.zeros((width, 2 * units), BF), gate_up, (z * depth, 0))
    down_w = place(
        jnp.zeros((units, width), BF),
        lax.dynamic_slice_in_dim(w_down, z * units, units, 0),
        (0, z * depth),
    )
    gate_strip = lax.dynamic_slice_in_dim(w_gate, c * strip, strip, 0)
    up_strip = lax.dynamic_slice_in_dim(w_up, c * strip, strip, 0)
    for by in range(1, planes):
        goal = (z + by) % planes
        home = (z - by + planes) % planes
        piece = jnp.concatenate([unit_cols(gate_strip, goal), unit_cols(up_strip, goal)], 1)
        for index, found in gather_context(shift_z(piece, by)):
            gate_up_w = place(gate_up_w, found, (home * depth + index * strip, 0))
    for by in range(1, planes):
        goal = (z + by) % planes
        home = (z - by + planes) % planes
        piece = lax.dynamic_slice_in_dim(w_down, goal * units + c * unit_strip, unit_strip, 0)
        for index, found in gather_context(shift_z(piece, by)):
            down_w = place(down_w, found, (index * unit_strip, home * depth))

    heads_q = query_cols // HEAD_WIDTH
    heads_kv = kv_cols // HEAD_WIDTH
    group_size = heads_q // heads_kv
    half_rows = rows // 2
    scale_one = lax.rsqrt(jnp.mean(resid_in * resid_in, -1, keepdims=True) + EPS)
    first_normalized = (resid_in * scale_one * gain_one).astype(BF)
    qkv_lin = dot(first_normalized, qkv_w)

    slot = jnp.arange(rows, dtype=jnp.int32)

    def positions(index):
        spans = pick(span_order, index)
        return spans[slot // half_rows] * half_rows + slot % half_rows

    pos_mine = positions(c)
    angles = pos_mine.astype(F32)[:, None] * rope_freqs(HEAD_WIDTH)[None, :]
    cosine_table = jnp.cos(angles)[:, None, :]
    sine_table = jnp.sin(angles)[:, None, :]
    factor = 1.0 / math.sqrt(HEAD_WIDTH)
    qk_rot = apply_rotary(
        qkv_lin[:, : query_cols + kv_cols].reshape(rows, heads_q + heads_kv, HEAD_WIDTH),
        cosine_table,
        sine_table,
    ).astype(BF)
    query_rot = qk_rot[:, :heads_q]
    key_value = jnp.concatenate(
        [
            qk_rot[:, heads_q:].reshape(rows, kv_cols),
            qkv_lin[:, query_cols + kv_cols :].astype(BF),
        ],
        1,
    )
    found = gather_context(key_value)
    kv_all = jnp.concatenate([piece for _, piece in found], 0)
    pos_all = jnp.concatenate([positions(index) for index, _ in found], 0)
    seq_len = rows * contexts
    allowed = pos_mine[:, None] >= pos_all[None, :]
    query_heads = query_rot.reshape(rows, heads_kv, group_size, HEAD_WIDTH).transpose(1, 2, 0, 3)
    heads_of_key = kv_all[:, :kv_cols].reshape(seq_len, heads_kv, HEAD_WIDTH).transpose(1, 0, 2)
    heads_of_value = kv_all[:, kv_cols:].reshape(seq_len, heads_kv, HEAD_WIDTH).transpose(1, 0, 2)

    def scores_of(query_block, key_block):
        raw_scores = (
            jnp.einsum("gtd,ld->gtl", query_block, key_block, preferred_element_type=F32) * factor
        )
        return jnp.where(allowed[None], raw_scores, NEG)

    def attend(item):
        query_block, key_block, value_block = item
        scores = scores_of(query_block, key_block)
        top_score = jnp.max(scores, -1, keepdims=True)
        expo = jnp.exp(scores - top_score)
        total = jnp.sum(expo, -1, keepdims=True)
        weights = expo / total
        attended = jnp.einsum(
            "gtl,ld->gtd", weights.astype(BF), value_block, preferred_element_type=F32
        )
        return (attended, top_score + jnp.log(total))

    attended, log_sums = lax.map(attend, (query_heads, heads_of_key, heads_of_value))
    attn_low = attended.transpose(2, 0, 1, 3).reshape(rows, query_cols).astype(BF)
    attn_part = dot(attn_low, out_w)
    mid_own = own_in + own_half(attn_part) + swap_t(other_half(attn_part).astype(BF)).astype(F32)

    def row_total(v):
        part = jnp.sum(v, -1)
        return (part + swap_t(part))[:, None]

    gain_one_own, gain_two_own = own_half(gain_one), own_half(gain_two)
    scale_two = lax.rsqrt(row_total(mid_own * mid_own) / width + EPS)
    normal_two = mid_own * scale_two
    normed_own = (normal_two * gain_two_own).astype(BF)

    normed_blocks, hidden_blocks, unit_grad_blocks = [], [], []
    mlp_sum = None
    normed_grad = None
    for by in range(planes):
        piece = normed_own if by == 0 else shift_z(normed_own, by)
        normed = whole_cols(piece, swap_t(piece))
        cot = cot_blocks[by]
        gate_up_val = dot(normed, gate_up_w)
        gate_val, up_val = gate_up_val[:, :units], gate_up_val[:, units:]
        sigmoid_gate = jax.nn.sigmoid(gate_val)
        hidden = (gate_val * sigmoid_gate * up_val).astype(BF)
        hidden_grad = dot_t(cot, down_w)
        gate_grad = hidden_grad * up_val * sigmoid_gate * (1.0 + gate_val * (1.0 - sigmoid_gate))
        up_grad = hidden_grad * gate_val * sigmoid_gate
        unit_grad = jnp.concatenate([gate_grad.astype(BF), up_grad.astype(BF)], 1)
        normed_part = dot_t(unit_grad, gate_up_w)
        mlp_part = dot(hidden, down_w)
        grad_own = own_half(normed_part) + swap_t(other_half(normed_part).astype(BF)).astype(F32)
        mlp_own = own_half(mlp_part) + swap_t(other_half(mlp_part).astype(BF)).astype(F32)
        if by == 0:
            normed_grad, mlp_sum = grad_own, mlp_own
        else:
            normed_grad = normed_grad + shift_z(grad_own.astype(BF), planes - by).astype(F32)
            mlp_sum = mlp_sum + shift_z(mlp_own.astype(BF), planes - by).astype(F32)
        normed_blocks.append(normed)
        hidden_blocks.append(hidden)
        unit_grad_blocks.append(unit_grad)
    result = (mid_own + mlp_sum).astype(BF)

    normed_all = jnp.concatenate(normed_blocks, 0)
    hidden_all = jnp.concatenate(hidden_blocks, 0)
    unit_grad_all = jnp.concatenate(unit_grad_blocks, 0)
    cot_all = jnp.concatenate(cot_blocks, 0)
    gate_up_grad = t_dot(normed_all, unit_grad_all)
    down_grad = t_dot(hidden_all, cot_all)

    gate_up_sum = sum_context(gate_up_grad.reshape(planes, contexts, strip, 2 * units)).astype(BF)
    gate_strips = jnp.zeros((2, strip, planes * units), BF)
    for by in range(planes):
        home = (z - by + planes) % planes
        block = pick(gate_up_sum, (z + by) % planes)
        piece = block if by == 0 else shift_z(block, by)
        piece = jnp.stack([piece[:, :units], piece[:, units:]])
        gate_strips = place(gate_strips, piece, (0, 0, home * units))
    gate_out = jnp.zeros((depth, planes * units), F32)
    up_out = jnp.zeros((depth, planes * units), F32)
    for index, piece in gather_context(gate_strips):
        gate_out = place(gate_out, piece[0].astype(F32), (index * strip, 0))
        up_out = place(up_out, piece[1].astype(F32), (index * strip, 0))

    down_parts = down_grad.reshape(1, contexts, unit_strip, width)
    down_sum = sum_context(down_parts)[0].astype(BF)
    down_strips = jnp.zeros((planes, unit_strip, depth), BF)
    for by in range(planes):
        home = (z - by + planes) % planes
        block = lax.dynamic_slice_in_dim(down_sum, ((z + by) % planes) * depth, depth, 1)
        piece = block if by == 0 else shift_z(block, by)
        down_strips = place(down_strips, piece[None], (home, 0, 0))
    down_out = jnp.zeros((planes, contexts, unit_strip, depth), F32)
    for index, piece in gather_context(down_strips):
        down_out = place(down_out, piece[:, None].astype(F32), (0, index, 0, 0))
    down_out = down_out.reshape(planes * units, depth)

    def norm_backward(grad_out, normal, scale_row, gain):
        scaled = grad_out * gain
        gain_grad = jnp.sum(grad_out * normal, 0)
        inner = row_total(scaled * normal) / width
        return (gain_grad, scale_row * (scaled - normal * inner))

    gain_two_grad, mid_from_norm = norm_backward(normed_grad, normal_two, scale_two, gain_two_own)
    mid_grad = cot_own.astype(F32) + mid_from_norm
    mid_grad_own = mid_grad.astype(BF)
    mid_grad_low = whole_cols(mid_grad_own, swap_t(mid_grad_own))

    out_w_grad = t_dot(attn_low, mid_grad_low)
    attn_grad_heads = (
        dot_t(mid_grad_low, out_w)
        .astype(BF)
        .reshape(rows, heads_kv, group_size, HEAD_WIDTH)
        .transpose(1, 2, 0, 3)
    )

    def attend_back(item):
        query_block, key_block, value_block, grad_block, log_block = item
        scores = scores_of(query_block, key_block)
        weights = jnp.exp(scores - log_block)
        weight_grad = jnp.einsum(
            "gtd,ld->gtl", grad_block, value_block, preferred_element_type=F32
        )
        value_grad = jnp.einsum(
            "gtl,gtd->ld", weights.astype(BF), grad_block, preferred_element_type=F32
        )
        inner = jnp.sum(weights * weight_grad, -1, keepdims=True)
        score_grad = (weights * (weight_grad - inner)).astype(BF)
        query_grad = (
            jnp.einsum("gtl,ld->gtd", score_grad, key_block, preferred_element_type=F32) * factor
        )
        key_grad = (
            jnp.einsum("gtl,gtd->ld", score_grad, query_block, preferred_element_type=F32) * factor
        )
        return (query_grad, key_grad, value_grad)

    query_grad, key_grad, value_grad = lax.map(
        attend_back, (query_heads, heads_of_key, heads_of_value, attn_grad_heads, log_sums)
    )
    kv_grad = jnp.concatenate(
        [
            key_grad.transpose(1, 0, 2).reshape(seq_len, kv_cols),
            value_grad.transpose(1, 0, 2).reshape(seq_len, kv_cols),
        ],
        1,
    ).reshape(outers, 2, rows, 2 * kv_cols)
    kv_core = kv_grad[:, 0] + swap_k(kv_grad[:, 1].astype(BF)).astype(F32)
    kv_grad_own = kv_core[0]
    for by in range(1, outers):
        kv_grad_own = kv_grad_own + shift_o(kv_core[by].astype(BF), outers - by).astype(F32)
    qk_grad = jnp.concatenate(
        [
            query_grad.transpose(2, 0, 1, 3).reshape(rows, query_cols),
            kv_grad_own[:, :kv_cols],
        ],
        1,
    ).reshape(rows, heads_q + heads_kv, HEAD_WIDTH)
    qk_grad = apply_rotary(qk_grad, cosine_table, -sine_table)
    qkv_grad = jnp.concatenate(
        [qk_grad.reshape(rows, query_cols + kv_cols), kv_grad_own[:, kv_cols:]], 1
    ).astype(BF)
    qkv_w_grad = t_dot(first_normalized, qkv_grad)
    normed_one_part = dot_t(qkv_grad, qkv_w)
    normed_one_grad = own_half(normed_one_part) + swap_t(
        other_half(normed_one_part).astype(BF)
    ).astype(F32)
    gain_one_grad, in_from_norm = norm_backward(
        normed_one_grad, own_in * scale_one, scale_one, gain_one_own
    )
    input_result = (mid_grad + in_from_norm).astype(BF)

    def sum_planes(parts):
        total = pick(parts, z)
        for by in range(1, planes):
            total = total + shift_z(pick(parts, (z + by) % planes).astype(BF), by).astype(F32)
        return total

    out_sum = sum_context(out_w_grad.reshape(1, contexts, out_strip_rows, width))[0]
    out_sum = sum_planes(out_sum.reshape(out_strip_rows, planes, depth).transpose(1, 0, 2))
    out_out = jnp.zeros((out_rows, depth), F32)
    for index, piece in gather_context(out_sum.astype(BF)):
        out_out = place(out_out, piece.astype(F32), (index * out_strip_rows, 0))

    qkv_sum = sum_context(qkv_w_grad.reshape(planes, contexts, strip, -1))
    qkv_sum = sum_planes(qkv_sum)
    qkv_out = jnp.zeros((depth, qkv_own.shape[1]), F32)
    for index, piece in gather_context(qkv_sum.astype(BF)):
        qkv_out = place(qkv_out, piece.astype(F32), (index * strip, 0))

    gain_grads = lax.psum(jnp.stack([gain_one_grad, gain_two_grad]), ("fsdp", "context"))
    gain_all = whole_cols(gain_grads, swap_t(gain_grads))
    gain_out = lax.dynamic_slice_in_dim(gain_all, z * depth, depth, 1)
    return (
        result[None],
        input_result[None],
        gain_out[0],
        qkv_out[:, :query_cols],
        qkv_out[:, query_cols : query_cols + kv_cols],
        qkv_out[:, query_cols + kv_cols :],
        out_out,
        gain_out[1],
        gate_out,
        up_out,
        down_out,
    )


def solution(mesh):
    weight = P("fsdp", "tensor")
    turned = P("tensor", "fsdp")
    block = P("fsdp", "context", "tensor")
    gain = P("fsdp")
    return jax.shard_map(
        shards,
        mesh=mesh,
        in_specs=(
            block, P(), gain, weight, weight, weight, turned, gain, weight, weight, turned, block,
        ),
        out_specs=(
            block, block, gain, weight, weight, weight, turned, gain, weight, weight, turned,
        ),
        check_vma=False,
    )
```

time: 2890 us -> 971 us (0.34)
  waiting for transfers between devices: 2440 us -> 296 us
  local copies, waits for them, and re-layouts: 23.2 us -> 196 us
  starting transfers between devices: 1.47 us -> 160 us
  blocking collectives: 122 us -> 44.2 us
  matrix products: 198 us -> 159 us
    reduce_scatter x8 -> x0, waiting for transfers between devices: 1160 us -> none  [the longest x2 440 us: spread_grads(): lax.psum_scatter(last_grad, ('fsdp', 'context'), scatter_dimension=1, til...]
    all_gather x14 -> x0, waiting for transfers between devices: 1140 us -> none  [the longest x1 288 us: shards(): lax.all_gather(w_down, 'fsdp', axis=1, tiled=True)]
    ppermute x0 -> x107, waiting for transfers between devices: none -> 296 us  [the longest x39 147 us: shift_z(): lax.ppermute(v, 'fsdp', [(i, (i + by) % planes) for i in range(planes)])]
    ppermute x0 -> x107, starting transfers between devices: none -> 160 us  [the longest x39 114 us: shift_z(): lax.ppermute(v, 'fsdp', [(i, (i + by) % planes) for i in range(planes)])]
    psum x3 -> x0, waiting for transfers between devices: 123 us -> none  [the longest x1 61.2 us: shards(): lax.psum(jnp.dot(hidden, down_w, preferred_element_type=jnp.float32).asty...]
    dynamic_update_slice x0 -> x56, local copies, waits for them, and re-layouts: none -> 92 us  [place(): return lax.dynamic_update_slice(whole, block, starts)]
    unnamed x1 -> x0, blocking collectives: 62.4 us -> none
    all_gather x7 -> x0, blocking collectives: 60.1 us -> none  [the longest x1 13.5 us: shards(): lax.all_gather(attn_gain, 'fsdp', axis=0, tiled=True)]
  transfers between devices with their start and end apart: 25 -> 107, of which waited for: 22 -> 37; matrix products, arithmetic and copies ran while one was open for 7% -> 46% of each run, Pallas kernels for 0% -> 0%
where the time goes in v1:
time: 971 us; the launch traced here: 955 us
  waiting for transfers between devices  296 us (30%)
  local copies, waits for them, and re-layouts  196 us (20%)
  starting transfers between devices  160 us (16%)
  matrix products  159 us (16%)
  other arithmetic  96.4 us (10%)
  blocking collectives  44.2 us (5%)
    ppermute x39, waiting for transfers between devices, shift_z(): lax.ppermute(v, 'fsdp', [(i, (i + by) % planes) for i in range(planes)])  147 us
    ppermute x39, starting transfers between devices, shift_z(): lax.ppermute(v, 'fsdp', [(i, (i + by) % planes) for i in range(planes)])  114 us
    ppermute x22, waiting for transfers between devices, shift_o(): lax.ppermute(v, 'context', [(i, (i // 2 + by) % outers * 2 + i % 2) for i...  97 us
    dynamic_update_slice x56, local copies, waits for them, and re-layouts, place(): return lax.dynamic_update_slice(whole, block, starts)  92 us
    ppermute x24, waiting for transfers between devices, swap_t(): return lax.ppermute(v, 'tensor', [(0, 1), (1, 0)])  51.5 us
    dot_general x10, matrix products, dot_t(): lax.dot_general(left, right, (((1,), (1,)), ((), ())), preferred_element_...  46.7 us
    psum x1, blocking collectives, shards(): lax.psum(jnp.stack([gain_one_grad, gain_two_grad]), ('fsdp', 'context'))  44.2 us
    dot_general x10, matrix products, dot(): return jnp.dot(left, right, preferred_element_type=F32)  41.9 us
  transfers between devices with their start and end apart: 107, of which 37 were waited for; matrix products, arithmetic and copies ran while one was open for 46% of the time, Pallas kernels for 0%

profile of v1, /device:TPU:0, one launch (start us, length us, event | category | flops | bytes accessed | tf_op | source)
XLA Modules:
  0.0 954.9 jit_solution(13664319125846805947)
XLA Ops:
  54.4 8.9 collective-permute-done.36
  73.5 5.3 collective-permute-start.27
  87.1 7.4 collective-permute-done.27
  99.2 6.5 collective-permute-done.39
  118.0 12.4 %collective-permute-done.7 = bf16[128,1536]{1,0:T(8,128)(2,1)S(1)} collective-permute-done((bf16[128,1536]{1,0:T(8,128)(2,1)}, bf16[128,1536]{1,0:T(8,128)(2,1)S(1)}, u32[]{:S(2)}, u32[]{:S(2)}) %collective-permute-start.7) | collective-permute-done | bytes 393248 | tf_op jit(solution)/shard_map/ppermute | solution.py:92
  138.7 7.6 collective-permute-done.8
  146.3 17.5 %collective-permute-start.68 = (bf16[256,1024]{1,0:T(8,128)(2,1)S(1)}, bf16[256,1024]{1,0:T(8,128)(2,1)S(1)}, u32[]{:S(2)}, u32[]{:S(2)}) collective-permute-start(bf16[256,1024]{1,0:T(8,128)(2,1)S(1)} %bitcast.592), channel_id=1, source_target_pairs={{0,24},{8,0},{16,8},{24,16},{1,25},{9,1},{17,9},{25,17},{2,26},{10... | collective-permute-start | bytes 1572872 | tf_op jit(solution)/shard_map/ppermute | solution.py:92
  165.5 17.7 %collective-permute-start.33 = (bf16[128,2048]{1,0:T(8,128)(2,1)}, bf16[128,2048]{1,0:T(8,128)(2,1)S(1)}, u32[]{:S(2)}, u32[]{:S(2)}) collective-permute-start(bf16[128,2048]{1,0:T(8,128)(2,1)} %pad_maximum_fusion.23), channel_id=1, source_target_pairs={{0,24},{8,0},{16,8},{24,16},{1,25},{9,1},{17,9},{25,17},{2,26},{10... | collective-permute-start | bytes 1572872 | tf_op jit(solution)/shard_map/ppermute | solution.py:92
  216.8 12.4 %collective-permute-done.64 = bf16[256,1024]{1,0:T(8,128)(2,1)S(1)} collective-permute-done((bf16[256,1024]{1,0:T(8,128)(2,1)S(1)}, bf16[256,1024]{1,0:T(8,128)(2,1)S(1)}, u32[]{:S(2)}, u32[]{:S(2)}) %collective-permute-start.64) | collective-permute-done | bytes 524320 | tf_op jit(solution)/shard_map/ppermute | solution.py:92
  280.9 6.1 collective-permute-done.13
  296.9 16.0 %while.30 = (s32[]{:T(128)}, bf16[4,4,256,64]{2,3,1,0:T(8,128)(2,1)S(1)}, f32[4,4,256,1]{2,1,3,0:T(4,128)S(1)}, bf16[4,4,256,64]{2,3,1,0:T(8,128)(2,1)S(1)}, bf1...) while((s32[]{:T(128)}, ...), condition=%wide.region_4.5_spmd.clone.clone, body=%wide.region_1.4_spmd.clone.sunk.clone | while | flops 281279488 | bytes 14326881 | solution.py:247
  320.2 11.1 %collective-permute-done.24 = bf16[256,1024]{1,0:T(8,128)(2,1)S(1)} collective-permute-done((bf16[256,1024]{1,0:T(8,128)(2,1)S(1)}, bf16[256,1024]{1,0:T(8,128)(2,1)S(1)}, u32[]{:S(2)}, u32[]{:S(2)}) %collective-permute-start.24) | collective-permute-done | bytes 524320 | tf_op jit(solution)/shard_map/ppermute | solution.py:79
  340.9 6.9 collective-permute-done.26
  348.2 6.1 fusion.135
  356.1 6.3 fusion.155
  369.0 14.9 %collective-permute-done.50 = bf16[256,1024]{1,0:T(8,128)(2,1)S(1)} collective-permute-done((bf16[256,1024]{1,0:T(8,128)(2,1)S(1)}, bf16[256,1024]{1,0:T(8,128)(2,1)S(1)}, u32[]{:S(2)}, u32[]{:S(2)}) %collective-permute-start.50) | collective-permute-done | bytes 524320 | tf_op jit(solution)/shard_map/ppermute | solution.py:92
  389.9 6.1 fusion.147
  398.6 7.7 fusion.179
  406.3 6.0 collective-permute-done.51
  412.4 6.1 fusion.143
  421.0 7.4 fusion.171
  428.6 6.1 fusion.139
  438.3 7.0 fusion.163
  445.3 18.5 %fusion.59 = f32[2048,2048]{1,0:T(8,128)} fusion(bf16[256,1024]{1,0:T(8,128)(2,1)} %copy-done.68, bf16[256,1024]{1,0:T(8,128)(2,1)} %copy-done.67, bf16[256,1024]{1,0:T(8,128)(2,1)} %copy-done.70, bf16[256,1024]{1,0:T(8,128)(2,1)} %copy-done.69, bf16[256,1024]{1,0:T(8,128)(2,1)} %copy-done.72, bf16[256,1024]{1,0:T(8,128)(2,1)} %copy-done.71, ...), kind=kOutput, calls=%fused_computation.68 | convolution fusion | flops 8657043456 | bytes 25165824 | tf_op jit(solution)/shard_map/dot_general | solution.py:45
  477.1 7.3 fusion.90
  502.0 6.7 collective-permute-done.71
  509.4 14.6 %collective-permute-done.67 = bf16[256,1024]{1,0:T(8,128)(2,1)S(1)} collective-permute-done((bf16[256,1024]{1,0:T(8,128)(2,1)S(1)}, bf16[256,1024]{1,0:T(8,128)(2,1)S(1)}, u32[]{:S(2)}, u32[]{:S(2)}) %collective-permute-start.67) | collective-permute-done | bytes 524320 | tf_op jit(solution)/shard_map/ppermute | solution.py:92
  527.8 6.1 fusion.58
  544.1 7.3 collective-permute-done.73
  551.4 6.8 collective-permute-start.57
  565.5 37.6 %while.31 = (s32[]{:T(128)}, f32[4,4,256,64]{2,3,1,0:T(8,128)}, f32[4,1024,64]{1,2,0:T(8,128)}, f32[4,1024,64]{1,2,0:T(8,128)}, bf16[4,4,256,64]{2,3,1,0:T(8,128...) while((s32[]{:T(128)}, f32[4,4,256,64]{2,3,1,0:T(8,128)}, ...), condition=%wide.region_9.10_spmd.clone.clone, body=%wide.region_7.9_spmd.clone.sunk.clone | while | flops 687209472 | bytes 36346004 | solution.py:363
  628.0 5.7 collective-permute-done.75
  634.3 4.8 fusion.201
  644.6 8.2 collective-permute-done.76
  663.7 44.2 %psum.7 = f32[2,1024]{1,0:T(2,128)S(1)} all-reduce(f32[2,1024]{1,0:T(2,128)S(1)} %pad_maximum_fusion.32), channel_id=1, replica_groups=mesh['fsdp'=4,'context'=4,'tensor'=2] {'fsdp','context'}, use_global_device_ids=true, to_apply=%region_13.14 | all-reduce | flops 2048 | bytes 16384 | tf_op jit(solution)/shard_map/psum | solution.py:416
  714.9 10.9 %collective-permute-done.102 = bf16[256,512]{1,0:T(8,128)(2,1)S(1)} collective-permute-done((bf16[256,512]{1,0:T(8,128)(2,1)S(1)}, bf16[256,512]{1,0:T(8,128)(2,1)S(1)}, u32[]{:S(2)}, u32[]{:S(2)}) %collective-permute-start.102) | collective-permute-done | bytes 262176 | tf_op jit(solution)/shard_map/ppermute | solution.py:92
  729.6 6.4 collective-permute-done.103
  737.0 10.2 %bitcast_add_fusion = f32[4,2,128,2048]{3,2,1,0:T(8,128)} fusion(bf16[4,2,128,2048]{3,2,1,0:T(8,128)(2,1)} %collective-permute-done.93, f32[4,2,2,128,2048]{4,3,2,1,0:T(8,128)} %bitcast.580, s32[]{:T(128)S(6)} %select_n.756), kind=kLoop, calls=%fused_computation.63 | loop fusion | flops 4194304 | bytes 20971524 | tf_op jit(solution)/shard_map/add | solution.py:108
  747.2 8.4 collective-permute-done.87
  769.2 12.8 %collective-permute-start.88 = (bf16[256,512]{1,0:T(8,128)(2,1)S(1)}, bf16[256,512]{1,0:T(8,128)(2,1)S(1)}, u32[]{:S(2)}, u32[]{:S(2)}) collective-permute-start(bf16[256,512]{1,0:T(8,128)(2,1)S(1)} %bitcast.640), channel_id=1, source_target_pairs={{0,8},{8,16},{16,24},{24,0},{1,9},{9,17},{17,25},{25,1},{2,10},{10... | collective-permute-start | bytes 786440 | tf_op jit(solution)/shard_map/ppermute | solution.py:92
  792.1 33.4 %collective-permute-done.91 = bf16[256,512]{1,0:T(8,128)(2,1)S(1)} collective-permute-done((bf16[256,512]{1,0:T(8,128)(2,1)S(1)}, bf16[256,512]{1,0:T(8,128)(2,1)S(1)}, u32[]{:S(2)}, u32[]{:S(2)}) %collective-permute-start.91) | collective-permute-done | bytes 262176 | tf_op jit(solution)/shard_map/ppermute | solution.py:85
  825.7 5.9 bitcast_add_fusion.1
  841.9 12.4 %collective-permute-done.95 = bf16[128,2048]{1,0:T(8,128)(2,1)S(1)} collective-permute-done((bf16[128,2048]{1,0:T(8,128)(2,1)S(1)}, bf16[128,2048]{1,0:T(8,128)(2,1)S(1)}, u32[]{:S(2)}, u32[]{:S(2)}) %collective-permute-start.95) | collective-permute-done | bytes 524320 | tf_op jit(solution)/shard_map/ppermute | solution.py:92
  854.4 21.5 %collective-permute-done.96 = bf16[128,2048]{1,0:T(8,128)(2,1)S(1)} collective-permute-done((bf16[128,2048]{1,0:T(8,128)(2,1)S(1)}, bf16[128,2048]{1,0:T(8,128)(2,1)S(1)}, u32[]{:S(2)}, u32[]{:S(2)}) %collective-permute-start.96) | collective-permute-done | bytes 524320 | tf_op jit(solution)/shard_map/ppermute | solution.py:92
  884.3 11.7 %collective-permute-start.83 = (bf16[128,1536]{1,0:T(8,128)(2,1)S(1)}, bf16[128,1536]{1,0:T(8,128)(2,1)S(1)}, u32[]{:S(2)}, u32[]{:S(2)}) collective-permute-start(bf16[128,1536]{1,0:T(8,128)(2,1)S(1)} %get-tuple-element.223), channel_id=1, source_target_pairs={{0,24},{8,0},{16,8},{24,16},{1,25},{9,1},{17,9},{25,17},{2,26},{10... | collective-permute-start | bytes 1179656 | tf_op jit(solution)/shard_map/ppermute | solution.py:92
  897.5 26.0 %collective-permute-done.98 = bf16[2,128,4096]{2,1,0:T(8,128)(2,1)S(1)} collective-permute-done((bf16[2,128,4096]{2,1,0:T(8,128)(2,1)S(1)}, bf16[2,128,4096]{2,1,0:T(8,128)(2,1)S(1)}, u32[]{:S(2)}, u32[]{:S(2)}) %collective-permute-start.98) | collective-permute-done | bytes 2097184 | tf_op jit(solution)/shard_map/ppermute | solution.py:85
  925.9 5.8 collective-permute-done.82
  934.6 7.8 collective-permute-done.84
  (722 shorter events, 454.7 us)
Async XLA Ops:
  2.1 50.1 %collective-permute-start.1 = (bf16[2,512]{1,0:T(2,128)(2,1)S(1)}, bf16[2,512]{1,0:T(2,128)(2,1)S(1)}, u32[]{:S(2)}, u32[]{:S(2)}) collective-permute-start(bf16[2,512]{1,0:T(2,128)(2,1)S(1)} %get-tuple-element.204), channel_id=1, source_target_pairs={{0,8},{8,16},{16,24},{24,0},{1,9},{9,17},{17,25},{25,1},{2,10},{10... | collective-permute-start | bytes 6152 | tf_op jit(solution)/shard_map/ppermute | solution.py:92
  5.1 47.3 %collective-permute-start.2 = (bf16[2,512]{1,0:T(2,128)(2,1)S(1)}, bf16[2,512]{1,0:T(2,128)(2,1)S(1)}, u32[]{:S(2)}, u32[]{:S(2)}) collective-permute-start(bf16[2,512]{1,0:T(2,128)(2,1)S(1)} %get-tuple-element.204), channel_id=1, source_target_pairs={{0,16},{8,24},{16,0},{24,8},{1,17},{9,25},{17,1},{25,9},{2,18},{10... | collective-permute-start | bytes 6152 | tf_op jit(solution)/shard_map/ppermute | solution.py:92
  7.7 45.5 %collective-permute-start.3 = (bf16[2,512]{1,0:T(2,128)(2,1)S(1)}, bf16[2,512]{1,0:T(2,128)(2,1)S(1)}, u32[]{:S(2)}, u32[]{:S(2)}) collective-permute-start(bf16[2,512]{1,0:T(2,128)(2,1)S(1)} %get-tuple-element.204), channel_id=1, source_target_pairs={{0,24},{8,0},{16,8},{24,16},{1,25},{9,1},{17,9},{25,17},{2,26},{10... | collective-permute-start | bytes 6152 | tf_op jit(solution)/shard_map/ppermute | solution.py:92
  9.1 71.6 %collective-permute-start = (bf16[256,1024]{1,0:T(8,128)(2,1)}, bf16[256,1024]{1,0:T(8,128)(2,1)S(1)}, u32[]{:S(2)}, u32[]{:S(2)}) collective-permute-start(bf16[256,1024]{1,0:T(8,128)(2,1)} %bitcast.582), channel_id=1, source_target_pairs={{0,1},{1,0},{2,3},{3,2},{4,5},{5,4},{6,7},{7,6},{8,9},{9,8},{10,11... | collective-permute-start | bytes 1572872 | tf_op jit(solution)/shard_map/ppermute | solution.py:79
  14.6 59.0 %collective-permute-start.4 = (bf16[128,1536]{1,0:T(8,128)(2,1)}, bf16[128,1536]{1,0:T(8,128)(2,1)}, u32[]{:S(2)}, u32[]{:S(2)}) collective-permute-start(bf16[128,1536]{1,0:T(8,128)(2,1)} %constant_dynamic-slice_fusion.16), channel_id=1, source_target_pairs={{0,8},{8,16},{16,24},{24,0},{1,9},{9,17},{17,25},{25,1},{2,10},{10... | collective-permute-start | bytes 1179656 | tf_op jit(solution)/shard_map/ppermute | solution.py:92
  53.2 31.8 %collective-permute-start.58 = (bf16[256,1024]{1,0:T(8,128)(2,1)S(1)}, bf16[256,1024]{1,0:T(8,128)(2,1)S(1)}, u32[]{:S(2)}, u32[]{:S(2)}) collective-permute-start(bf16[256,1024]{1,0:T(8,128)(2,1)S(1)} %bitcast.591), channel_id=1, source_target_pairs={{0,1},{1,0},{2,3},{3,2},{4,5},{5,4},{6,7},{7,6},{8,9},{9,8},{10,11... | collective-permute-start | bytes 1572872 | tf_op jit(solution)/shard_map/ppermute | solution.py:79
  63.3 33.8 %collective-permute-start.18 = (bf16[256,512]{1,0:T(8,128)(2,1)}, bf16[256,512]{1,0:T(8,128)(2,1)S(1)}, u32[]{:S(2)}, u32[]{:S(2)}) collective-permute-start(bf16[256,512]{1,0:T(8,128)(2,1)} %constant_dynamic-slice_fusion.15), channel_id=1, source_target_pairs={{0,16},{8,24},{16,0},{24,8},{1,17},{9,25},{17,1},{25,9},{2,18},{10... | collective-permute-start | bytes 786440 | tf_op jit(solution)/shard_map/ppermute | solution.py:92
  130.4 35.0 %collective-permute-start.30 = (bf16[128,2048]{1,0:T(8,128)(2,1)S(1)}, bf16[128,2048]{1,0:T(8,128)(2,1)S(1)}, u32[]{:S(2)}, u32[]{:S(2)}) collective-permute-start(bf16[128,2048]{1,0:T(8,128)(2,1)S(1)} %pad_maximum_fusion.22), channel_id=1, source_target_pairs={{0,16},{8,24},{16,0},{24,8},{1,17},{9,25},{17,1},{25,9},{2,18},{10... | collective-permute-start | bytes 1572872 | tf_op jit(solution)/shard_map/ppermute | solution.py:92
  136.3 46.9 %collective-permute-start.38 = (bf16[2,256,512]{2,1,0:T(8,128)(2,1)S(1)}, bf16[2,256,512]{2,1,0:T(8,128)(2,1)S(1)}, u32[]{:S(2)}, u32[]{:S(2)}) collective-permute-start(bf16[2,256,512]{2,1,0:T(8,128)(2,1)S(1)} %pad_maximum_fusion.24), channel_id=1, source_target_pairs={{0,2},{2,0},{4,6},{6,4},{1,3},{3,1},{5,7},{7,5},{8,10},{10,8},{12,... | collective-permute-start | bytes 1572872 | tf_op jit(solution)/shard_map/ppermute | solution.py:82
  137.6 45.6 %collective-permute-start.17 = (bf16[2,256,512]{2,1,0:T(8,128)(2,1)S(1)}, bf16[2,256,512]{2,1,0:T(8,128)(2,1)S(1)}, u32[]{:S(2)}, u32[]{:S(2)}) collective-permute-start(bf16[2,256,512]{2,1,0:T(8,128)(2,1)S(1)} %pad_maximum_fusion.18), channel_id=1, source_target_pairs={{0,2},{2,0},{4,6},{6,4},{1,3},{3,1},{5,7},{7,5},{8,10},{10,8},{12,... | collective-permute-start | bytes 1572872 | tf_op jit(solution)/shard_map/ppermute | solution.py:82
  146.3 62.8 %collective-permute-start.68 = (bf16[256,1024]{1,0:T(8,128)(2,1)S(1)}, bf16[256,1024]{1,0:T(8,128)(2,1)S(1)}, u32[]{:S(2)}, u32[]{:S(2)}) collective-permute-start(bf16[256,1024]{1,0:T(8,128)(2,1)S(1)} %bitcast.592), channel_id=1, source_target_pairs={{0,24},{8,0},{16,8},{24,16},{1,25},{9,1},{17,9},{25,17},{2,26},{10... | collective-permute-start | bytes 1572872 | tf_op jit(solution)/shard_map/ppermute | solution.py:92
  163.8 30.9 %collective-permute-start.28 = (bf16[128,2048]{1,0:T(8,128)(2,1)S(1)}, bf16[128,2048]{1,0:T(8,128)(2,1)S(1)}, u32[]{:S(2)}, u32[]{:S(2)}) collective-permute-start(bf16[128,2048]{1,0:T(8,128)(2,1)S(1)} %collective-permute-done.27), channel_id=1, source_target_pairs={{0,4},{2,6},{4,0},{6,2},{1,5},{3,7},{5,1},{7,3},{8,12},{10,14},{12... | collective-permute-start | bytes 1572872 | tf_op jit(solution)/shard_map/ppermute | solution.py:85
  165.5 30.4 %collective-permute-start.33 = (bf16[128,2048]{1,0:T(8,128)(2,1)}, bf16[128,2048]{1,0:T(8,128)(2,1)S(1)}, u32[]{:S(2)}, u32[]{:S(2)}) collective-permute-start(bf16[128,2048]{1,0:T(8,128)(2,1)} %pad_maximum_fusion.23), channel_id=1, source_target_pairs={{0,24},{8,0},{16,8},{24,16},{1,25},{9,1},{17,9},{25,17},{2,26},{10... | collective-permute-start | bytes 1572872 | tf_op jit(solution)/shard_map/ppermute | solution.py:92
  194.7 34.5 %collective-permute-start.64 = (bf16[256,1024]{1,0:T(8,128)(2,1)S(1)}, bf16[256,1024]{1,0:T(8,128)(2,1)S(1)}, u32[]{:S(2)}, u32[]{:S(2)}) collective-permute-start(bf16[256,1024]{1,0:T(8,128)(2,1)S(1)} %bitcast.593), channel_id=1, source_target_pairs={{0,16},{8,24},{16,0},{24,8},{1,17},{9,25},{17,1},{25,9},{2,18},{10... | collective-permute-start | bytes 1572872 | tf_op jit(solution)/shard_map/ppermute | solution.py:92
  195.9 33.4 %collective-permute-start.60 = (bf16[256,1024]{1,0:T(8,128)(2,1)S(1)}, bf16[256,1024]{1,0:T(8,128)(2,1)S(1)}, u32[]{:S(2)}, u32[]{:S(2)}) collective-permute-start(bf16[256,1024]{1,0:T(8,128)(2,1)S(1)} %bitcast.594), channel_id=1, source_target_pairs={{0,8},{8,16},{16,24},{24,0},{1,9},{9,17},{17,25},{25,1},{2,10},{10... | collective-permute-start | bytes 1572872 | tf_op jit(solution)/shard_map/ppermute | solution.py:92
  209.1 33.7 %collective-permute-start.23 = (bf16[2,256,512]{2,1,0:T(8,128)(2,1)S(1)}, bf16[2,256,512]{2,1,0:T(8,128)(2,1)S(1)}, u32[]{:S(2)}, u32[]{:S(2)}) collective-permute-start(bf16[2,256,512]{2,1,0:T(8,128)(2,1)S(1)} %pad_maximum_fusion.20), channel_id=1, source_target_pairs={{0,2},{2,0},{4,6},{6,4},{1,3},{3,1},{5,7},{7,5},{8,10},{10,8},{12,... | collective-permute-start | bytes 1572872 | tf_op jit(solution)/shard_map/ppermute | solution.py:82
  210.0 31.7 %collective-permute-start.69 = (bf16[256,1024]{1,0:T(8,128)(2,1)S(1)}, bf16[256,1024]{1,0:T(8,128)(2,1)S(1)}, u32[]{:S(2)}, u32[]{:S(2)}) collective-permute-start(bf16[256,1024]{1,0:T(8,128)(2,1)S(1)} %collective-permute-done.68), channel_id=1, source_target_pairs={{0,1},{1,0},{2,3},{3,2},{4,5},{5,4},{6,7},{7,6},{8,9},{9,8},{10,11... | collective-permute-start | bytes 1572872 | tf_op jit(solution)/shard_map/ppermute | solution.py:79
  229.8 30.4 %collective-permute-start.61 = (bf16[256,1024]{1,0:T(8,128)(2,1)S(1)}, bf16[256,1024]{1,0:T(8,128)(2,1)S(1)}, u32[]{:S(2)}, u32[]{:S(2)}) collective-permute-start(bf16[256,1024]{1,0:T(8,128)(2,1)S(1)} %collective-permute-done.60), channel_id=1, source_target_pairs={{0,1},{1,0},{2,3},{3,2},{4,5},{5,4},{6,7},{7,6},{8,9},{9,8},{10,11... | collective-permute-start | bytes 1572872 | tf_op jit(solution)/shard_map/ppermute | solution.py:79
  260.2 33.4 %collective-permute-start.32 = (bf16[2,128,2048]{2,1,0:T(8,128)(2,1)}, bf16[2,128,2048]{2,1,0:T(8,128)(2,1)}, u32[]{:S(2)}, u32[]{:S(2)}) collective-permute-start(bf16[2,128,2048]{2,1,0:T(8,128)(2,1)} %pad_maximum_fusion.6), channel_id=1, source_target_pairs={{0,2},{2,0},{4,6},{6,4},{1,3},{3,1},{5,7},{7,5},{8,10},{10,8},{12,... | collective-permute-start | bytes 3145736 | tf_op jit(solution)/shard_map/ppermute | solution.py:82
  261.7 70.4 %collective-permute-start.35 = (bf16[2,128,2048]{2,1,0:T(8,128)(2,1)}, bf16[2,128,2048]{2,1,0:T(8,128)(2,1)}, u32[]{:S(2)}, u32[]{:S(2)}) collective-permute-start(bf16[2,128,2048]{2,1,0:T(8,128)(2,1)} %pad_maximum_fusion.7), channel_id=1, source_target_pairs={{0,2},{2,0},{4,6},{6,4},{1,3},{3,1},{5,7},{7,5},{8,10},{10,8},{12,... | collective-permute-start | bytes 3145736 | tf_op jit(solution)/shard_map/ppermute | solution.py:82
  338.7 45.1 %collective-permute-start.50 = (bf16[256,1024]{1,0:T(8,128)(2,1)S(1)}, bf16[256,1024]{1,0:T(8,128)(2,1)S(1)}, u32[]{:S(2)}, u32[]{:S(2)}) collective-permute-start(bf16[256,1024]{1,0:T(8,128)(2,1)S(1)} %multiply_convert_fusion.13), channel_id=1, source_target_pairs={{0,16},{8,24},{16,0},{24,8},{1,17},{9,25},{17,1},{25,9},{2,18},{10... | collective-permute-start | bytes 1572872 | tf_op jit(solution)/shard_map/ppermute | solution.py:92
  339.4 45.3 %collective-permute-start.46 = (bf16[256,1024]{1,0:T(8,128)(2,1)S(1)}, bf16[256,1024]{1,0:T(8,128)(2,1)S(1)}, u32[]{:S(2)}, u32[]{:S(2)}) collective-permute-start(bf16[256,1024]{1,0:T(8,128)(2,1)S(1)} %multiply_convert_fusion.13), channel_id=1, source_target_pairs={{0,8},{8,16},{16,24},{24,0},{1,9},{9,17},{17,25},{25,1},{2,10},{10... | collective-permute-start | bytes 1572872 | tf_op jit(solution)/shard_map/ppermute | solution.py:92
  363.5 137.2 %collective-permute-start.59 = (bf16[256,1024]{1,0:T(8,128)(2,1)}, bf16[256,1024]{1,0:T(8,128)(2,1)}, u32[]{:S(2)}, u32[]{:S(2)}) collective-permute-start(bf16[256,1024]{1,0:T(8,128)(2,1)} %dynamic-slice_convert_fusion.11), channel_id=1, source_target_pairs={{0,1},{1,0},{2,3},{3,2},{4,5},{5,4},{6,7},{7,6},{8,9},{9,8},{10,11... | collective-permute-start | bytes 1572872 | tf_op jit(solution)/shard_map/ppermute | solution.py:79
  367.8 289.4 %collective-permute-start.45 = (bf16[256,1024]{1,0:T(8,128)(2,1)}, bf16[256,1024]{1,0:T(8,128)(2,1)}, u32[]{:S(2)}, u32[]{:S(2)}) collective-permute-start(bf16[256,1024]{1,0:T(8,128)(2,1)} %dynamic-slice_convert_fusion.15), channel_id=1, source_target_pairs={{0,1},{1,0},{2,3},{3,2},{4,5},{5,4},{6,7},{7,6},{8,9},{9,8},{10,11... | collective-permute-start | bytes 1572872 | tf_op jit(solution)/shard_map/ppermute | solution.py:79
  384.7 43.8 %collective-permute-start.47 = (bf16[256,1024]{1,0:T(8,128)(2,1)S(1)}, bf16[256,1024]{1,0:T(8,128)(2,1)S(1)}, u32[]{:S(2)}, u32[]{:S(2)}) collective-permute-start(bf16[256,1024]{1,0:T(8,128)(2,1)S(1)} %collective-permute-done.46), channel_id=1, source_target_pairs={{0,1},{1,0},{2,3},{3,2},{4,5},{5,4},{6,7},{7,6},{8,9},{9,8},{10,11... | collective-permute-start | bytes 1572872 | tf_op jit(solution)/shard_map/ppermute | solution.py:79
  493.8 30.2 %collective-permute-start.67 = (bf16[256,1024]{1,0:T(8,128)(2,1)S(1)}, bf16[256,1024]{1,0:T(8,128)(2,1)S(1)}, u32[]{:S(2)}, u32[]{:S(2)}) collective-permute-start(bf16[256,1024]{1,0:T(8,128)(2,1)S(1)} %add_convert_fusion.1), channel_id=1, source_target_pairs={{0,16},{8,24},{16,0},{24,8},{1,17},{9,25},{17,1},{25,9},{2,18},{10... | collective-permute-start | bytes 1572872 | tf_op jit(solution)/shard_map/ppermute | solution.py:92
  500.6 39.9 %collective-permute-start.56 = (bf16[256,1024]{1,0:T(8,128)(2,1)}, bf16[256,1024]{1,0:T(8,128)(2,1)}, u32[]{:S(2)}, u32[]{:S(2)}) collective-permute-start(bf16[256,1024]{1,0:T(8,128)(2,1)} %dynamic-slice_convert_fusion.12), channel_id=1, source_target_pairs={{0,1},{1,0},{2,3},{3,2},{4,5},{5,4},{6,7},{7,6},{8,9},{9,8},{10,11... | collective-permute-start | bytes 1572872 | tf_op jit(solution)/shard_map/ppermute | solution.py:79
  508.6 34.0 %collective-permute-start.52 = (bf16[256,1024]{1,0:T(8,128)(2,1)}, bf16[256,1024]{1,0:T(8,128)(2,1)S(1)}, u32[]{:S(2)}, u32[]{:S(2)}) collective-permute-start(bf16[256,1024]{1,0:T(8,128)(2,1)} %dynamic-slice_convert_fusion.13), channel_id=1, source_target_pairs={{0,1},{1,0},{2,3},{3,2},{4,5},{5,4},{6,7},{7,6},{8,9},{9,8},{10,11... | collective-permute-start | bytes 1572872 | tf_op jit(solution)/shard_map/ppermute | solution.py:79
  524.0 93.5 %collective-permute-start.48 = (bf16[256,1024]{1,0:T(8,128)(2,1)}, bf16[256,1024]{1,0:T(8,128)(2,1)}, u32[]{:S(2)}, u32[]{:S(2)}) collective-permute-start(bf16[256,1024]{1,0:T(8,128)(2,1)} %dynamic-slice_convert_fusion.14), channel_id=1, source_target_pairs={{0,1},{1,0},{2,3},{3,2},{4,5},{5,4},{6,7},{7,6},{8,9},{9,8},{10,11... | collective-permute-start | bytes 1572872 | tf_op jit(solution)/shard_map/ppermute | solution.py:79
  540.6 196.4 %collective-permute-start.93 = (bf16[4,2,128,2048]{3,2,1,0:T(8,128)(2,1)}, bf16[4,2,128,2048]{3,2,1,0:T(8,128)(2,1)}, u32[]{:S(2)}, u32[]{:S(2)}) collective-permute-start(bf16[4,2,128,2048]{3,2,1,0:T(8,128)(2,1)} %fusion.58), channel_id=1, source_target_pairs={{0,2},{2,0},{4,6},{6,4},{1,3},{3,1},{5,7},{7,5},{8,10},{10,8},{12,... | collective-permute-start | bytes 12582920 | tf_op jit(solution)/shard_map/ppermute | solution.py:82
  542.6 96.6 %collective-permute-start.100 = (bf16[1,2,256,2048]{3,2,1,0:T(8,128)(2,1)}, bf16[1,2,256,2048]{3,2,1,0:T(8,128)(2,1)}, u32[]{:S(2)}, u32[]{:S(2)}) collective-permute-start(bf16[1,2,256,2048]{3,2,1,0:T(8,128)(2,1)} %fusion.113), channel_id=1, source_target_pairs={{0,2},{2,0},{4,6},{6,4},{1,3},{3,1},{5,7},{7,5},{8,10},{10,8},{12,... | collective-permute-start | bytes 6291464 | tf_op jit(solution)/shard_map/ppermute | solution.py:82
  551.4 107.9 %collective-permute-start.57 = (bf16[256,1024]{1,0:T(8,128)(2,1)}, bf16[256,1024]{1,0:T(8,128)(2,1)}, u32[]{:S(2)}, u32[]{:S(2)}) collective-permute-start(bf16[256,1024]{1,0:T(8,128)(2,1)} %add_convert_fusion.4), channel_id=1, source_target_pairs={{0,8},{8,16},{16,24},{24,0},{1,9},{9,17},{17,25},{25,1},{2,10},{10... | collective-permute-start | bytes 1572872 | tf_op jit(solution)/shard_map/ppermute | solution.py:92
  633.7 74.2 %collective-permute-start.53 = (bf16[256,1024]{1,0:T(8,128)(2,1)}, bf16[256,1024]{1,0:T(8,128)(2,1)}, u32[]{:S(2)}, u32[]{:S(2)}) collective-permute-start(bf16[256,1024]{1,0:T(8,128)(2,1)} %add_convert_fusion.5), channel_id=1, source_target_pairs={{0,16},{8,24},{16,0},{24,8},{1,17},{9,25},{17,1},{25,9},{2,18},{10... | collective-permute-start | bytes 1572872 | tf_op jit(solution)/shard_map/ppermute | solution.py:92
  657.2 50.9 %collective-permute-start.49 = (bf16[256,1024]{1,0:T(8,128)(2,1)}, bf16[256,1024]{1,0:T(8,128)(2,1)}, u32[]{:S(2)}, u32[]{:S(2)}) collective-permute-start(bf16[256,1024]{1,0:T(8,128)(2,1)} %add_convert_fusion.6), channel_id=1, source_target_pairs={{0,24},{8,0},{16,8},{24,16},{1,25},{9,1},{17,9},{25,17},{2,26},{10... | collective-permute-start | bytes 1572872 | tf_op jit(solution)/shard_map/ppermute | solution.py:92
  659.3 66.5 %collective-permute-start.86 = (bf16[1,2,256,2048]{3,2,1,0:T(8,128)(2,1)}, bf16[1,2,256,2048]{3,2,1,0:T(8,128)(2,1)}, u32[]{:S(2)}, u32[]{:S(2)}) collective-permute-start(bf16[1,2,256,2048]{3,2,1,0:T(8,128)(2,1)} %fusion.111), channel_id=1, source_target_pairs={{0,2},{2,0},{4,6},{6,4},{1,3},{3,1},{5,7},{7,5},{8,10},{10,8},{12,... | collective-permute-start | bytes 6291464 | tf_op jit(solution)/shard_map/ppermute | solution.py:82
  659.3 53.6 %collective-permute-start.101 = (bf16[1,256,2048]{2,1,0:T(8,128)(2,1)}, bf16[1,256,2048]{2,1,0:T(8,128)(2,1)}, u32[]{:S(2)}, u32[]{:S(2)}) collective-permute-start(bf16[1,256,2048]{2,1,0:T(8,128)(2,1)} %fusion.134), channel_id=1, source_target_pairs={{0,4},{2,6},{4,0},{6,2},{1,5},{3,7},{5,1},{7,3},{8,12},{10,14},{12... | collective-permute-start | bytes 3145736 | tf_op jit(solution)/shard_map/ppermute | solution.py:85
  707.9 117.7 %collective-permute-start.79 = (bf16[4,2,128,1536]{3,2,0,1:T(8,128)(2,1)}, bf16[4,2,128,1536]{3,2,0,1:T(8,128)(2,1)}, u32[]{:S(2)}, u32[]{:S(2)}) collective-permute-start(bf16[4,2,128,1536]{3,2,0,1:T(8,128)(2,1)} %fusion.107), channel_id=1, source_target_pairs={{0,2},{2,0},{4,6},{6,4},{1,3},{3,1},{5,7},{7,5},{8,10},{10,8},{12,... | collective-permute-start | bytes 9437192 | tf_op jit(solution)/shard_map/ppermute | solution.py:82
  736.9 51.1 %collective-permute-start.105 = (bf16[4,256,512]{2,1,0:T(8,128)(2,1)S(1)}, bf16[4,256,512]{2,1,0:T(8,128)(2,1)}, u32[]{:S(2)}, u32[]{:S(2)}) collective-permute-start(bf16[4,256,512]{2,1,0:T(8,128)(2,1)S(1)} %bitcast_dynamic-update-slice_fusion.1), channel_id=1, source_target_pairs={{0,4},{2,6},{4,0},{6,2},{1,5},{3,7},{5,1},{7,3},{8,12},{10,14},{12... | collective-permute-start | bytes 3145736 | tf_op jit(solution)/shard_map/ppermute | solution.py:85
  765.1 69.6 %collective-permute-start.94 = (bf16[4,128,2048]{2,1,0:T(8,128)(2,1)}, bf16[4,128,2048]{2,1,0:T(8,128)(2,1)}, u32[]{:S(2)}, u32[]{:S(2)}) collective-permute-start(bf16[4,128,2048]{2,1,0:T(8,128)(2,1)} %fusion.112), channel_id=1, source_target_pairs={{0,4},{2,6},{4,0},{6,2},{1,5},{3,7},{5,1},{7,3},{8,12},{10,14},{12... | collective-permute-start | bytes 6291464 | tf_op jit(solution)/shard_map/ppermute | solution.py:85
  786.3 39.1 %collective-permute-start.91 = (bf16[256,512]{1,0:T(8,128)(2,1)S(1)}, bf16[256,512]{1,0:T(8,128)(2,1)S(1)}, u32[]{:S(2)}, u32[]{:S(2)}) collective-permute-start(bf16[256,512]{1,0:T(8,128)(2,1)S(1)} %get-tuple-element.197), channel_id=1, source_target_pairs={{0,4},{2,6},{4,0},{6,2},{1,5},{3,7},{5,1},{7,3},{8,12},{10,14},{12... | collective-permute-start | bytes 786440 | tf_op jit(solution)/shard_map/ppermute | solution.py:85
  792.1 86.1 %collective-permute-start.106 = (bf16[2,4,256,512]{3,2,1,0:T(8,128)(2,1)}, bf16[2,4,256,512]{3,2,1,0:T(8,128)(2,1)}, u32[]{:S(2)}, u32[]{:S(2)}) collective-permute-start(bf16[2,4,256,512]{3,2,1,0:T(8,128)(2,1)} %pad_maximum_fusion.1), channel_id=1, source_target_pairs={{0,2},{2,0},{4,6},{6,4},{1,3},{3,1},{5,7},{7,5},{8,10},{10,8},{12,... | collective-permute-start | bytes 6291464 | tf_op jit(solution)/shard_map/ppermute | solution.py:82
  833.6 50.0 %collective-permute-start.80 = (bf16[4,128,1536]{2,1,0:T(8,128)(2,1)S(1)}, bf16[4,128,1536]{2,1,0:T(8,128)(2,1)S(1)}, u32[]{:S(2)}, u32[]{:S(2)}) collective-permute-start(bf16[4,128,1536]{2,1,0:T(8,128)(2,1)S(1)} %fusion.122), channel_id=1, source_target_pairs={{0,4},{2,6},{4,0},{6,2},{1,5},{3,7},{5,1},{7,3},{8,12},{10,14},{12... | collective-permute-start | bytes 4718600 | tf_op jit(solution)/shard_map/ppermute | solution.py:85
  838.6 37.2 %collective-permute-start.96 = (bf16[128,2048]{1,0:T(8,128)(2,1)S(1)}, bf16[128,2048]{1,0:T(8,128)(2,1)S(1)}, u32[]{:S(2)}, u32[]{:S(2)}) collective-permute-start(bf16[128,2048]{1,0:T(8,128)(2,1)S(1)} %get-tuple-element.234), channel_id=1, source_target_pairs={{0,16},{8,24},{16,0},{24,8},{1,17},{9,25},{17,1},{25,9},{2,18},{10... | collective-permute-start | bytes 1572872 | tf_op jit(solution)/shard_map/ppermute | solution.py:92
  838.7 37.2 %collective-permute-start.97 = (bf16[128,2048]{1,0:T(8,128)(2,1)S(1)}, bf16[128,2048]{1,0:T(8,128)(2,1)S(1)}, u32[]{:S(2)}, u32[]{:S(2)}) collective-permute-start(bf16[128,2048]{1,0:T(8,128)(2,1)S(1)} %get-tuple-element.233), channel_id=1, source_target_pairs={{0,24},{8,0},{16,8},{24,16},{1,25},{9,1},{17,9},{25,17},{2,26},{10... | collective-permute-start | bytes 1572872 | tf_op jit(solution)/shard_map/ppermute | solution.py:92
  876.0 47.4 %collective-permute-start.98 = (bf16[2,128,4096]{2,1,0:T(8,128)(2,1)S(1)}, bf16[2,128,4096]{2,1,0:T(8,128)(2,1)S(1)}, u32[]{:S(2)}, u32[]{:S(2)}) collective-permute-start(bf16[2,128,4096]{2,1,0:T(8,128)(2,1)S(1)} %maximum_dynamic-update-slice_fusion.4), channel_id=1, source_target_pairs={{0,4},{2,6},{4,0},{6,2},{1,5},{3,7},{5,1},{7,3},{8,12},{10,14},{12... | collective-permute-start | bytes 6291464 | tf_op jit(solution)/shard_map/ppermute | solution.py:85
  884.3 41.5 %collective-permute-start.83 = (bf16[128,1536]{1,0:T(8,128)(2,1)S(1)}, bf16[128,1536]{1,0:T(8,128)(2,1)S(1)}, u32[]{:S(2)}, u32[]{:S(2)}) collective-permute-start(bf16[128,1536]{1,0:T(8,128)(2,1)S(1)} %get-tuple-element.223), channel_id=1, source_target_pairs={{0,24},{8,0},{16,8},{24,16},{1,25},{9,1},{17,9},{25,17},{2,26},{10... | collective-permute-start | bytes 1179656 | tf_op jit(solution)/shard_map/ppermute | solution.py:92
  896.0 35.7 %collective-permute-start.82 = (bf16[128,1536]{1,0:T(8,128)(2,1)S(1)}, bf16[128,1536]{1,0:T(8,128)(2,1)S(1)}, u32[]{:S(2)}, u32[]{:S(2)}) collective-permute-start(bf16[128,1536]{1,0:T(8,128)(2,1)S(1)} %get-tuple-element.224), channel_id=1, source_target_pairs={{0,16},{8,24},{16,0},{24,8},{1,17},{9,25},{17,1},{25,9},{2,18},{10... | collective-permute-start | bytes 1179656 | tf_op jit(solution)/shard_map/ppermute | solution.py:92
  897.4 34.2 %collective-permute-start.81 = (bf16[128,1536]{1,0:T(8,128)(2,1)S(1)}, bf16[128,1536]{1,0:T(8,128)(2,1)S(1)}, u32[]{:S(2)}, u32[]{:S(2)}) collective-permute-start(bf16[128,1536]{1,0:T(8,128)(2,1)S(1)} %get-tuple-element.222), channel_id=1, source_target_pairs={{0,8},{8,16},{16,24},{24,0},{1,9},{9,17},{17,25},{25,1},{2,10},{10... | collective-permute-start | bytes 1179656 | tf_op jit(solution)/shard_map/ppermute | solution.py:92
  (169 other events, 3343.4 us)

commit v2 on v1

v2 whole, which is shorter than its diff:
```python
import math

import jax
import jax.numpy as jnp
from jax import lax
from jax.experimental import pallas as pl
from jax.experimental.pallas import tpu as pltpu
from jax.sharding import PartitionSpec as P

HEAD_WIDTH = 64
EPS = 1e-05
NEG = -1e30
BF = jnp.bfloat16
F32 = jnp.float32
LANES = 128
GAIN_ROWS = 16
FACTOR = 1.0 / math.sqrt(HEAD_WIDTH)
VMEM_LIMIT = 60 * 2**20
MESH = pl.DeviceIdType.MESH


def rope_freqs(head_size):
    half_size = head_size // 2
    index = jnp.arange(half_size, dtype=jnp.float32)
    base_freq = jnp.exp(-(2.0 * index / head_size) * math.log(500000.0))
    wavelen = 2.0 * math.pi / base_freq
    smooth = (8192.0 / wavelen - 1.0) / 3.0
    blended = (1.0 - smooth) * base_freq / 32.0 + smooth * base_freq
    return jnp.where(
        wavelen > 8192.0, base_freq / 32.0, jnp.where(wavelen < 2048.0, base_freq, blended)
    )


def apply_rotary(values, cosine_table, sine_table):
    half_size = values.shape[-1] // 2
    first = values[..., :half_size]
    second = values[..., half_size:]
    return jnp.concatenate(
        [first * cosine_table - second * sine_table, second * cosine_table + first * sine_table], -1
    )


def dot(left, right):
    return jnp.dot(left, right, preferred_element_type=F32)


def dot_t(left, right):
    return lax.dot_general(left, right, (((1,), (1,)), ((), ())), preferred_element_type=F32)


def t_dot(left, right):
    return lax.dot_general(left, right, (((0,), (0,)), ((), ())), preferred_element_type=F32)


def pick(blocks, index, axis=0):
    return lax.dynamic_index_in_dim(blocks, index, axis, keepdims=False)


def place(whole, block, starts):
    return lax.dynamic_update_slice(whole, block, starts)


def build_front(planes, contexts, rows, width, query_cols, kv_cols, units):
    outers = contexts // 2
    half = width // 2
    depth = width // planes
    strip = depth // contexts
    out_strip = query_cols // contexts
    unit_strip = units // contexts
    seq_len = rows * contexts
    n_q, n_kv = query_cols // LANES, kv_cols // LANES
    heads = query_cols // HEAD_WIDTH
    group = query_cols // kv_cols
    qkv_cols = query_cols + 2 * kv_cols
    QKV, OUT, GATE, UP, DOWN, COT, NORM, GAIN = range(8)

    def kernel(
        tok, cot, gains_own, qkv_own, out_own, gate_own, up_own, down_own, cosine, sine, pos_q, pos_k,
        gate_w, up_w, down_w, cot_all, norm_all, qkv_w, out_w, gains, q_pad, kv_all, attn, log_sum,
        mid_own, normed_one, tok_all,
        lin, heads_out, send_half, recv_half, norm_own, sq_send, sq_recv,
        z_send, z_recv, y_send, y_recv, k_send, k_recv, x_send, x_recv, own_sem,
    ):
        z = lax.axis_index("fsdp")
        c = lax.axis_index("context")
        t = lax.axis_index("tensor")
        o, k = c // 2, c % 2

        def at_z(p):
            return (p, c, t)

        def at_o(other):
            return (z, other * 2 + k, t)

        at_k = (z, o * 2 + 1 - k, t)
        at_x = (z, c, 1 - t)

        def copy(src, dst, send_sem, recv_sem, device):
            return pltpu.make_async_remote_copy(
                src_ref=src, dst_ref=dst, send_sem=send_sem, recv_sem=recv_sem,
                device_id=device, device_id_type=MESH,
            )

        barrier = pltpu.get_barrier_semaphore()
        peers = [at_z(lax.rem(z + s, planes)) for s in range(1, planes)]
        peers += [at_o(lax.rem(o + s, outers)) for s in range(1, outers)] + [at_k, at_x]
        for peer in peers:
            pl.semaphore_signal(barrier, inc=1, device_id=peer, device_id_type=MESH)
        pl.semaphore_wait(barrier, len(peers))

        order = []
        for i in range(planes - 1):
            p = jnp.int32(0)
            for plane in range(planes):
                far = sorted((abs(q - plane), q) for q in range(planes) if q != plane)
                p = p + jnp.where(z == plane, far[i][1], 0)
            order.append(p)

        def slot(item, p, q):
            if item == QKV:
                return qkv_w.at[pl.ds(p * depth + q * strip, strip), :]
            if item == OUT:
                return out_w.at[pl.ds(q * out_strip, out_strip), pl.ds(p * depth, depth)]
            if item == GATE:
                return gate_w.at[pl.ds(p * depth + q * strip, strip), :]
            if item == UP:
                return up_w.at[pl.ds(p * depth + q * strip, strip), :]
            if item == DOWN:
                return down_w.at[pl.ds(q * unit_strip, unit_strip), pl.ds(p * depth, depth)]
            if item == COT:
                return cot_all.at[p, :, pl.ds(t * half, half)]
            return norm_all.at[p, :, pl.ds(t * half, half)]

        def z_copy(item, p, src, goal, way):
            return copy(src, slot(item, p, c), z_send.at[item, p, way], z_recv.at[item, p], at_z(goal))

        def z_wait(item, p):
            z_copy(item, p, slot(item, p, c), z, 0).wait_recv()

        def spread(item, src):
            @pl.when(z + 1 < planes)
            def _():
                z_copy(item, z, src, z + 1, 0).start()

            @pl.when(z > 0)
            def _():
                z_copy(item, z, src, z - 1, 1).start()

        def spread_done(item, src):
            @pl.when(z + 1 < planes)
            def _():
                z_copy(item, z, src, z + 1, 0).wait_send()

            @pl.when(z > 0)
            def _():
                z_copy(item, z, src, z - 1, 1).wait_send()

        def passes_on(p):
            return ((p < z) & (z + 1 < planes)) | ((p > z) & (z > 0))

        def onward(p):
            return jnp.where(p < z, z + 1, z - 1)

        def forward(item, p):
            @pl.when(passes_on(p))
            def _():
                z_copy(item, p, slot(item, p, c), onward(p), 0).start()

        def forward_done(item, p):
            @pl.when(passes_on(p))
            def _():
                z_copy(item, p, slot(item, p, c), onward(p), 0).wait_send()

        def y_copy(item, p, by):
            here = slot(item, p, c)
            return copy(here, here, y_send.at[item, p, by], y_recv.at[item, p, by], at_o(lax.rem(o + by, outers)))

        def y_wait(item, p, by):
            there = slot(item, p, lax.rem(o - by + outers, outers) * 2 + k)
            copy(there, there, y_send.at[item, p, by], y_recv.at[item, p, by], at_k).wait_recv()

        def k_copy(item, p, by):
            here = slot(item, p, lax.rem(o - by + outers, outers) * 2 + k)
            return copy(here, here, k_send.at[item, p, by], k_recv.at[item, p, by], at_k)

        def k_wait(item, p, by):
            there = slot(item, p, lax.rem(o - by + outers, outers) * 2 + 1 - k)
            copy(there, there, k_send.at[item, p, by], k_recv.at[item, p, by], at_k).wait_recv()

        def share(item, p):
            for by in range(1, outers):
                y_copy(item, p, by).start()
            k_copy(item, p, 0).start()

        def share_on(item, p):
            for by in range(1, outers):
                y_wait(item, p, by)
                k_copy(item, p, by).start()

        def shared(item, p):
            for by in range(outers):
                k_wait(item, p, by)

        def share_done(item, p):
            for by in range(1, outers):
                y_copy(item, p, by).wait_send()
            for by in range(outers):
                k_copy(item, p, by).wait_send()

        def x_copy(i, src, dst):
            return copy(src, dst, x_send.at[i], x_recv.at[i], at_x)

        tok_cols = pl.ds(t * half, half)
        tok_copy = x_copy(0, tok, tok_all.at[:, tok_cols])
        tok_copy.start()
        gain_copies = [
            copy(
                gains_own, gains.at[:, pl.ds(z * depth, depth)], z_send.at[GAIN, lax.rem(z + s, planes), 0],
                z_recv.at[GAIN, z], at_z(lax.rem(z + s, planes)),
            )
            for s in range(1, planes)
        ]
        for one in gain_copies:
            one.start()
        qkv_src = qkv_own.at[pl.ds(c * strip, strip), :]
        out_src = out_own.at[pl.ds(c * out_strip, out_strip), :]
        spread(QKV, qkv_src)
        own_copies = [
            pltpu.make_async_copy(qkv_own, qkv_w.at[pl.ds(z * depth, depth), :], own_sem.at[0]),
            pltpu.make_async_copy(out_own, out_w.at[:, pl.ds(z * depth, depth)], own_sem.at[1]),
            pltpu.make_async_copy(
                gate_own.at[:, pl.ds(z * units, units)], gate_w.at[pl.ds(z * depth, depth), :], own_sem.at[2]
            ),
            pltpu.make_async_copy(
                up_own.at[:, pl.ds(z * units, units)], up_w.at[pl.ds(z * depth, depth), :], own_sem.at[3]
            ),
            pltpu.make_async_copy(
                down_own.at[pl.ds(z * units, units), :], down_w.at[:, pl.ds(z * depth, depth)], own_sem.at[4]
            ),
            pltpu.make_async_copy(cot, slot(COT, z, c), own_sem.at[5]),
        ]
        for one in own_copies:
            one.start()
        gains[:, pl.ds(z * depth, depth)] = gains_own[...]
        tok_all[:, tok_cols] = tok[...]

        tok_copy.wait()
        for s in range(1, planes):
            p = lax.rem(z + s, planes)
            there = gains.at[:, pl.ds(p * depth, depth)]
            copy(there, there, z_send.at[GAIN, p, 0], z_recv.at[GAIN, p], at_k).wait_recv()
        x = tok_all[...].astype(F32)
        scale = lax.rsqrt(jnp.mean(x * x, -1, keepdims=True) + EPS)
        normed_one[...] = (x * scale * gains[0:1, :].astype(F32)).astype(BF)

        for p in order:
            z_wait(QKV, p)
            forward(QKV, p)
            share(QKV, p)

        spread(OUT, out_src)
        sends = []
        for s in range(1, planes):
            goal = lax.rem(z + s, planes)
            cols = pl.ds(goal * units, units)
            sends += [
                z_copy(GATE, z, gate_own.at[pl.ds(c * strip, strip), cols], goal, s - 1),
                z_copy(UP, z, up_own.at[pl.ds(c * strip, strip), cols], goal, s - 1),
                z_copy(
                    DOWN, z, down_own.at[pl.ds(goal * units + c * unit_strip, unit_strip), :], goal, s - 1
                ),
            ]
        for one in sends:
            one.start()
        spread(COT, cot)
        cot_copy = x_copy(1 + z, cot, slot(COT, z, c))
        cot_copy.start()

        for p in order:
            share_on(QKV, p)
        for p in order:
            shared(QKV, p)
        own_copies[0].wait()

        n_tile = 2 * LANES

        @pl.loop(0, qkv_cols // n_tile)
        def _(i):
            cols = pl.ds(pl.multiple_of(i * n_tile, n_tile), n_tile)
            found = jnp.dot(normed_one[...], qkv_w[:, cols], preferred_element_type=F32)
            lin[2 * i] = found[:, :LANES]
            lin[2 * i + 1] = found[:, LANES:]

        lane = lax.broadcasted_iota(jnp.int32, (rows, LANES), 1)
        first = lax.rem(lane, HEAD_WIDTH) < HEAD_WIDTH // 2
        low = lane < HEAD_WIDTH

        def rotated(u):
            partner = jnp.where(
                first, pltpu.roll(u, LANES - HEAD_WIDTH // 2, 1), pltpu.roll(u, HEAD_WIDTH // 2, 1)
            )
            return u * cosine[...] + partner * sine[...]

        for i in range(n_kv):
            kv_all[c, i] = rotated(lin[n_q + i]).astype(BF)
            kv_all[c, n_kv + i] = lin[n_q + n_kv + i].astype(BF)

        def kv_slot(q):
            return kv_all.at[q]

        kv_sends = [
            copy(kv_slot(c), kv_slot(c), y_send.at[COT, 0, by], y_recv.at[COT, 0, by], at_o(lax.rem(o + by, outers)))
            for by in range(1, outers)
        ]
        kv_sends.append(copy(kv_slot(c), kv_slot(c), k_send.at[COT, 0, 0], k_recv.at[COT, 0, 0], at_k))
        for one in kv_sends:
            one.start()

        @pl.loop(0, n_q)
        def _(j):
            u = rotated(lin[j]).astype(BF).astype(F32) * FACTOR
            side = lax.rem((2 * j) // group, 2)
            lo = jnp.where(low, u, 0.0)
            hi = jnp.where(low, 0.0, u)
            q_pad[2 * j] = jnp.where(side == 0, lo, pltpu.roll(lo, HEAD_WIDTH, 1)).astype(BF)
            q_pad[2 * j + 1] = jnp.where(side == 1, hi, pltpu.roll(hi, HEAD_WIDTH, 1)).astype(BF)

        for by in range(1, outers):
            q = lax.rem(o - by + outers, outers) * 2 + k
            copy(kv_slot(q), kv_slot(q), y_send.at[COT, 0, by], y_recv.at[COT, 0, by], at_k).wait_recv()
            one = copy(kv_slot(q), kv_slot(q), k_send.at[COT, 0, by], k_recv.at[COT, 0, by], at_k)
            one.start()
            kv_sends.append(one)
        for by in range(outers):
            q = lax.rem(o - by + outers, outers) * 2 + 1 - k
            copy(kv_slot(q), kv_slot(q), k_send.at[COT, 0, by], k_recv.at[COT, 0, by], at_k).wait_recv()

        for p in order:
            z_wait(OUT, p)
            forward(OUT, p)
            share(OUT, p)

        def attend(first_head, last_head):
            @pl.loop(first_head, last_head)
            def _(h):
                pair = h // (2 * group)
                keys = kv_all[:, pair].reshape(seq_len, LANES)
                values = kv_all[:, n_kv + pair].reshape(seq_len, LANES)
                scores = dot_t(keys, q_pad[h])
                scores = jnp.where(pos_q[0:1, :] >= pos_k[...], scores, NEG)
                top = jnp.max(scores, 0, keepdims=True)
                expo = jnp.exp(scores - top)
                total = jnp.sum(expo, 0, keepdims=True)
                weights = (expo * (1.0 / total)).astype(BF)
                heads_out[h] = t_dot(values, weights).T
                log_sum[pl.ds(h, 1), :] = top + jnp.log(total)

        attend(0, heads // 2)
        for p in order:
            share_on(OUT, p)
        for p in order:
            z_wait(COT, p)
            forward(COT, p)
            x_copy(1 + p, slot(COT, p, c), slot(COT, p, c)).start()
        attend(heads // 2, heads)

        for j in range(n_q):
            side = (2 * j) // group % 2
            lo, hi = heads_out[2 * j], heads_out[2 * j + 1]
            if side == 0:
                hi = pltpu.roll(hi, HEAD_WIDTH, 1)
            else:
                lo = pltpu.roll(lo, HEAD_WIDTH, 1)
            attn[:, j * LANES : (j + 1) * LANES] = jnp.where(low, lo, hi).astype(BF)

        for p in order:
            shared(OUT, p)
        own_copies[1].wait()

        n_out = half // n_tile

        @pl.loop(0, n_out)
        def _(i):
            cols = pl.ds(pl.multiple_of((1 - t) * half + i * n_tile, n_tile), n_tile)
            here = pl.ds(pl.multiple_of(i * n_tile, n_tile), n_tile)
            send_half[:, here] = jnp.dot(attn[...], out_w[:, cols], preferred_element_type=F32).astype(BF)

        half_copy = x_copy(1 + planes, send_half, recv_half)
        half_copy.start()

        @pl.loop(0, n_out)
        def _(i):
            cols = pl.ds(pl.multiple_of(t * half + i * n_tile, n_tile), n_tile)
            here = pl.ds(pl.multiple_of(i * n_tile, n_tile), n_tile)
            part = jnp.dot(attn[...], out_w[:, cols], preferred_element_type=F32)
            mid_own[:, here] = tok[:, here].astype(F32) + part

        half_copy.wait_recv()
        mid = mid_own[...] + recv_half[...].astype(F32)
        mid_own[...] = mid
        squares = jnp.sum(mid * mid, -1, keepdims=True)
        sq_send[...] = jnp.broadcast_to(squares, (rows, LANES))
        sq_copy = x_copy(2 + planes, sq_send, sq_recv)
        sq_copy.start()
        sq_copy.wait_recv()
        scale_two = lax.rsqrt((squares + sq_recv[:, 0:1]) * (1.0 / width) + EPS)
        gain_two = gains[1:2, pl.ds(pl.multiple_of(t * half, half), half)].astype(F32)
        norm_own[...] = (mid_own[...] * scale_two * gain_two).astype(BF)

        spread(NORM, norm_own)
        norm_copy = x_copy(3 + planes + z, norm_own, slot(NORM, z, c))
        norm_copy.start()
        norm_keep = pltpu.make_async_copy(norm_own, slot(NORM, z, c), own_sem.at[6])
        norm_keep.start()
        items = (GATE, UP, DOWN)
        for s in range(1, planes):
            p = lax.rem(z + planes - s, planes)
            for item in items:
                z_wait(item, p)
                share(item, p)
        for i, p in enumerate(order):
            z_wait(NORM, p)
            forward(NORM, p)
            x_copy(3 + planes + p, slot(NORM, p, c), slot(NORM, p, c)).start()
            for item in items:
                share_on(item, lax.rem(z + planes - 1 - i, planes))

        for s in range(1, planes):
            p = lax.rem(z + s, planes)
            for item in items:
                shared(item, p)
        for p in [z] + order:
            for base, item in ((1, COT), (3 + planes, NORM)):
                there = (cot_all if item == COT else norm_all).at[p, :, pl.ds((1 - t) * half, half)]
                copy(there, there, x_send.at[base + p], x_recv.at[base + p], at_x).wait_recv()
        for one in own_copies[2:]:
            one.wait()
        norm_keep.wait()
        tok_copy_out = [half_copy, sq_copy, cot_copy, norm_copy]
        for one in gain_copies + sends + kv_sends + tok_copy_out:
            one.wait_send()
        spread_done(QKV, qkv_src)
        spread_done(OUT, out_src)
        spread_done(COT, cot)
        spread_done(NORM, norm_own)
        for p in order:
            for item in (QKV, OUT, COT, NORM):
                forward_done(item, p)
            for item in (QKV, OUT, GATE, UP, DOWN):
                share_done(item, p)
            x_copy(1 + p, slot(COT, p, c), slot(COT, p, c)).wait_send()
            x_copy(3 + planes + p, slot(NORM, p, c), slot(NORM, p, c)).wait_send()

    hbm = pl.BlockSpec(memory_space=pl.ANY)
    vmem = pl.BlockSpec(memory_space=pltpu.VMEM)
    dma = pltpu.SemaphoreType.DMA
    shape = jax.ShapeDtypeStruct
    return pl.pallas_call(
        kernel,
        name="front",
        out_shape=(
            shape((width, units), BF),
            shape((width, units), BF),
            shape((units, width), BF),
            shape((planes, rows, width), BF),
            shape((planes, rows, width), BF),
            shape((width, qkv_cols), BF),
            shape((query_cols, width), BF),
            shape((GAIN_ROWS, width), BF),
            shape((heads, rows, LANES), BF),
            shape((contexts, 2 * n_kv, rows, LANES), BF),
            shape((rows, query_cols), BF),
            shape((heads, rows), F32),
            shape((rows, half), F32),
            shape((rows, width), BF),
            shape((rows, width), BF),
        ),
        in_specs=[vmem, hbm, vmem, hbm, hbm, hbm, hbm, hbm, vmem, vmem, vmem, vmem],
        out_specs=(hbm,) * 5 + (vmem,) * 10,
        scratch_shapes=[
            pltpu.VMEM((qkv_cols // LANES, rows, LANES), F32),
            pltpu.VMEM((heads, rows, LANES), F32),
            pltpu.VMEM((rows, half), BF),
            pltpu.VMEM((rows, half), BF),
            pltpu.VMEM((rows, half), BF),
            pltpu.VMEM((rows, LANES), F32),
            pltpu.VMEM((rows, LANES), F32),
            dma((8, planes, planes)),
            dma((8, planes)),
            dma((6, planes, max(outers, 2))),
            dma((6, planes, max(outers, 2))),
            dma((6, planes, max(outers, 2))),
            dma((6, planes, max(outers, 2))),
            dma((3 + 2 * planes,)),
            dma((3 + 2 * planes,)),
            dma((8,)),
        ],
        compiler_params=pltpu.CompilerParams(
            collective_id=0, has_side_effects=True, vmem_limit_bytes=VMEM_LIMIT
        ),
        cost_estimate=pl.CostEstimate(flops=8 * 10**9, bytes_accessed=80 * 10**6, transcendentals=4 * 10**6),
    )


def build_attend_back(contexts, rows, query_cols, kv_cols):
    seq_len = rows * contexts
    n_q, n_kv = query_cols // LANES, kv_cols // LANES
    heads = query_cols // HEAD_WIDTH
    group = query_cols // kv_cols

    def kernel(
        q_pad, kv_all, attn_grad, log_sum, cosine, sine, pos_q, pos_k, query_grad, kv_grad,
        grad_pad, query_out, key_sum, value_sum,
    ):
        lane = lax.broadcasted_iota(jnp.int32, (rows, LANES), 1)
        first = lax.rem(lane, HEAD_WIDTH) < HEAD_WIDTH // 2
        low = lane < HEAD_WIDTH
        for j in range(n_q):
            u = attn_grad[:, j * LANES : (j + 1) * LANES].astype(F32)
            side = (2 * j) // group % 2
            lo = jnp.where(low, u, 0.0)
            hi = jnp.where(low, 0.0, u)
            if side == 0:
                hi = pltpu.roll(hi, HEAD_WIDTH, 1)
            else:
                lo = pltpu.roll(lo, HEAD_WIDTH, 1)
            grad_pad[2 * j] = lo.astype(BF)
            grad_pad[2 * j + 1] = hi.astype(BF)
        key_sum[...] = jnp.zeros_like(key_sum)
        value_sum[...] = jnp.zeros_like(value_sum)

        @pl.loop(0, heads)
        def _(h):
            pair = h // (2 * group)
            keys = kv_all[:, pair].reshape(seq_len, LANES)
            values = kv_all[:, n_kv + pair].reshape(seq_len, LANES)
            scores = dot_t(keys, q_pad[h])
            scores = jnp.where(pos_q[0:1, :] >= pos_k[...], scores, NEG)
            weights = jnp.exp(scores - log_sum[pl.ds(h, 1), :])
            weight_grad = dot_t(values, grad_pad[h])
            inner = jnp.sum(weights * weight_grad, 0, keepdims=True)
            score_grad = (weights * (weight_grad - inner)).astype(BF)
            value_sum[pair] += jnp.dot(weights.astype(BF), grad_pad[h], preferred_element_type=F32)
            key_sum[pair] += jnp.dot(score_grad, q_pad[h], preferred_element_type=F32)
            query_out[h] = t_dot(keys, score_grad).T

        for j in range(n_q):
            side = (2 * j) // group % 2
            lo, hi = query_out[2 * j], query_out[2 * j + 1]
            if side == 0:
                hi = pltpu.roll(hi, HEAD_WIDTH, 1)
            else:
                lo = pltpu.roll(lo, HEAD_WIDTH, 1)
            u = jnp.where(low, lo, hi) * FACTOR
            partner = jnp.where(
                first, pltpu.roll(u, LANES - HEAD_WIDTH // 2, 1), pltpu.roll(u, HEAD_WIDTH // 2, 1)
            )
            turned = u * cosine[...] - partner * sine[...]
            query_grad[:, j * LANES : (j + 1) * LANES] = turned.astype(BF)
        for i in range(n_kv):
            kv_grad[:, i] = key_sum[i].astype(BF).reshape(contexts, rows, LANES)
            kv_grad[:, n_kv + i] = value_sum[i].astype(BF).reshape(contexts, rows, LANES)

    vmem = pl.BlockSpec(memory_space=pltpu.VMEM)
    return pl.pallas_call(
        kernel,
        name="attend_back",
        out_shape=(
            jax.ShapeDtypeStruct((rows, query_cols), BF),
            jax.ShapeDtypeStruct((contexts, 2 * n_kv, rows, LANES), BF),
        ),
        in_specs=[vmem] * 8,
        out_specs=(vmem, vmem),
        scratch_shapes=[
            pltpu.VMEM((heads, rows, LANES), BF),
            pltpu.VMEM((heads, rows, LANES), F32),
            pltpu.VMEM((n_kv, seq_len, LANES), F32),
            pltpu.VMEM((n_kv, seq_len, LANES), F32),
        ],
        compiler_params=pltpu.CompilerParams(vmem_limit_bytes=VMEM_LIMIT),
        cost_estimate=pl.CostEstimate(
            flops=10 * heads * rows * seq_len * LANES, bytes_accessed=8 * 10**6,
            transcendentals=heads * rows * seq_len,
        ),
    )


def shards(
    tokens,
    span_order,
    attn_gain,
    w_query,
    key_weight,
    value_weight,
    w_out,
    mlp_gain,
    w_gate,
    w_up,
    w_down,
    out_grad,
):
    planes = lax.axis_size("fsdp")
    contexts = lax.axis_size("context")
    z = lax.axis_index("fsdp")
    c = lax.axis_index("context")
    t = lax.axis_index("tensor")
    outers = contexts // 2
    o, k = c // 2, c % 2

    def swap_t(v):
        return lax.ppermute(v, "tensor", [(0, 1), (1, 0)])

    def swap_k(v):
        return lax.ppermute(v, "context", [(i, i ^ 1) for i in range(contexts)])

    def shift_o(v, by):
        return lax.ppermute(
            v,
            "context",
            [(i, ((i // 2 + by) % outers) * 2 + i % 2) for i in range(contexts)],
        )

    def shift_z(v, by):
        return lax.ppermute(v, "fsdp", [(i, (i + by) % planes) for i in range(planes)])

    def gather_context(piece):
        column = [piece] + [shift_o(piece, by) for by in range(1, outers)]
        other = swap_k(jnp.stack(column))
        found = []
        for by in range(outers):
            home = (o - by + outers) % outers
            found.append((home * 2 + k, column[by]))
            found.append((home * 2 + 1 - k, other[by]))
        return found

    def sum_context(part):
        shape = part.shape
        part = part.reshape(shape[0], outers, 2, *shape[2:])
        got = swap_k(pick(part, 1 - k, 2).astype(BF))
        total = pick(part, k, 2) + got.astype(F32)
        sums = pick(total, o, 1)
        for by in range(1, outers):
            sums = sums + shift_o(pick(total, (o + by) % outers, 1).astype(BF), by).astype(F32)
        return sums

    tok_own, cot_own = tokens[0], out_grad[0]
    rows, own_cols = tok_own.shape
    width = own_cols * 2
    depth = width // planes
    strip = depth // contexts
    units = w_gate.shape[1] // planes
    unit_strip = units // contexts

    def whole_cols(mine, theirs):
        return jnp.concatenate(
            [jnp.where(t == 0, mine, theirs), jnp.where(t == 0, theirs, mine)], -1
        )

    def own_half(v):
        return lax.dynamic_slice_in_dim(v, t * own_cols, own_cols, v.ndim - 1)

    def other_half(v):
        return lax.dynamic_slice_in_dim(v, (1 - t) * own_cols, own_cols, v.ndim - 1)

    query_cols = w_query.shape[1]
    kv_cols = key_weight.shape[1]
    half_rows = rows // 2
    slot = jnp.arange(rows, dtype=jnp.int32)

    def positions(index):
        spans = pick(span_order, index)
        return spans[slot // half_rows] * half_rows + slot % half_rows

    pos_mine = positions(c)
    pos_q = jnp.broadcast_to(pos_mine[None, :], (8, rows))
    pos_k = jnp.concatenate([positions(i) for i in range(contexts)])[:, None]
    angles = pos_mine.astype(F32)[:, None] * rope_freqs(HEAD_WIDTH)[None, :]
    cosine, sine = jnp.cos(angles), jnp.sin(angles)
    cosine_table = jnp.concatenate([cosine] * 4, 1)
    sine_table = jnp.concatenate([-sine, sine] * 2, 1)

    own_in = tok_own.astype(F32)
    qkv_own = jnp.concatenate([w_query, key_weight, value_weight], 1)
    gains_own = jnp.concatenate(
        [attn_gain[None], mlp_gain[None], jnp.zeros((GAIN_ROWS - 2, depth), BF)], 0
    )
    front = build_front(planes, contexts, rows, width, query_cols, kv_cols, units)
    (
        gate_w, up_w, down_w, cot_all, norm_all, qkv_w, out_w, gains, q_pad, kv_all, attn_low, log_sum,
        mid_own, first_normalized, resid_low,
    ) = front(
        tok_own, cot_own, gains_own, qkv_own, w_out, w_gate, w_up, w_down, cosine_table, sine_table,
        pos_q, pos_k,
    )
    gain_one, gain_two = gains[0].astype(F32), gains[1].astype(F32)
    resid_in = resid_low.astype(F32)
    scale_one = lax.rsqrt(jnp.mean(resid_in * resid_in, -1, keepdims=True) + EPS)

    def row_total(v):
        part = jnp.sum(v, -1)
        return (part + swap_t(part))[:, None]

    gain_one_own, gain_two_own = own_half(gain_one), own_half(gain_two)
    scale_two = lax.rsqrt(row_total(mid_own * mid_own) / width + EPS)
    normal_two = mid_own * scale_two

    normed_blocks, cot_blocks, hidden_blocks, unit_grad_blocks = [], [], [], []
    mlp_sum = None
    normed_grad = None
    for by in range(planes):
        home = (z - by + planes) % planes
        normed = pick(norm_all, home)
        cot = pick(cot_all, home)
        gate_val, up_val = dot(normed, gate_w), dot(normed, up_w)
        sigmoid_gate = jax.nn.sigmoid(gate_val)
        hidden = (gate_val * sigmoid_gate * up_val).astype(BF)
        hidden_grad = dot_t(cot, down_w)
        gate_grad = hidden_grad * up_val * sigmoid_gate * (1.0 + gate_val * (1.0 - sigmoid_gate))
        up_grad = hidden_grad * gate_val * sigmoid_gate
        gate_grad, up_grad = gate_grad.astype(BF), up_grad.astype(BF)
        unit_grad = jnp.concatenate([gate_grad, up_grad], 1)
        normed_part = dot_t(gate_grad, gate_w) + dot_t(up_grad, up_w)
        mlp_part = dot(hidden, down_w)
        grad_own = own_half(normed_part) + swap_t(other_half(normed_part).astype(BF)).astype(F32)
        mlp_own = own_half(mlp_part) + swap_t(other_half(mlp_part).astype(BF)).astype(F32)
        if by == 0:
            normed_grad, mlp_sum = grad_own, mlp_own
        else:
            normed_grad = normed_grad + shift_z(grad_own.astype(BF), planes - by).astype(F32)
            mlp_sum = mlp_sum + shift_z(mlp_own.astype(BF), planes - by).astype(F32)
        normed_blocks.append(normed)
        cot_blocks.append(cot)
        hidden_blocks.append(hidden)
        unit_grad_blocks.append(unit_grad)
    result = (mid_own + mlp_sum).astype(BF)

    normed_all = jnp.concatenate(normed_blocks, 0)
    hidden_all = jnp.concatenate(hidden_blocks, 0)
    unit_grad_all = jnp.concatenate(unit_grad_blocks, 0)
    cot_all = jnp.concatenate(cot_blocks, 0)
    gate_up_grad = t_dot(normed_all, unit_grad_all)
    down_grad = t_dot(hidden_all, cot_all)

    gate_up_sum = sum_context(gate_up_grad.reshape(planes, contexts, strip, 2 * units)).astype(BF)
    gate_strips = jnp.zeros((2, strip, planes * units), BF)
    for by in range(planes):
        home = (z - by + planes) % planes
        block = pick(gate_up_sum, (z + by) % planes)
        piece = block if by == 0 else shift_z(block, by)
        piece = jnp.stack([piece[:, :units], piece[:, units:]])
        gate_strips = place(gate_strips, piece, (0, 0, home * units))
    gate_out = jnp.zeros((depth, planes * units), F32)
    up_out = jnp.zeros((depth, planes * units), F32)
    for index, piece in gather_context(gate_strips):
        gate_out = place(gate_out, piece[0].astype(F32), (index * strip, 0))
        up_out = place(up_out, piece[1].astype(F32), (index * strip, 0))

    down_parts = down_grad.reshape(1, contexts, unit_strip, width)
    down_sum = sum_context(down_parts)[0].astype(BF)
    down_strips = jnp.zeros((planes, unit_strip, depth), BF)
    for by in range(planes):
        home = (z - by + planes) % planes
        block = lax.dynamic_slice_in_dim(down_sum, ((z + by) % planes) * depth, depth, 1)
        piece = block if by == 0 else shift_z(block, by)
        down_strips = place(down_strips, piece[None], (home, 0, 0))
    down_out = jnp.zeros((planes, contexts, unit_strip, depth), F32)
    for index, piece in gather_context(down_strips):
        down_out = place(down_out, piece[:, None].astype(F32), (0, index, 0, 0))
    down_out = down_out.reshape(planes * units, depth)

    def norm_backward(grad_out, normal, scale_row, gain):
        scaled = grad_out * gain
        gain_grad = jnp.sum(grad_out * normal, 0)
        inner = row_total(scaled * normal) / width
        return (gain_grad, scale_row * (scaled - normal * inner))

    gain_two_grad, mid_from_norm = norm_backward(normed_grad, normal_two, scale_two, gain_two_own)
    mid_grad = cot_own.astype(F32) + mid_from_norm
    mid_grad_own = mid_grad.astype(BF)
    mid_grad_low = whole_cols(mid_grad_own, swap_t(mid_grad_own))

    out_w_grad = t_dot(attn_low, mid_grad_low)
    attn_grad = dot_t(mid_grad_low, out_w).astype(BF)
    query_grad, kv_grad = build_attend_back(contexts, rows, query_cols, kv_cols)(
        q_pad, kv_all, attn_grad, log_sum, cosine_table, sine_table, pos_q, pos_k
    )
    kv_sum = sum_context(kv_grad[None].astype(F32))[0]
    n_kv = kv_cols // LANES
    key_grad = apply_rotary(
        kv_sum[:n_kv].reshape(n_kv, rows, 2, HEAD_WIDTH), cosine[:, None, :], -sine[:, None, :]
    )
    kv_tiles = jnp.concatenate([key_grad.reshape(n_kv, rows, LANES), kv_sum[n_kv:]], 0)
    qkv_grad = jnp.concatenate(
        [query_grad, kv_tiles.transpose(1, 0, 2).reshape(rows, 2 * kv_cols).astype(BF)], 1
    )
    qkv_w_grad = t_dot(first_normalized, qkv_grad)
    normed_one_part = dot_t(qkv_grad, qkv_w)
    normed_one_grad = own_half(normed_one_part) + swap_t(
        other_half(normed_one_part).astype(BF)
    ).astype(F32)
    gain_one_grad, in_from_norm = norm_backward(
        normed_one_grad, own_in * scale_one, scale_one, gain_one_own
    )
    input_result = (mid_grad + in_from_norm).astype(BF)

    def sum_planes(parts):
        total = pick(parts, z)
        for by in range(1, planes):
            total = total + shift_z(pick(parts, (z + by) % planes).astype(BF), by).astype(F32)
        return total

    out_rows = w_out.shape[0]
    out_strip_rows = out_rows // contexts
    out_sum = sum_context(out_w_grad.reshape(1, contexts, out_strip_rows, width))[0]
    out_sum = sum_planes(out_sum.reshape(out_strip_rows, planes, depth).transpose(1, 0, 2))
    out_out = jnp.zeros((out_rows, depth), F32)
    for index, piece in gather_context(out_sum.astype(BF)):
        out_out = place(out_out, piece.astype(F32), (index * out_strip_rows, 0))

    qkv_sum = sum_context(qkv_w_grad.reshape(planes, contexts, strip, -1))
    qkv_sum = sum_planes(qkv_sum)
    qkv_out = jnp.zeros((depth, qkv_own.shape[1]), F32)
    for index, piece in gather_context(qkv_sum.astype(BF)):
        qkv_out = place(qkv_out, piece.astype(F32), (index * strip, 0))

    gain_grads = lax.psum(jnp.stack([gain_one_grad, gain_two_grad]), ("fsdp", "context"))
    gain_all = whole_cols(gain_grads, swap_t(gain_grads))
    gain_out = lax.dynamic_slice_in_dim(gain_all, z * depth, depth, 1)
    return (
        result[None],
        input_result[None],
        gain_out[0],
        qkv_out[:, :query_cols],
        qkv_out[:, query_cols : query_cols + kv_cols],
        qkv_out[:, query_cols + kv_cols :],
        out_out,
        gain_out[1],
        gate_out,
        up_out,
        down_out,
    )


def solution(mesh):
    weight = P("fsdp", "tensor")
    turned = P("tensor", "fsdp")
    block = P("fsdp", "context", "tensor")
    gain = P("fsdp")
    return jax.shard_map(
        shards,
        mesh=mesh,
        in_specs=(
            block, P(), gain, weight, weight, weight, turned, gain, weight, weight, turned, block,
        ),
        out_specs=(
            block, block, gain, weight, weight, weight, turned, gain, weight, weight, turned,
        ),
        check_vma=False,
    )
```

time: 971 us -> 842 us (0.87); the launches traced: 955 us -> 836 us
  Pallas kernels: 0 us -> 262 us
  local copies, waits for them, and re-layouts: 196 us -> 95.8 us
  starting transfers between devices: 160 us -> 62.6 us
  waiting for transfers between devices: 296 us -> 200 us
  matrix products: 159 us -> 92.2 us
  other arithmetic: 96.4 us -> 77.4 us
    pallas_call x0 -> x2, Pallas kernels: none -> 262 us  [the longest x1 241 us: shards(): front(tok_own, cot_own, gains_own, qkv_own, w_out, w_gate, w_up, w_down,...]
    dynamic_update_slice x56 -> x7, local copies, waits for them, and re-layouts: 92 us -> 0.24 us  [place(): return lax.dynamic_update_slice(whole, block, starts)]
    ppermute x39 -> x18, starting transfers between devices: 114 us -> 40.4 us  [shift_z(): lax.ppermute(v, 'fsdp', [(i, (i + by) % planes) for i in range(planes)])]
    ppermute x39 -> x18, waiting for transfers between devices: 147 us -> 86.4 us  [shift_z(): lax.ppermute(v, 'fsdp', [(i, (i + by) % planes) for i in range(planes)])]
    dot_general x28 -> x0, matrix products: 41.3 us -> none  [the longest x4 9.76 us: attend_back(): jnp.einsum('gtd,ld->gtl', grad_block, value_block, preferred_element_type...]
    ppermute x24 -> x14, waiting for transfers between devices: 51.5 us -> 29.4 us  [swap_t(): return lax.ppermute(v, 'tensor', [(0, 1), (1, 0)])]
    dynamic_slice x1 -> x7, local copies, waits for them, and re-layouts: 0.08 us -> 17 us  [pick(): return lax.dynamic_index_in_dim(blocks, index, axis, keepdims=False)]
    dot_general x10 -> x12, matrix products: 41.9 us -> 26.1 us  [dot(): return jnp.dot(left, right, preferred_element_type=F32)]
  transfers between devices with their start and end apart: 107 -> 50, of which waited for: 37 -> 20; matrix products, arithmetic and copies ran while one was open for 46% -> 27% of each run, Pallas kernels for 0% -> 3%
where the time goes in v2:
time: 842 us; the launch traced here: 836 us
  Pallas kernels  262 us (31%)
  waiting for transfers between devices  200 us (24%)
  local copies, waits for them, and re-layouts  95.8 us (11%)
  matrix products  92.2 us (11%)
  other arithmetic  77.4 us (9%)
  starting transfers between devices  62.6 us (7%)
  blocking collectives  43.5 us (5%)
    pallas_call x1, Pallas kernels, shards(): front(tok_own, cot_own, gains_own, qkv_own, w_out, w_gate, w_up, w_down,...  241 us
    ppermute x18, waiting for transfers between devices, shift_z(): lax.ppermute(v, 'fsdp', [(i, (i + by) % planes) for i in range(planes)])  86.4 us
    ppermute x9, waiting for transfers between devices, shift_o(): lax.ppermute(v, 'context', [(i, (i // 2 + by) % outers * 2 + i % 2) for i...  83.5 us
    psum x1, blocking collectives, shards(): lax.psum(jnp.stack([gain_one_grad, gain_two_grad]), ('fsdp', 'context'))  43.5 us
    ppermute x18, starting transfers between devices, shift_z(): lax.ppermute(v, 'fsdp', [(i, (i + by) % planes) for i in range(planes)])  40.4 us
    dot_general x4, matrix products, t_dot(): lax.dot_general(left, right, (((0,), (0,)), ((), ())), preferred_element_...  33.9 us
    dot_general x14, matrix products, dot_t(): lax.dot_general(left, right, (((1,), (1,)), ((), ())), preferred_element_...  32.2 us
    ppermute x14, waiting for transfers between devices, swap_t(): return lax.ppermute(v, 'tensor', [(0, 1), (1, 0)])  29.4 us
  transfers between devices with their start and end apart: 50, of which 20 were waited for; matrix products, arithmetic and copies ran while one was open for 27% of the time, Pallas kernels for 3%

profile of v2, /device:TPU:0, one launch (start us, length us, event | category | flops | bytes accessed | tf_op | source)
XLA Modules:
  0.0 836.3 jit_solution(9849775461438941641)
XLA Ops:
  13.8 2.6 pad_maximum_fusion.2.qkv_own
  18.0 241.0 %front.1 = (bf16[2048,1024]{1,0:T(8,128)(2,1)}, bf16[2048,1024]{1,0:T(8,128)(2,1)}, bf16[1024,2048]{1,0:T(8,128)(2,1)}, bf16[4,256,2048]{2,1,0:T(8,128)(2,1)}, b...) custom-call(bf16[256,1024]{1,0:T(8,128)(2,1)} %bitcast.340, ...), custom_call_target="tpu_custom_call" | custom-call | flops 8000000000 | bytes 80000000 | tf_op jit(solution)/shard_map/front/pallas_call | solution.py:691
  262.4 4.2 dynamic-slice_bitcast_fusion.7
  273.8 2.6 multiply_convert_fusion
  279.8 4.3 convolution_add_fusion
  285.2 4.4 fusion.98
  320.6 18.2 %fusion.1 = f32[2048,2048]{1,0:T(8,128)} fusion(bf16[256,2048]{1,0:T(8,128)(2,1)} %copy-done.40, bf16[256,2048]{1,0:T(8,128)(2,1)} %get-tuple-element.60, bf16[256,2048]{1,0:T(8,128)(2,1)} %get-tuple-element.61, bf16[256,2048]{1,0:T(8,128)(2,1)} %get-tuple-element.58, bf16[256,1024]{1,0:T(8,128)(2,1)} %get-tuple-element.83, ...), kind=kOutput, calls=%fused_computation.5 | convolution fusion | flops 8640266240 | bytes 25165824 | tf_op jit(solution)/shard_map/dot_general | solution.py:52
  338.8 4.9 fusion.103
  343.8 2.8 fusion.100
  351.7 8.0 fusion.24
  360.9 6.0 fusion
  385.9 3.9 fusion.35
  391.9 2.6 collective-permute-done.14
  395.3 18.9 %collective-permute-done.12 = bf16[256,1024]{1,0:T(8,128)(2,1)S(1)} collective-permute-done((bf16[256,1024]{1,0:T(8,128)(2,1)}, bf16[256,1024]{1,0:T(8,128)(2,1)S(1)}, u32[]{:S(2)}, u32[]{:S(2)}) %collective-permute-start.12) | collective-permute-done | bytes 524320 | tf_op jit(solution)/shard_map/ppermute | solution.py:624
  419.4 16.0 %collective-permute-done.15 = f32[256]{0:T(256)S(1)} collective-permute-done((f32[256]{0:T(256)S(1)}, f32[256]{0:T(256)S(1)}, u32[]{:S(2)}, u32[]{:S(2)}) %collective-permute-start.15) | collective-permute-done | bytes 1056 | tf_op jit(solution)/shard_map/ppermute | solution.py:611
  444.4 5.7 collective-permute-done.16
  452.3 21.1 %attend_back.1 = (bf16[256,1024]{1,0:T(8,128)(2,1)}, bf16[4,4,256,128]{3,2,1,0:T(8,128)(2,1)}) custom-call(bf16[16,256,128]{2,1,0:T(8,128)(2,1)} %get-tuple-element.36.q_pad, bf16[4,4,256,128]{3,2,1,0:T(8,128)(2,1)} %get-tuple-element.37.kv_all, bf16[256,1024]{1,0:T(8,128)(2,1)} %convolution_convert_fusion.attn_grad, f32[16,256]{1,0:T(8,128)} %get-tuple-element.39.log_sum, ...), custom_call_target="tpu_custom_call" | custom-call | flops 5368709120 | bytes 8000000 | tf_op jit(solution)/shard_map/attend_back/pallas_call | solution.py:784
  479.0 5.9 fusion.50
  486.3 4.7 constant_dynamic-slice_fusion.2
  491.0 5.5 copy.57
  499.8 3.8 constant_dynamic-slice_fusion.1
  503.6 3.9 copy.69
  510.3 4.8 fusion.57
  516.2 3.4 bitcast_add_fusion.2
  520.8 7.8 collective-permute-done.19
  538.6 43.5 %psum.7 = f32[2,1024]{1,0:T(2,128)S(1)} all-reduce(f32[2,1024]{1,0:T(2,128)S(1)} %pad_maximum_fusion.15), channel_id=1, replica_groups=mesh['fsdp'=4,'context'=4,'tensor'=2] {'fsdp','context'}, use_global_device_ids=true, to_apply=%region_6.7 | all-reduce | flops 2048 | bytes 16384 | tf_op jit(solution)/shard_map/psum | solution.py:826
  583.4 4.1 fusion.52
  589.6 10.9 %collective-permute-done.45 = bf16[256,512]{1,0:T(8,128)(2,1)S(1)} collective-permute-done((bf16[256,512]{1,0:T(8,128)(2,1)S(1)}, bf16[256,512]{1,0:T(8,128)(2,1)S(1)}, u32[]{:S(2)}, u32[]{:S(2)}) %collective-permute-start.45) | collective-permute-done | bytes 262176 | tf_op jit(solution)/shard_map/ppermute | solution.py:624
  604.5 6.5 collective-permute-done.46
  612.1 5.9 bitcast_add_fusion
  618.1 12.1 %collective-permute-done.30 = bf16[1,256,2048]{1,2,0:T(8,128)(2,1)} collective-permute-done((bf16[1,256,2048]{1,2,0:T(8,128)(2,1)}, bf16[1,256,2048]{1,2,0:T(8,128)(2,1)}, u32[]{:S(2)}, u32[]{:S(2)}) %collective-permute-start.30) | collective-permute-done | bytes 1048608 | tf_op jit(solution)/shard_map/ppermute | solution.py:617
  634.7 2.7 collective-permute-start.32
  639.5 12.0 %collective-permute-start.31 = (bf16[256,512]{0,1:T(8,128)(2,1)S(1)}, bf16[256,512]{0,1:T(8,128)(2,1)S(1)}, u32[]{:S(2)}, u32[]{:S(2)}) collective-permute-start(bf16[256,512]{0,1:T(8,128)(2,1)S(1)} %get-tuple-element.71), channel_id=1, source_target_pairs={{0,8},{8,16},{16,24},{24,0},{1,9},{9,17},{17,25},{25,1},{2,10},{10... | collective-permute-start | bytes 786440 | tf_op jit(solution)/shard_map/ppermute | solution.py:624
  655.9 2.7 pad_maximum_fusion.1
  659.1 41.5 %collective-permute-done.34 = bf16[256,512]{0,1:T(8,128)(2,1)S(1)} collective-permute-done((bf16[256,512]{0,1:T(8,128)(2,1)S(1)}, bf16[256,512]{0,1:T(8,128)(2,1)S(1)}, u32[]{:S(2)}, u32[]{:S(2)}) %collective-permute-start.34) | collective-permute-done | bytes 262176 | tf_op jit(solution)/shard_map/ppermute | solution.py:617
  701.6 4.9 bitcast_add_fusion.1
  709.2 3.5 fusion.32
  722.1 9.1 %collective-permute-done.38 = bf16[128,2048]{1,0:T(8,128)(2,1)} collective-permute-done((bf16[128,2048]{1,0:T(8,128)(2,1)}, bf16[128,2048]{1,0:T(8,128)(2,1)}, u32[]{:S(2)}, u32[]{:S(2)}) %collective-permute-start.38) | collective-permute-done | bytes 524320 | tf_op jit(solution)/shard_map/ppermute | solution.py:624
  732.2 20.7 %collective-permute-done.39 = bf16[128,2048]{1,0:T(8,128)(2,1)S(1)} collective-permute-done((bf16[128,2048]{1,0:T(8,128)(2,1)}, bf16[128,2048]{1,0:T(8,128)(2,1)S(1)}, u32[]{:S(2)}, u32[]{:S(2)}) %collective-permute-start.39) | collective-permute-done | bytes 524320 | tf_op jit(solution)/shard_map/ppermute | solution.py:624
  754.7 3.7 convert_dynamic-update-slice_fusion.2
  758.4 2.8 convert_dynamic-update-slice_fusion.1
  761.2 2.8 convert_dynamic-update-slice_fusion
  766.2 11.2 %collective-permute-start.26 = (bf16[128,1536]{1,0:T(8,128)(2,1)S(1)}, bf16[128,1536]{1,0:T(8,128)(2,1)S(1)}, u32[]{:S(2)}, u32[]{:S(2)}) collective-permute-start(bf16[128,1536]{1,0:T(8,128)(2,1)S(1)} %get-tuple-element.65), channel_id=1, source_target_pairs={{0,24},{8,0},{16,8},{24,16},{1,25},{9,1},{17,9},{25,17},{2,26},{10... | collective-permute-start | bytes 1179656 | tf_op jit(solution)/shard_map/ppermute | solution.py:624
  779.3 21.4 %collective-permute-done.41 = bf16[2,128,4096]{2,1,0:T(8,128)(2,1)S(1)} collective-permute-done((bf16[2,128,4096]{2,1,0:T(8,128)(2,1)S(1)}, bf16[2,128,4096]{2,1,0:T(8,128)(2,1)S(1)}, u32[]{:S(2)}, u32[]{:S(2)}) %collective-permute-start.41) | collective-permute-done | bytes 2097184 | tf_op jit(solution)/shard_map/ppermute | solution.py:617
  801.2 12.1 %collective-permute-done.25 = bf16[128,1536]{1,0:T(8,128)(2,1)S(1)} collective-permute-done((bf16[128,1536]{1,0:T(8,128)(2,1)S(1)}, bf16[128,1536]{1,0:T(8,128)(2,1)S(1)}, u32[]{:S(2)}, u32[]{:S(2)}) %collective-permute-start.25) | collective-permute-done | bytes 393248 | tf_op jit(solution)/shard_map/ppermute | solution.py:624
  816.1 7.8 collective-permute-done.27
  830.4 2.9 copy-done.11
  833.4 2.8 copy-done.9
  (364 shorter events, 179.3 us)
Async XLA Ops:
  260.4 129.4 %collective-permute-start.7 = (f32[256]{0:T(256)S(1)}, f32[256]{0:T(256)S(1)}, u32[]{:S(2)}, u32[]{:S(2)}) collective-permute-start(f32[256]{0:T(256)S(1)} %multiply_reduce_fusion.5), channel_id=1, source_target_pairs={{0,1},{1,0},{2,3},{3,2},{4,5},{5,4},{6,7},{7,6},{8,9},{9,8},{10,11... | collective-permute-start | bytes 3080 | tf_op jit(solution)/shard_map/ppermute | solution.py:611
  285.1 90.4 %collective-permute-start.13 = (bf16[256,1024]{1,0:T(8,128)(2,1)}, bf16[256,1024]{1,0:T(8,128)(2,1)}, u32[]{:S(2)}, u32[]{:S(2)}) collective-permute-start(bf16[256,1024]{1,0:T(8,128)(2,1)} %dynamic-slice_convert_fusion.7), channel_id=1, source_target_pairs={{0,1},{1,0},{2,3},{3,2},{4,5},{5,4},{6,7},{7,6},{8,9},{9,8},{10,11... | collective-permute-start | bytes 1572872 | tf_op jit(solution)/shard_map/ppermute | solution.py:611
  298.4 79.1 %collective-permute-start.11 = (bf16[256,1024]{1,0:T(8,128)(2,1)}, bf16[256,1024]{1,0:T(8,128)(2,1)}, u32[]{:S(2)}, u32[]{:S(2)}) collective-permute-start(bf16[256,1024]{1,0:T(8,128)(2,1)} %dynamic-slice_convert_fusion.8), channel_id=1, source_target_pairs={{0,1},{1,0},{2,3},{3,2},{4,5},{5,4},{6,7},{7,6},{8,9},{9,8},{10,11... | collective-permute-start | bytes 1572872 | tf_op jit(solution)/shard_map/ppermute | solution.py:611
  308.4 73.6 %collective-permute-start.9 = (bf16[256,1024]{1,0:T(8,128)(2,1)}, bf16[256,1024]{1,0:T(8,128)(2,1)}, u32[]{:S(2)}, u32[]{:S(2)}) collective-permute-start(bf16[256,1024]{1,0:T(8,128)(2,1)} %dynamic-slice_convert_fusion.9), channel_id=1, source_target_pairs={{0,1},{1,0},{2,3},{3,2},{4,5},{5,4},{6,7},{7,6},{8,9},{9,8},{10,11... | collective-permute-start | bytes 1572872 | tf_op jit(solution)/shard_map/ppermute | solution.py:611
  319.4 71.2 %collective-permute-start.8 = (bf16[256,1024]{1,0:T(8,128)(2,1)}, bf16[256,1024]{1,0:T(8,128)(2,1)}, u32[]{:S(2)}, u32[]{:S(2)}) collective-permute-start(bf16[256,1024]{1,0:T(8,128)(2,1)} %dynamic-slice_convert_fusion.10), channel_id=1, source_target_pairs={{0,1},{1,0},{2,3},{3,2},{4,5},{5,4},{6,7},{7,6},{8,9},{9,8},{10,11... | collective-permute-start | bytes 1572872 | tf_op jit(solution)/shard_map/ppermute | solution.py:611
  377.5 17.0 %collective-permute-start.14 = (bf16[256,1024]{1,0:T(8,128)(2,1)}, bf16[256,1024]{1,0:T(8,128)(2,1)S(1)}, u32[]{:S(2)}, u32[]{:S(2)}) collective-permute-start(bf16[256,1024]{1,0:T(8,128)(2,1)} %add_convert_fusion.1), channel_id=1, source_target_pairs={{0,8},{8,16},{16,24},{24,0},{1,9},{9,17},{17,25},{25,1},{2,10},{10... | collective-permute-start | bytes 1572872 | tf_op jit(solution)/shard_map/ppermute | solution.py:624
  379.9 34.3 %collective-permute-start.12 = (bf16[256,1024]{1,0:T(8,128)(2,1)}, bf16[256,1024]{1,0:T(8,128)(2,1)S(1)}, u32[]{:S(2)}, u32[]{:S(2)}) collective-permute-start(bf16[256,1024]{1,0:T(8,128)(2,1)} %add_convert_fusion.2), channel_id=1, source_target_pairs={{0,16},{8,24},{16,0},{24,8},{1,17},{9,25},{17,1},{25,9},{2,18},{10... | collective-permute-start | bytes 1572872 | tf_op jit(solution)/shard_map/ppermute | solution.py:624
  383.9 31.2 %collective-permute-start.10 = (bf16[256,1024]{1,0:T(8,128)(2,1)}, bf16[256,1024]{1,0:T(8,128)(2,1)S(1)}, u32[]{:S(2)}, u32[]{:S(2)}) collective-permute-start(bf16[256,1024]{1,0:T(8,128)(2,1)} %add_convert_fusion.3), channel_id=1, source_target_pairs={{0,24},{8,0},{16,8},{24,16},{1,25},{9,1},{17,9},{25,17},{2,26},{10... | collective-permute-start | bytes 1572872 | tf_op jit(solution)/shard_map/ppermute | solution.py:624
  389.8 45.9 %collective-permute-start.5 = (bf16[256,1024]{1,0:T(8,128)(2,1)}, bf16[256,1024]{1,0:T(8,128)(2,1)}, u32[]{:S(2)}, u32[]{:S(2)}) collective-permute-start(bf16[256,1024]{1,0:T(8,128)(2,1)} %dynamic-slice_convert_fusion.11), channel_id=1, source_target_pairs={{0,1},{1,0},{2,3},{3,2},{4,5},{5,4},{6,7},{7,6},{8,9},{9,8},{10,11... | collective-permute-start | bytes 1572872 | tf_op jit(solution)/shard_map/ppermute | solution.py:611
  390.5 48.7 %collective-permute-start.3 = (bf16[256,1024]{1,0:T(8,128)(2,1)}, bf16[256,1024]{1,0:T(8,128)(2,1)}, u32[]{:S(2)}, u32[]{:S(2)}) collective-permute-start(bf16[256,1024]{1,0:T(8,128)(2,1)} %dynamic-slice_convert_fusion.12), channel_id=1, source_target_pairs={{0,1},{1,0},{2,3},{3,2},{4,5},{5,4},{6,7},{7,6},{8,9},{9,8},{10,11... | collective-permute-start | bytes 1572872 | tf_op jit(solution)/shard_map/ppermute | solution.py:611
  394.5 47.1 %collective-permute-start.1 = (bf16[256,1024]{1,0:T(8,128)(2,1)}, bf16[256,1024]{1,0:T(8,128)(2,1)}, u32[]{:S(2)}, u32[]{:S(2)}) collective-permute-start(bf16[256,1024]{1,0:T(8,128)(2,1)} %dynamic-slice_convert_fusion.13), channel_id=1, source_target_pairs={{0,1},{1,0},{2,3},{3,2},{4,5},{5,4},{6,7},{7,6},{8,9},{9,8},{10,11... | collective-permute-start | bytes 1572872 | tf_op jit(solution)/shard_map/ppermute | solution.py:611
  414.2 117.8 %collective-permute-start = (bf16[256,1024]{1,0:T(8,128)(2,1)}, bf16[256,1024]{1,0:T(8,128)(2,1)}, u32[]{:S(2)}, u32[]{:S(2)}) collective-permute-start(bf16[256,1024]{1,0:T(8,128)(2,1)} %dynamic-slice_convert_fusion.14), channel_id=1, source_target_pairs={{0,1},{1,0},{2,3},{3,2},{4,5},{5,4},{6,7},{7,6},{8,9},{9,8},{10,11... | collective-permute-start | bytes 1572872 | tf_op jit(solution)/shard_map/ppermute | solution.py:611
  418.2 17.1 %collective-permute-start.15 = (f32[256]{0:T(256)S(1)}, f32[256]{0:T(256)S(1)}, u32[]{:S(2)}, u32[]{:S(2)}) collective-permute-start(f32[256]{0:T(256)S(1)} %get-tuple-element.48), channel_id=1, source_target_pairs={{0,1},{1,0},{2,3},{3,2},{4,5},{5,4},{6,7},{7,6},{8,9},{9,8},{10,11... | collective-permute-start | bytes 3080 | tf_op jit(solution)/shard_map/ppermute | solution.py:611
  435.3 176.8 %collective-permute-start.36 = (bf16[4,2,128,2048]{3,2,1,0:T(8,128)(2,1)}, bf16[4,2,128,2048]{3,2,1,0:T(8,128)(2,1)}, u32[]{:S(2)}, u32[]{:S(2)}) collective-permute-start(bf16[4,2,128,2048]{3,2,1,0:T(8,128)(2,1)} %fusion), channel_id=1, source_target_pairs={{0,2},{2,0},{4,6},{6,4},{1,3},{3,1},{5,7},{7,5},{8,10},{10,8},{12,... | collective-permute-start | bytes 12582920 | tf_op jit(solution)/shard_map/ppermute | solution.py:614
  435.7 14.4 %collective-permute-start.16 = (bf16[256,1024]{1,0:T(8,128)(2,1)S(1)}, bf16[256,1024]{1,0:T(8,128)(2,1)S(1)}, u32[]{:S(2)}, u32[]{:S(2)}) collective-permute-start(bf16[256,1024]{1,0:T(8,128)(2,1)S(1)} %fusion.85), channel_id=1, source_target_pairs={{0,1},{1,0},{2,3},{3,2},{4,5},{5,4},{6,7},{7,6},{8,9},{9,8},{10,11... | collective-permute-start | bytes 1572872 | tf_op jit(solution)/shard_map/ppermute | solution.py:611
  439.2 76.0 %collective-permute-start.43 = (bf16[1,2,256,2048]{3,2,1,0:T(8,128)(2,1)}, bf16[1,2,256,2048]{3,2,1,0:T(8,128)(2,1)}, u32[]{:S(2)}, u32[]{:S(2)}) collective-permute-start(bf16[1,2,256,2048]{3,2,1,0:T(8,128)(2,1)} %fusion.35), channel_id=1, source_target_pairs={{0,2},{2,0},{4,6},{6,4},{1,3},{3,1},{5,7},{7,5},{8,10},{10,8},{12,... | collective-permute-start | bytes 6291464 | tf_op jit(solution)/shard_map/ppermute | solution.py:614
  441.6 92.1 %collective-permute-start.6 = (bf16[256,1024]{1,0:T(8,128)(2,1)}, bf16[256,1024]{1,0:T(8,128)(2,1)}, u32[]{:S(2)}, u32[]{:S(2)}) collective-permute-start(bf16[256,1024]{1,0:T(8,128)(2,1)} %add_convert_fusion.5), channel_id=1, source_target_pairs={{0,8},{8,16},{16,24},{24,0},{1,9},{9,17},{17,25},{25,1},{2,10},{10... | collective-permute-start | bytes 1572872 | tf_op jit(solution)/shard_map/ppermute | solution.py:624
  479.0 17.4 %collective-permute-start.17 = (bf16[1,2,4,256,128]{3,4,2,1,0:T(8,128)(2,1)}, bf16[1,2,4,256,128]{3,4,2,1,0:T(8,128)(2,1)}, u32[]{:S(2)}, u32[]{:S(2)}) collective-permute-start(bf16[1,2,4,256,128]{3,4,2,1,0:T(8,128)(2,1)} %bitcast.348), channel_id=1, source_target_pairs={{0,2},{2,0},{4,6},{6,4},{1,3},{3,1},{5,7},{7,5},{8,10},{10,8},{12,... | collective-permute-start | bytes 1572872 | tf_op jit(solution)/shard_map/ppermute | solution.py:614
  499.3 8.9 %collective-permute-start.18 = (bf16[1,4,256,128]{2,3,1,0:T(8,128)(2,1)}, bf16[1,4,256,128]{2,3,1,0:T(8,128)(2,1)S(1)}, u32[]{:S(2)}, u32[]{:S(2)}) collective-permute-start(bf16[1,4,256,128]{2,3,1,0:T(8,128)(2,1)} %fusion.61), channel_id=1, source_target_pairs={{0,4},{2,6},{4,0},{6,2},{1,5},{3,7},{5,1},{7,3},{8,12},{10,14},{12... | collective-permute-start | bytes 786440 | tf_op jit(solution)/shard_map/ppermute | solution.py:617
  508.2 73.9 %collective-permute-start.4 = (bf16[256,1024]{1,0:T(8,128)(2,1)}, bf16[256,1024]{1,0:T(8,128)(2,1)}, u32[]{:S(2)}, u32[]{:S(2)}) collective-permute-start(bf16[256,1024]{1,0:T(8,128)(2,1)} %add_convert_fusion.6), channel_id=1, source_target_pairs={{0,16},{8,24},{16,0},{24,8},{1,17},{9,25},{17,1},{25,9},{2,18},{10... | collective-permute-start | bytes 1572872 | tf_op jit(solution)/shard_map/ppermute | solution.py:624
  515.3 13.3 %collective-permute-start.19 = (bf16[256,1024]{1,0:T(8,128)(2,1)S(1)}, bf16[256,1024]{1,0:T(8,128)(2,1)S(1)}, u32[]{:S(2)}, u32[]{:S(2)}) collective-permute-start(bf16[256,1024]{1,0:T(8,128)(2,1)S(1)} %dynamic-slice_convert_fusion.6), channel_id=1, source_target_pairs={{0,1},{1,0},{2,3},{3,2},{4,5},{5,4},{6,7},{7,6},{8,9},{9,8},{10,11... | collective-permute-start | bytes 1572872 | tf_op jit(solution)/shard_map/ppermute | solution.py:611
  532.0 50.2 %collective-permute-start.2 = (bf16[256,1024]{1,0:T(8,128)(2,1)}, bf16[256,1024]{1,0:T(8,128)(2,1)}, u32[]{:S(2)}, u32[]{:S(2)}) collective-permute-start(bf16[256,1024]{1,0:T(8,128)(2,1)} %add_convert_fusion.7), channel_id=1, source_target_pairs={{0,24},{8,0},{16,8},{24,16},{1,25},{9,1},{17,9},{25,17},{2,26},{10... | collective-permute-start | bytes 1572872 | tf_op jit(solution)/shard_map/ppermute | solution.py:624
  533.7 66.9 %collective-permute-start.29 = (bf16[1,2,256,2048]{2,3,1,0:T(8,128)(2,1)}, bf16[1,2,256,2048]{2,3,1,0:T(8,128)(2,1)}, u32[]{:S(2)}, u32[]{:S(2)}) collective-permute-start(bf16[1,2,256,2048]{2,3,1,0:T(8,128)(2,1)} %bitcast.268), channel_id=1, source_target_pairs={{0,2},{2,0},{4,6},{6,4},{1,3},{3,1},{5,7},{7,5},{8,10},{10,8},{12,... | collective-permute-start | bytes 6291464 | tf_op jit(solution)/shard_map/ppermute | solution.py:614
  533.7 53.8 %collective-permute-start.44 = (bf16[1,256,2048]{2,1,0:T(8,128)(2,1)}, bf16[1,256,2048]{2,1,0:T(8,128)(2,1)}, u32[]{:S(2)}, u32[]{:S(2)}) collective-permute-start(bf16[1,256,2048]{2,1,0:T(8,128)(2,1)} %fusion.46), channel_id=1, source_target_pairs={{0,4},{2,6},{4,0},{6,2},{1,5},{3,7},{5,1},{7,3},{8,12},{10,14},{12... | collective-permute-start | bytes 3145736 | tf_op jit(solution)/shard_map/ppermute | solution.py:617
  582.1 119.5 %collective-permute-start.22 = (bf16[4,2,128,1536]{3,2,0,1:T(8,128)(2,1)}, bf16[4,2,128,1536]{3,2,0,1:T(8,128)(2,1)}, u32[]{:S(2)}, u32[]{:S(2)}) collective-permute-start(bf16[4,2,128,1536]{3,2,0,1:T(8,128)(2,1)} %fusion.33), channel_id=1, source_target_pairs={{0,2},{2,0},{4,6},{6,4},{1,3},{3,1},{5,7},{7,5},{8,10},{10,8},{12,... | collective-permute-start | bytes 9437192 | tf_op jit(solution)/shard_map/ppermute | solution.py:614
  582.2 7.3 collective-permute-start.21
  589.4 11.1 %collective-permute-start.45 = (bf16[256,512]{1,0:T(8,128)(2,1)S(1)}, bf16[256,512]{1,0:T(8,128)(2,1)S(1)}, u32[]{:S(2)}, u32[]{:S(2)}) collective-permute-start(bf16[256,512]{1,0:T(8,128)(2,1)S(1)} %get-tuple-element.88), channel_id=1, source_target_pairs={{0,8},{8,16},{16,24},{24,0},{1,9},{9,17},{17,25},{25,1},{2,10},{10... | collective-permute-start | bytes 786440 | tf_op jit(solution)/shard_map/ppermute | solution.py:624
  589.6 21.4 %collective-permute-start.46 = (bf16[256,512]{1,0:T(8,128)(2,1)S(1)}, bf16[256,512]{1,0:T(8,128)(2,1)S(1)}, u32[]{:S(2)}, u32[]{:S(2)}) collective-permute-start(bf16[256,512]{1,0:T(8,128)(2,1)S(1)} %get-tuple-element.87), channel_id=1, source_target_pairs={{0,16},{8,24},{16,0},{24,8},{1,17},{9,25},{17,1},{25,9},{2,18},{10... | collective-permute-start | bytes 786440 | tf_op jit(solution)/shard_map/ppermute | solution.py:624
  600.5 11.5 %collective-permute-start.47 = (bf16[256,512]{1,0:T(8,128)(2,1)S(1)}, bf16[256,512]{1,0:T(8,128)(2,1)S(1)}, u32[]{:S(2)}, u32[]{:S(2)}) collective-permute-start(bf16[256,512]{1,0:T(8,128)(2,1)S(1)} %get-tuple-element.86), channel_id=1, source_target_pairs={{0,24},{8,0},{16,8},{24,16},{1,25},{9,1},{17,9},{25,17},{2,26},{10... | collective-permute-start | bytes 786440 | tf_op jit(solution)/shard_map/ppermute | solution.py:624
  603.7 26.4 %collective-permute-start.30 = (bf16[1,256,2048]{1,2,0:T(8,128)(2,1)}, bf16[1,256,2048]{1,2,0:T(8,128)(2,1)}, u32[]{:S(2)}, u32[]{:S(2)}) collective-permute-start(bf16[1,256,2048]{1,2,0:T(8,128)(2,1)} %fusion.45), channel_id=1, source_target_pairs={{0,4},{2,6},{4,0},{6,2},{1,5},{3,7},{5,1},{7,3},{8,12},{10,14},{12... | collective-permute-start | bytes 3145736 | tf_op jit(solution)/shard_map/ppermute | solution.py:617
  612.0 43.9 %collective-permute-start.48 = (bf16[4,256,512]{2,1,0:T(8,128)(2,1)S(1)}, bf16[4,256,512]{2,1,0:T(8,128)(2,1)}, u32[]{:S(2)}, u32[]{:S(2)}) collective-permute-start(bf16[4,256,512]{2,1,0:T(8,128)(2,1)S(1)} %bitcast_dynamic-update-slice_fusion), channel_id=1, source_target_pairs={{0,4},{2,6},{4,0},{6,2},{1,5},{3,7},{5,1},{7,3},{8,12},{10,14},{12... | collective-permute-start | bytes 3145736 | tf_op jit(solution)/shard_map/ppermute | solution.py:617
  631.7 7.8 collective-permute-start.33
  633.4 75.8 %collective-permute-start.37 = (bf16[4,128,2048]{2,1,0:T(8,128)(2,1)}, bf16[4,128,2048]{2,1,0:T(8,128)(2,1)}, u32[]{:S(2)}, u32[]{:S(2)}) collective-permute-start(bf16[4,128,2048]{2,1,0:T(8,128)(2,1)} %fusion.34), channel_id=1, source_target_pairs={{0,4},{2,6},{4,0},{6,2},{1,5},{3,7},{5,1},{7,3},{8,12},{10,14},{12... | collective-permute-start | bytes 6291464 | tf_op jit(solution)/shard_map/ppermute | solution.py:617
  634.7 19.0 %collective-permute-start.32 = (bf16[256,512]{0,1:T(8,128)(2,1)S(1)}, bf16[256,512]{0,1:T(8,128)(2,1)S(1)}, u32[]{:S(2)}, u32[]{:S(2)}) collective-permute-start(bf16[256,512]{0,1:T(8,128)(2,1)S(1)} %get-tuple-element.73), channel_id=1, source_target_pairs={{0,16},{8,24},{16,0},{24,8},{1,17},{9,25},{17,1},{25,9},{2,18},{10... | collective-permute-start | bytes 786440 | tf_op jit(solution)/shard_map/ppermute | solution.py:624
  639.5 15.9 %collective-permute-start.31 = (bf16[256,512]{0,1:T(8,128)(2,1)S(1)}, bf16[256,512]{0,1:T(8,128)(2,1)S(1)}, u32[]{:S(2)}, u32[]{:S(2)}) collective-permute-start(bf16[256,512]{0,1:T(8,128)(2,1)S(1)} %get-tuple-element.71), channel_id=1, source_target_pairs={{0,8},{8,16},{16,24},{24,0},{1,9},{9,17},{17,25},{25,1},{2,10},{10... | collective-permute-start | bytes 786440 | tf_op jit(solution)/shard_map/ppermute | solution.py:624
  655.5 45.0 %collective-permute-start.34 = (bf16[256,512]{0,1:T(8,128)(2,1)S(1)}, bf16[256,512]{0,1:T(8,128)(2,1)S(1)}, u32[]{:S(2)}, u32[]{:S(2)}) collective-permute-start(bf16[256,512]{0,1:T(8,128)(2,1)S(1)} %fusion.55), channel_id=1, source_target_pairs={{0,4},{2,6},{4,0},{6,2},{1,5},{3,7},{5,1},{7,3},{8,12},{10,14},{12... | collective-permute-start | bytes 786440 | tf_op jit(solution)/shard_map/ppermute | solution.py:617
  658.6 96.1 %collective-permute-start.49 = (bf16[2,4,256,512]{3,2,1,0:T(8,128)(2,1)}, bf16[2,4,256,512]{3,2,1,0:T(8,128)(2,1)}, u32[]{:S(2)}, u32[]{:S(2)}) collective-permute-start(bf16[2,4,256,512]{3,2,1,0:T(8,128)(2,1)} %pad_maximum_fusion.1), channel_id=1, source_target_pairs={{0,2},{2,0},{4,6},{6,4},{1,3},{3,1},{5,7},{7,5},{8,10},{10,8},{12,... | collective-permute-start | bytes 6291464 | tf_op jit(solution)/shard_map/ppermute | solution.py:614
  700.6 15.2 %collective-permute-start.35 = (bf16[2,256,512]{1,2,0:T(8,128)(2,1)S(1)}, bf16[2,256,512]{1,2,0:T(8,128)(2,1)}, u32[]{:S(2)}, u32[]{:S(2)}) collective-permute-start(bf16[2,256,512]{1,2,0:T(8,128)(2,1)S(1)} %pad_maximum_fusion.8), channel_id=1, source_target_pairs={{0,2},{2,0},{4,6},{6,4},{1,3},{3,1},{5,7},{7,5},{8,10},{10,8},{12,... | collective-permute-start | bytes 1572872 | tf_op jit(solution)/shard_map/ppermute | solution.py:614
  708.0 56.1 %collective-permute-start.23 = (bf16[4,128,1536]{2,1,0:T(8,128)(2,1)}, bf16[4,128,1536]{2,1,0:T(8,128)(2,1)}, u32[]{:S(2)}, u32[]{:S(2)}) collective-permute-start(bf16[4,128,1536]{2,1,0:T(8,128)(2,1)} %fusion.44), channel_id=1, source_target_pairs={{0,4},{2,6},{4,0},{6,2},{1,5},{3,7},{5,1},{7,3},{8,12},{10,14},{12... | collective-permute-start | bytes 4718600 | tf_op jit(solution)/shard_map/ppermute | solution.py:617
  714.1 17.0 %collective-permute-start.38 = (bf16[128,2048]{1,0:T(8,128)(2,1)}, bf16[128,2048]{1,0:T(8,128)(2,1)}, u32[]{:S(2)}, u32[]{:S(2)}) collective-permute-start(bf16[128,2048]{1,0:T(8,128)(2,1)} %get-tuple-element.69), channel_id=1, source_target_pairs={{0,8},{8,16},{16,24},{24,0},{1,9},{9,17},{17,25},{25,1},{2,10},{10... | collective-permute-start | bytes 1572872 | tf_op jit(solution)/shard_map/ppermute | solution.py:624
  718.1 34.8 %collective-permute-start.39 = (bf16[128,2048]{1,0:T(8,128)(2,1)}, bf16[128,2048]{1,0:T(8,128)(2,1)S(1)}, u32[]{:S(2)}, u32[]{:S(2)}) collective-permute-start(bf16[128,2048]{1,0:T(8,128)(2,1)} %get-tuple-element.68), channel_id=1, source_target_pairs={{0,16},{8,24},{16,0},{24,8},{1,17},{9,25},{17,1},{25,9},{2,18},{10... | collective-permute-start | bytes 1572872 | tf_op jit(solution)/shard_map/ppermute | solution.py:624
  718.2 34.8 %collective-permute-start.40 = (bf16[128,2048]{1,0:T(8,128)(2,1)}, bf16[128,2048]{1,0:T(8,128)(2,1)S(1)}, u32[]{:S(2)}, u32[]{:S(2)}) collective-permute-start(bf16[128,2048]{1,0:T(8,128)(2,1)} %get-tuple-element.67), channel_id=1, source_target_pairs={{0,24},{8,0},{16,8},{24,16},{1,25},{9,1},{17,9},{25,17},{2,26},{10... | collective-permute-start | bytes 1572872 | tf_op jit(solution)/shard_map/ppermute | solution.py:624
  753.2 47.6 %collective-permute-start.41 = (bf16[2,128,4096]{2,1,0:T(8,128)(2,1)S(1)}, bf16[2,128,4096]{2,1,0:T(8,128)(2,1)S(1)}, u32[]{:S(2)}, u32[]{:S(2)}) collective-permute-start(bf16[2,128,4096]{2,1,0:T(8,128)(2,1)S(1)} %maximum_dynamic-update-slice_fusion.3), channel_id=1, source_target_pairs={{0,4},{2,6},{4,0},{6,2},{1,5},{3,7},{5,1},{7,3},{8,12},{10,14},{12... | collective-permute-start | bytes 6291464 | tf_op jit(solution)/shard_map/ppermute | solution.py:617
  766.2 35.1 %collective-permute-start.26 = (bf16[128,1536]{1,0:T(8,128)(2,1)S(1)}, bf16[128,1536]{1,0:T(8,128)(2,1)S(1)}, u32[]{:S(2)}, u32[]{:S(2)}) collective-permute-start(bf16[128,1536]{1,0:T(8,128)(2,1)S(1)} %get-tuple-element.65), channel_id=1, source_target_pairs={{0,24},{8,0},{16,8},{24,16},{1,25},{9,1},{17,9},{25,17},{2,26},{10... | collective-permute-start | bytes 1179656 | tf_op jit(solution)/shard_map/ppermute | solution.py:624
  777.3 36.0 %collective-permute-start.25 = (bf16[128,1536]{1,0:T(8,128)(2,1)S(1)}, bf16[128,1536]{1,0:T(8,128)(2,1)S(1)}, u32[]{:S(2)}, u32[]{:S(2)}) collective-permute-start(bf16[128,1536]{1,0:T(8,128)(2,1)S(1)} %get-tuple-element.66), channel_id=1, source_target_pairs={{0,16},{8,24},{16,0},{24,8},{1,17},{9,25},{17,1},{25,9},{2,18},{10... | collective-permute-start | bytes 1179656 | tf_op jit(solution)/shard_map/ppermute | solution.py:624
  779.3 34.0 %collective-permute-start.24 = (bf16[128,1536]{1,0:T(8,128)(2,1)S(1)}, bf16[128,1536]{1,0:T(8,128)(2,1)S(1)}, u32[]{:S(2)}, u32[]{:S(2)}) collective-permute-start(bf16[128,1536]{1,0:T(8,128)(2,1)S(1)} %get-tuple-element.64), channel_id=1, source_target_pairs={{0,8},{8,16},{16,24},{24,0},{1,9},{9,17},{17,25},{25,1},{2,10},{10... | collective-permute-start | bytes 1179656 | tf_op jit(solution)/shard_map/ppermute | solution.py:624
  801.1 28.0 %collective-permute-start.42 = (bf16[2,2,128,4096]{3,2,1,0:T(8,128)(2,1)S(1)}, bf16[2,2,128,4096]{3,2,1,0:T(8,128)(2,1)S(1)}, u32[]{:S(2)}, u32[]{:S(2)}) collective-permute-start(bf16[2,2,128,4096]{3,2,1,0:T(8,128)(2,1)S(1)} %pad_maximum_fusion), channel_id=1, source_target_pairs={{0,2},{2,0},{4,6},{6,4},{1,3},{3,1},{5,7},{7,5},{8,10},{10,8},{12,... | collective-permute-start | bytes 12582920 | tf_op jit(solution)/shard_map/ppermute | solution.py:614
  813.9 9.9 %collective-permute-start.27 = (bf16[128,1536]{1,0:T(8,128)(2,1)S(1)}, bf16[128,1536]{1,0:T(8,128)(2,1)S(1)}, u32[]{:S(2)}, u32[]{:S(2)}) collective-permute-start(bf16[128,1536]{1,0:T(8,128)(2,1)S(1)} %get-tuple-element.50), channel_id=1, source_target_pairs={{0,4},{2,6},{4,0},{6,2},{1,5},{3,7},{5,1},{7,3},{8,12},{10,14},{12... | collective-permute-start | bytes 1179656 | tf_op jit(solution)/shard_map/ppermute | solution.py:617
  (68 other events, 567.6 us)

commit v3 on v2

--- a/solution.py
+++ b/solution.py
@@ -13,9 +13,10 @@
 BF = jnp.bfloat16
 F32 = jnp.float32
 LANES = 128
+TILE = 256
 GAIN_ROWS = 16
 FACTOR = 1.0 / math.sqrt(HEAD_WIDTH)
-VMEM_LIMIT = 60 * 2**20
+VMEM_LIMIT = 62 * 2**20
 MESH = pl.DeviceIdType.MESH
 
 
@@ -31,33 +32,12 @@
     )
 
 
-def apply_rotary(values, cosine_table, sine_table):
-    half_size = values.shape[-1] // 2
-    first = values[..., :half_size]
-    second = values[..., half_size:]
-    return jnp.concatenate(
-        [first * cosine_table - second * sine_table, second * cosine_table + first * sine_table], -1
-    )
-
-
-def dot(left, right):
-    return jnp.dot(left, right, preferred_element_type=F32)
-
-
 def dot_t(left, right):
     return lax.dot_general(left, right, (((1,), (1,)), ((), ())), preferred_element_type=F32)
 
 
 def t_dot(left, right):
     return lax.dot_general(left, right, (((0,), (0,)), ((), ())), preferred_element_type=F32)
-
-
-def pick(blocks, index, axis=0):
-    return lax.dynamic_index_in_dim(blocks, index, axis, keepdims=False)
-
-
-def place(whole, block, starts):
-    return lax.dynamic_update_slice(whole, block, starts)
 
 
 def build_front(planes, contexts, rows, width, query_cols, kv_cols, units):
@@ -77,7 +57,7 @@
     def kernel(
         tok, cot, gains_own, qkv_own, out_own, gate_own, up_own, down_own, cosine, sine, pos_q, pos_k,
         gate_w, up_w, down_w, cot_all, norm_all, qkv_w, out_w, gains, q_pad, kv_all, attn, log_sum,
-        mid_own, normed_one, tok_all,
+        mid_own, normed_one, tok_all, scales,
         lin, heads_out, send_half, recv_half, norm_own, sq_send, sq_recv,
         z_send, z_recv, y_send, y_recv, k_send, k_recv, x_send, x_recv, own_sem,
     ):
@@ -251,6 +231,7 @@
             copy(there, there, z_send.at[GAIN, p, 0], z_recv.at[GAIN, p], at_k).wait_recv()
         x = tok_all[...].astype(F32)
         scale = lax.rsqrt(jnp.mean(x * x, -1, keepdims=True) + EPS)
+        scales[0] = jnp.broadcast_to(scale, (rows, LANES))
         normed_one[...] = (x * scale * gains[0:1, :].astype(F32)).astype(BF)
 
         for p in order:
@@ -404,6 +385,7 @@
         sq_copy.start()
         sq_copy.wait_recv()
         scale_two = lax.rsqrt((squares + sq_recv[:, 0:1]) * (1.0 / width) + EPS)
+        scales[1] = jnp.broadcast_to(scale_two, (rows, LANES))
         gain_two = gains[1:2, pl.ds(pl.multiple_of(t * half, half), half)].astype(F32)
         norm_own[...] = (mid_own[...] * scale_two * gain_two).astype(BF)
 
@@ -474,9 +456,10 @@
             shape((rows, half), F32),
             shape((rows, width), BF),
             shape((rows, width), BF),
+            shape((2, rows, LANES), F32),
         ),
         in_specs=[vmem, hbm, vmem, hbm, hbm, hbm, hbm, hbm, vmem, vmem, vmem, vmem],
-        out_specs=(hbm,) * 5 + (vmem,) * 10,
+        out_specs=(hbm,) * 5 + (vmem,) * 11,
         scratch_shapes=[
             pltpu.VMEM((qkv_cols // LANES, rows, LANES), F32),
             pltpu.VMEM((heads, rows, LANES), F32),
@@ -502,86 +485,901 @@
     )
 
 
-def build_attend_back(contexts, rows, query_cols, kv_cols):
+def add_strips(total, terms, chunk):
+    lead, size, _ = total.shape
+    steps = size // chunk
+
+    @pl.loop(0, lead * steps)
+    def _(i):
+        a, r = i // steps, pl.ds(pl.multiple_of(lax.rem(i, steps) * chunk, chunk), chunk)
+        found = terms[0][a, r, :].astype(F32)
+        for term in terms[1:]:
+            found = found + term[a, r, :].astype(F32)
+        total[a, r, :] = found.astype(BF)
+
+
+class Ring:
+    def __init__(self, planes, contexts):
+        self.planes, self.outers = planes, contexts // 2
+        self.z = z = lax.axis_index("fsdp")
+        self.c = c = lax.axis_index("context")
+        self.t = t = lax.axis_index("tensor")
+        self.o, self.k = c // 2, c % 2
+        self.at_k = (z, self.o * 2 + 1 - self.k, t)
+        self.at_x = (z, c, 1 - t)
+
+    def at_z(self, p):
+        return (p, self.c, self.t)
+
+    def at_o(self, other):
+        return (self.z, other * 2 + self.k, self.t)
+
+    def after(self, by):
+        return lax.rem(self.o + by, self.outers)
+
+    def before(self, by):
+        return lax.rem(self.o - by + self.outers, self.outers)
+
+    def plane(self, by):
+        return lax.rem(self.z + by, self.planes)
+
+    def greet(self):
+        barrier = pltpu.get_barrier_semaphore()
+        peers = [self.at_z(self.plane(s)) for s in range(1, self.planes)]
+        peers += [self.at_o(self.after(s)) for s in range(1, self.outers)] + [self.at_k, self.at_x]
+        for peer in peers:
+            pl.semaphore_signal(barrier, inc=1, device_id=peer, device_id_type=MESH)
+        pl.semaphore_wait(barrier, len(peers))
+
+    def by_distance(self):
+        order = []
+        for i in range(self.planes - 1):
+            p = jnp.int32(0)
+            for plane in range(self.planes):
+                far = sorted((abs(q - plane), q) for q in range(self.planes) if q != plane)
+                p = p + jnp.where(self.z == plane, far[i][1], 0)
+            order.append(p)
+        return order
+
+
+def copy_to(src, dst, send_sem, recv_sem, device):
+    return pltpu.make_async_remote_copy(
+        src_ref=src, dst_ref=dst, send_sem=send_sem, recv_sem=recv_sem, device_id=device, device_id_type=MESH
+    )
+
+
+class Reduction:
+    def __init__(self, ring, item, part, core_in, outer_out, outer_in, strip_sum, sems):
+        self.ring, self.item, self.part = ring, item, part
+        self.core_in, self.outer_out, self.outer_in, self.strip_sum = core_in, outer_out, outer_in, strip_sum
+        self.k_send, self.k_recv, self.y_send, self.y_recv = sems
+        self.chunk = 32 if strip_sum.shape[2] > 1024 else 64
+        self.chunk = min(self.chunk, strip_sum.shape[1])
+
+    def core_copy(self, other):
+        g = self.ring
+        return copy_to(
+            self.part.at[:, other * 2 + 1 - g.k], self.core_in.at[other],
+            self.k_send.at[self.item, other], self.k_recv.at[self.item, other], g.at_k,
+        )
+
+    def to_core(self):
+        for other in range(self.ring.outers):
+            self.core_copy(other).start()
+
+    def outer_copy(self, by):
+        g = self.ring
+        return copy_to(
+            self.outer_out.at[by - 1], self.outer_in.at[by - 1],
+            self.y_send.at[self.item, by], self.y_recv.at[self.item, by], g.at_o(g.after(by)),
+        )
+
+    def from_core(self):
+        g = self.ring
+        for other in range(g.outers):
+            self.core_copy(other).wait_recv()
+        for by in range(1, g.outers):
+            goal = g.after(by)
+            add_strips(
+                self.outer_out.at[by - 1], [self.part.at[:, goal * 2 + g.k], self.core_in.at[goal]], self.chunk
+            )
+            self.outer_copy(by).start()
+        add_strips(self.strip_sum, [self.part.at[:, g.c], self.core_in.at[g.o]], self.chunk)
+
+    def core_done(self):
+        for other in range(self.ring.outers):
+            self.core_copy(other).wait_send()
+
+    def from_outer(self):
+        for by in range(1, self.ring.outers):
+            self.outer_copy(by).wait_recv()
+        terms = [self.strip_sum] + [self.outer_in.at[by - 1] for by in range(1, self.ring.outers)]
+        if len(terms) > 1:
+            add_strips(self.strip_sum, terms, self.chunk)
+
+    def outer_done(self):
+        for by in range(1, self.ring.outers):
+            self.outer_copy(by).wait_send()
+
+
+def rotate_tile(u, cosine, sine, first):
+    partner = jnp.where(
+        first, pltpu.roll(u, LANES - HEAD_WIDTH // 2, 1), pltpu.roll(u, HEAD_WIDTH // 2, 1)
+    )
+    return u * cosine + partner * sine
+
+
+def store_part(part, i, tile):
+    size = part.shape[2]
+    per = part.shape[1] * size // TILE
+    for r in range(TILE // size):
+        part[i // per, lax.rem(i, per) * (TILE // size) + r] = tile[r * size : (r + 1) * size].astype(BF)
+
+
+def build_back(planes, contexts, rows, width, query_cols, kv_cols, units):
+    outers = contexts // 2
+    half = width // 2
+    depth = width // planes
+    strip = depth // contexts
+    unit_strip = units // contexts
     seq_len = rows * contexts
     n_q, n_kv = query_cols // LANES, kv_cols // LANES
     heads = query_cols // HEAD_WIDTH
     group = query_cols // kv_cols
+    qkv_cols = query_cols + 2 * kv_cols
+    DOWN, GATE, UP, KV = range(4)
+    lots = max(outers - 1, 1)
 
     def kernel(
-        q_pad, kv_all, attn_grad, log_sum, cosine, sine, pos_q, pos_k, query_grad, kv_grad,
-        grad_pad, query_out, key_sum, value_sum,
+        gate_hbm, up_hbm, down_hbm, norm_hbm, cot_hbm, qkv_hbm, out_hbm, q_hbm, kv_hbm, mid_hbm, tok_hbm,
+        gains, cosine, sine, pos_q, pos_k, log_sum, scales,
+        result, input_grad, gate_strip, up_strip, down_strip, mid_full, qkv_grad, gain_rows,
+        norm_x_in, mlp_x_in, norm_z_in, mlp_z_in, norm_x_out, mlp_x_out, norm_sum, mlp_sum,
+        row_core_in, col_core_in, row_outer_in, col_outer_in, row_outer_out, col_outer_out, row_sum, col_sum,
+        kv_core_in, kv_outer_in, sq_out, sq_in, first_x_out, first_x_in,
+        x_send, x_recv, z_send, z_recv, k_send, k_recv, y_send, y_recv, grad_send, grad_recv, load_sem, credit,
     ):
-        lane = lax.broadcasted_iota(jnp.int32, (rows, LANES), 1)
-        first = lax.rem(lane, HEAD_WIDTH) < HEAD_WIDTH // 2
-        low = lane < HEAD_WIDTH
-        for j in range(n_q):
-            u = attn_grad[:, j * LANES : (j + 1) * LANES].astype(F32)
-            side = (2 * j) // group % 2
-            lo = jnp.where(low, u, 0.0)
-            hi = jnp.where(low, 0.0, u)
-            if side == 0:
-                hi = pltpu.roll(hi, HEAD_WIDTH, 1)
-            else:
-                lo = pltpu.roll(lo, HEAD_WIDTH, 1)
-            grad_pad[2 * j] = lo.astype(BF)
-            grad_pad[2 * j + 1] = hi.astype(BF)
-        key_sum[...] = jnp.zeros_like(key_sum)
-        value_sum[...] = jnp.zeros_like(value_sum)
-
-        @pl.loop(0, heads)
-        def _(h):
-            pair = h // (2 * group)
-            keys = kv_all[:, pair].reshape(seq_len, LANES)
-            values = kv_all[:, n_kv + pair].reshape(seq_len, LANES)
-            scores = dot_t(keys, q_pad[h])
-            scores = jnp.where(pos_q[0:1, :] >= pos_k[...], scores, NEG)
-            weights = jnp.exp(scores - log_sum[pl.ds(h, 1), :])
-            weight_grad = dot_t(values, grad_pad[h])
-            inner = jnp.sum(weights * weight_grad, 0, keepdims=True)
-            score_grad = (weights * (weight_grad - inner)).astype(BF)
-            value_sum[pair] += jnp.dot(weights.astype(BF), grad_pad[h], preferred_element_type=F32)
-            key_sum[pair] += jnp.dot(score_grad, q_pad[h], preferred_element_type=F32)
-            query_out[h] = t_dot(keys, score_grad).T
-
-        for j in range(n_q):
-            side = (2 * j) // group % 2
-            lo, hi = query_out[2 * j], query_out[2 * j + 1]
-            if side == 0:
-                hi = pltpu.roll(hi, HEAD_WIDTH, 1)
-            else:
-                lo = pltpu.roll(lo, HEAD_WIDTH, 1)
-            u = jnp.where(low, lo, hi) * FACTOR
-            partner = jnp.where(
-                first, pltpu.roll(u, LANES - HEAD_WIDTH // 2, 1), pltpu.roll(u, HEAD_WIDTH // 2, 1)
+        ring = Ring(planes, contexts)
+        z, c, t, k, o = ring.z, ring.c, ring.t, ring.k, ring.o
+        order = ring.by_distance()
+        blocks = order[::-1] + [z]
+        ring.greet()
+        own_cols = pl.multiple_of(t * half, half)
+        other_cols = pl.multiple_of((1 - t) * half, half)
+        n_half = half // TILE
+
+        def x_copy(i, src, dst):
+            return copy_to(src, dst, x_send.at[i], x_recv.at[i], ring.at_x)
+
+        NORM, MLP, MID, SQ_TWO, FIRST, SQ_ONE = 0, planes, 2 * planes, 2 * planes + 1, 2 * planes + 2, 2 * planes + 3
+
+        def norm_x(i):
+            return x_copy(NORM + i, norm_x_out.at[i % 2], norm_x_in.at[blocks[i]])
+
+        def mlp_x(p):
+            return x_copy(MLP + p, mlp_x_out.at[p], mlp_x_in.at[p])
+
+        def back_from(p, here):
+            return lax.rem(p - here + planes, planes) - 1
+
+        def norm_z(p):
+            return copy_to(
+                norm_sum.at[p], norm_z_in.at[back_from(z, p)], z_send.at[0, p], z_recv.at[0, z], ring.at_z(p)
             )
-            turned = u * cosine[...] - partner * sine[...]
-            query_grad[:, j * LANES : (j + 1) * LANES] = turned.astype(BF)
-        for i in range(n_kv):
-            kv_grad[:, i] = key_sum[i].astype(BF).reshape(contexts, rows, LANES)
-            kv_grad[:, n_kv + i] = value_sum[i].astype(BF).reshape(contexts, rows, LANES)
-
-    vmem = pl.BlockSpec(memory_space=pltpu.VMEM)
-    return pl.pallas_call(
-        kernel,
-        name="attend_back",
-        out_shape=(
-            jax.ShapeDtypeStruct((rows, query_cols), BF),
-            jax.ShapeDtypeStruct((contexts, 2 * n_kv, rows, LANES), BF),
-        ),
-        in_specs=[vmem] * 8,
-        out_specs=(vmem, vmem),
-        scratch_shapes=[
+
+        def mlp_z(p):
+            return copy_to(
+                mlp_sum.at[p], mlp_z_in.at[back_from(z, p)], z_send.at[1, p], z_recv.at[1, z], ring.at_z(p)
+            )
+
+        def z_wait(i, dst, p):
+            there = dst.at[back_from(p, z)]
+            copy_to(there, there, z_send.at[i, p], z_recv.at[i, p], ring.at_k).wait_recv()
+
+        def add_block(total, other, p):
+            n = rows // 64
+
+            @pl.loop(0, n)
+            def _(i):
+                r = pl.ds(pl.multiple_of(i * 64, 64), 64)
+                total[p, r, :] = (total[p, r, :].astype(F32) + other[p, r, :].astype(F32)).astype(BF)
+
+        def norm_on(i):
+            norm_x(i).wait_recv()
+            add_block(norm_sum, norm_x_in, blocks[i])
+
+        def mlp_on(p):
+            mlp_x(p).wait_recv()
+            add_block(mlp_sum, mlp_x_in, p)
+
+        sems = (k_send, k_recv, y_send, y_recv)
+
+        def feed_forward(norm, cot, hid, gate_grad, up_grad):
+            def load(i, src, dst):
+                one = pltpu.make_async_copy(src, dst, load_sem.at[i])
+                one.start()
+                return one
+
+            loads = [
+                (load(2 * i, norm_hbm.at[p], norm.at[p]), load(2 * i + 1, cot_hbm.at[p], cot.at[p]))
+                for i, p in enumerate(blocks)
+            ]
+
+            def with_weights(gate_w, up_w, down_w):
+                weights = [
+                    load(2 * planes, gate_hbm, gate_w),
+                    load(2 * planes + 1, up_hbm, up_w),
+                    load(2 * planes + 2, down_hbm, down_w),
+                ]
+                for one in weights:
+                    one.wait()
+                for i, p in enumerate(blocks):
+                    loads[i][0].wait()
+                    loads[i][1].wait()
+
+                    @pl.loop(0, units // TILE)
+                    def _(j):
+                        cols = pl.ds(pl.multiple_of(j * TILE, TILE), TILE)
+                        gate = jnp.dot(norm[p], gate_w[:, cols], preferred_element_type=F32)
+                        up = jnp.dot(norm[p], up_w[:, cols], preferred_element_type=F32)
+                        grad = dot_t(cot[p], down_w[cols, :])
+                        sig = jax.nn.sigmoid(gate)
+                        act = gate * sig
+                        hid[p, :, cols] = (act * up).astype(BF)
+                        gate_grad[p, :, cols] = (grad * up * sig * (1.0 + gate * (1.0 - sig))).astype(BF)
+                        up_grad[p, :, cols] = (grad * act).astype(BF)
+
+                    def norm_tile(at):
+                        r = pl.ds(pl.multiple_of(at, TILE), TILE)
+                        return dot_t(gate_grad[p], gate_w[r, :]) + dot_t(up_grad[p], up_w[r, :])
+
+                    def mlp_tile(at):
+                        r = pl.ds(pl.multiple_of(at, TILE), TILE)
+                        return jnp.dot(hid[p], down_w[:, r], preferred_element_type=F32)
+
+                    def halves(tile_of, out, total, start):
+                        @pl.loop(0, n_half)
+                        def _(j):
+                            here = pl.ds(pl.multiple_of(j * TILE, TILE), TILE)
+                            out[:, here] = tile_of(other_cols + j * TILE).astype(BF)
+
+                        start()
+
+                        @pl.loop(0, n_half)
+                        def _(j):
+                            here = pl.ds(pl.multiple_of(j * TILE, TILE), TILE)
+                            total[p, :, here] = tile_of(own_cols + j * TILE).astype(BF)
+
+                    if i > 1:
+                        norm_x(i - 2).wait_send()
+                    halves(norm_tile, norm_x_out.at[i % 2], norm_sum, lambda: norm_x(i).start())
+                    if i > 0:
+                        norm_on(i - 1)
+                        norm_z(blocks[i - 1]).start()
+                    halves(mlp_tile, mlp_x_out.at[p], mlp_sum, lambda: None)
+
+            pl.run_scoped(
+                with_weights,
+                pltpu.VMEM((width, units), BF), pltpu.VMEM((width, units), BF), pltpu.VMEM((units, width), BF),
+            )
+
+            def with_parts(row_part, col_part):
+                down = Reduction(
+                    ring, DOWN, col_part, col_core_in, col_outer_out, col_outer_in, col_sum, sems
+                )
+                gate = Reduction(
+                    ring, GATE, row_part, row_core_in, row_outer_out.at[0], row_outer_in.at[0], row_sum.at[0], sems
+                )
+                up = Reduction(
+                    ring, UP, row_part, row_core_in, row_outer_out.at[1], row_outer_in.at[1], row_sum.at[1], sems
+                )
+
+                def product(part, left, right):
+                    total = planes * rows
+
+                    @pl.loop(0, left.shape[2] // TILE)
+                    def _(i):
+                        cols = pl.ds(pl.multiple_of(i * TILE, TILE), TILE)
+                        tile = t_dot(left[:, :, cols].reshape(total, TILE), right[...].reshape(total, right.shape[2]))
+                        store_part(part, i, tile)
+
+                product(col_part, hid, cot)
+                down.to_core()
+                norm_on(planes - 1)
+                product(row_part, norm, gate_grad)
+                gate.to_core()
+                down.from_core()
+                gate.from_core()
+                gate.core_done()
+                pl.semaphore_signal(credit, inc=1, device_id=ring.at_k, device_id_type=MESH)
+                product(row_part, norm, up_grad)
+                pl.semaphore_wait(credit, 1)
+                up.to_core()
+                up.from_core()
+                up.core_done()
+                down.core_done()
+
+            pl.run_scoped(
+                with_parts,
+                pltpu.VMEM((planes, contexts, strip, units), BF), pltpu.VMEM((1, contexts, unit_strip, width), BF),
+            )
+
+        block_bf = pltpu.VMEM((planes, rows, width), BF)
+        unit_bf = pltpu.VMEM((planes, rows, units), BF)
+        pl.run_scoped(feed_forward, block_bf, block_bf, unit_bf, unit_bf, unit_bf)
+
+        down = Reduction(ring, DOWN, None, None, col_outer_out, col_outer_in, col_sum, sems)
+        gate = Reduction(ring, GATE, None, None, row_outer_out.at[0], row_outer_in.at[0], row_sum.at[0], sems)
+        up = Reduction(ring, UP, None, None, row_outer_out.at[1], row_outer_in.at[1], row_sum.at[1], sems)
+
+        def strip_src(item, goal):
+            if item == DOWN:
+                return col_sum.at[0, :, pl.ds(pl.multiple_of(goal * depth, depth), depth)]
+            return row_sum.at[0 if item == GATE else 1, goal]
+
+        def strip_dst(item, home):
+            if item == DOWN:
+                return down_strip.at[home]
+            return (gate_strip if item == GATE else up_strip).at[:, pl.ds(pl.multiple_of(home * units, units), units)]
+
+        def strip_copy(item, s):
+            goal = ring.plane(s)
+            return copy_to(
+                strip_src(item, goal), strip_dst(item, z), grad_send.at[item, s], grad_recv.at[item, z], ring.at_z(goal)
+            )
+
+        def strip_keep(item):
+            return pltpu.make_async_copy(strip_src(item, z), strip_dst(item, z), grad_send.at[item, 0])
+
+        def to_planes(item, reduction):
+            reduction.from_outer()
+            for s in range(1, planes):
+                strip_copy(item, s).start()
+            strip_keep(item).start()
+
+        def attention(mid, mid_grad, q_pad, kv_all, tok, grad_pad, query_out, key_sum, value_sum, kv_grad, kv_out):
+            loads = [
+                pltpu.make_async_copy(mid_hbm, mid, load_sem.at[0]),
+                pltpu.make_async_copy(tok_hbm.at[:, pl.ds(own_cols, half)], tok, load_sem.at[1]),
+                pltpu.make_async_copy(q_hbm, q_pad, load_sem.at[2]),
+                pltpu.make_async_copy(kv_hbm, kv_all, load_sem.at[3]),
+                pltpu.make_async_copy(cot_hbm.at[z, :, pl.ds(own_cols, half)], first_x_out, load_sem.at[4]),
+            ]
+            for one in loads:
+                one.start()
+            for one in loads:
+                one.wait()
+            key_sum[...] = jnp.zeros_like(key_sum)
+            value_sum[...] = jnp.zeros_like(value_sum)
+            gain_rows[...] = jnp.zeros_like(gain_rows)
+
+            def norm_back(grad, normal, scale, gain, gain_row, i):
+                scaled = grad * gain
+                gain_rows[gain_row : gain_row + 1, :] = jnp.sum(grad * normal, 0, keepdims=True)
+                mine = jnp.sum(scaled * normal, -1, keepdims=True)
+                sq_out[i] = jnp.broadcast_to(mine, (rows, LANES))
+                swap = x_copy(SQ_TWO if i == 0 else SQ_ONE, sq_out.at[i], sq_in.at[i])
+                swap.start()
+                swap.wait()
+                inner = (mine + sq_in[i][:, 0:1]) * (1.0 / width)
+                return scale * (scaled - normal * inner)
+
+            for p in order:
+                z_wait(0, norm_z_in, p)
+            grad = norm_sum[z].astype(F32)
+            for p in order:
+                grad = grad + norm_z_in[back_from(p, z)].astype(F32)
+            scale_two = scales[1][:, 0:1]
+            gain_two = gains[1:2, pl.ds(own_cols, half)].astype(F32)
+            back = norm_back(grad, mid[...] * scale_two, scale_two, gain_two, 1, 0)
+            mid_grad[...] = first_x_out[...].astype(F32) + back
+            mine = mid_full.at[:, pl.ds(own_cols, half)]
+            mid_full[:, pl.ds(own_cols, half)] = mid_grad[...].astype(BF)
+            mid_swap = x_copy(MID, mine, mine)
+            mid_swap.start()
+            for p in blocks:
+                mlp_x(p).start()
+            to_planes(DOWN, down)
+            mid_swap.wait_recv()
+
+            lane = lax.broadcasted_iota(jnp.int32, (rows, LANES), 1)
+            first = lax.rem(lane, HEAD_WIDTH) < HEAD_WIDTH // 2
+            low = lane < HEAD_WIDTH
+
+            def with_out(out_w):
+                one = pltpu.make_async_copy(out_hbm, out_w, load_sem.at[0])
+                one.start()
+                one.wait()
+
+                @pl.loop(0, query_cols // TILE)
+                def _(i):
+                    r = pl.ds(pl.multiple_of(i * TILE, TILE), TILE)
+                    found = dot_t(mid_full[...], out_w[r, :])
+                    for half_tile in range(TILE // LANES):
+                        j = i * (TILE // LANES) + half_tile
+                        u = found[:, half_tile * LANES : (half_tile + 1) * LANES]
+                        u = u.astype(BF).astype(F32)
+                        side = lax.rem((2 * j) // group, 2)
+                        lo = jnp.where(low, u, 0.0)
+                        hi = jnp.where(low, 0.0, u)
+                        grad_pad[2 * j] = jnp.where(side == 0, lo, pltpu.roll(lo, HEAD_WIDTH, 1)).astype(BF)
+                        grad_pad[2 * j + 1] = jnp.where(side == 1, hi, pltpu.roll(hi, HEAD_WIDTH, 1)).astype(BF)
+
+            pl.run_scoped(with_out, pltpu.VMEM((query_cols, width), BF))
+
+            def attend_back(first_head, last_head):
+                @pl.loop(first_head, last_head)
+                def _(h):
+                    pair = h // (2 * group)
+                    keys = kv_all[:, pair].reshape(seq_len, LANES)
+                    values = kv_all[:, n_kv + pair].reshape(seq_len, LANES)
+                    scores = dot_t(keys, q_pad[h])
+                    scores = jnp.where(pos_q[0:1, :] >= pos_k[...], scores, NEG)
+                    weights = jnp.exp(scores - log_sum[pl.ds(h, 1), :])
+                    weight_grad = dot_t(values, grad_pad[h])
+                    inner = jnp.sum(weights * weight_grad, 0, keepdims=True)
+                    score_grad = (weights * (weight_grad - inner)).astype(BF)
+                    value_sum[pair] += jnp.dot(weights.astype(BF), grad_pad[h], preferred_element_type=F32)
+                    key_sum[pair] += jnp.dot(score_grad, q_pad[h], preferred_element_type=F32)
+                    query_out[h] = t_dot(keys, score_grad).T
+
+            attend_back(0, heads // 2)
+            mlp_on(blocks[0])
+            mlp_z(blocks[0]).start()
+            attend_back(heads // 2, heads)
+            for i in range(n_kv):
+                kv_grad[:, i] = key_sum[i].astype(BF).reshape(contexts, rows, LANES)
+                kv_grad[:, n_kv + i] = value_sum[i].astype(BF).reshape(contexts, rows, LANES)
+
+            def kv_core(other):
+                return copy_to(
+                    kv_grad.at[other * 2 + 1 - k], kv_core_in.at[other], k_send.at[KV, other], k_recv.at[KV, other],
+                    ring.at_k,
+                )
+
+            def kv_outer(by):
+                return copy_to(
+                    kv_out.at[by - 1], kv_outer_in.at[by - 1], y_send.at[KV, by], y_recv.at[KV, by],
+                    ring.at_o(ring.after(by)),
+                )
+
+            for other in range(outers):
+                kv_core(other).start()
+            to_planes(GATE, gate)
+            for j in range(n_q):
+                side = (2 * j) // group % 2
+                lo, hi = query_out[2 * j], query_out[2 * j + 1]
+                if side == 0:
+                    hi = pltpu.roll(hi, HEAD_WIDTH, 1)
+                else:
+                    lo = pltpu.roll(lo, HEAD_WIDTH, 1)
+                u = jnp.where(low, lo, hi) * FACTOR
+                qkv_grad[:, j * LANES : (j + 1) * LANES] = rotate_tile(u, cosine[...], -sine[...], first).astype(BF)
+            for other in range(outers):
+                kv_core(other).wait_recv()
+            for by in range(1, outers):
+                goal = ring.after(by)
+                kv_out[by - 1] = (
+                    kv_grad[goal * 2 + k].astype(F32) + kv_core_in[goal].astype(F32)
+                ).astype(BF)
+                kv_outer(by).start()
+            kv_sum = kv_grad[c].astype(F32) + kv_core_in[o].astype(F32)
+            for by in range(1, outers):
+                kv_outer(by).wait_recv()
+                kv_sum = kv_sum + kv_outer_in[by - 1].astype(F32)
+            for i in range(n_kv):
+                at = query_cols + i * LANES
+                qkv_grad[:, at : at + LANES] = rotate_tile(kv_sum[i], cosine[...], -sine[...], first).astype(BF)
+                qkv_grad[:, at + kv_cols : at + kv_cols + LANES] = kv_sum[n_kv + i].astype(BF)
+            for other in range(outers):
+                kv_core(other).wait_send()
+            for by in range(1, outers):
+                kv_outer(by).wait_send()
+
+            first_swap = x_copy(FIRST, first_x_out, first_x_in)
+
+            def with_qkv(qkv_w, own):
+                one = pltpu.make_async_copy(qkv_hbm, qkv_w, load_sem.at[0])
+                one.start()
+                one.wait()
+
+                def tile_of(at):
+                    return dot_t(qkv_grad[...], qkv_w[pl.ds(pl.multiple_of(at, TILE), TILE), :])
+
+                @pl.loop(0, n_half)
+                def _(j):
+                    here = pl.ds(pl.multiple_of(j * TILE, TILE), TILE)
+                    first_x_out[:, here] = tile_of(other_cols + j * TILE).astype(BF)
+
+                first_swap.start()
+
+                @pl.loop(0, n_half)
+                def _(j):
+                    here = pl.ds(pl.multiple_of(j * TILE, TILE), TILE)
+                    own[:, here] = tile_of(own_cols + j * TILE)
+
+                for p in blocks[1:]:
+                    mlp_on(p)
+                    if p is not z:
+                        mlp_z(p).start()
+                first_swap.wait()
+                scale_one = scales[0][:, 0:1]
+                gain_one = gains[0:1, pl.ds(own_cols, half)].astype(F32)
+                back = norm_back(
+                    own[...] + first_x_in[...].astype(F32), tok[...].astype(F32) * scale_one, scale_one, gain_one, 0, 1
+                )
+                input_grad[...] = (mid_grad[...] + back).astype(BF)
+
+            pl.run_scoped(with_qkv, pltpu.VMEM((width, qkv_cols), BF), pltpu.VMEM((rows, half), F32))
+            to_planes(UP, up)
+            mid_swap.wait_send()
+            total = mid[...] + mlp_sum[z].astype(F32)
+            for p in order:
+                z_wait(1, mlp_z_in, p)
+                total = total + mlp_z_in[back_from(p, z)].astype(F32)
+            result[...] = total.astype(BF)
+
+        tile_f32 = pltpu.VMEM((rows, half), F32)
+        pl.run_scoped(
+            attention,
+            tile_f32,
+            tile_f32,
+            pltpu.VMEM((heads, rows, LANES), BF),
+            pltpu.VMEM((contexts, 2 * n_kv, rows, LANES), BF),
+            pltpu.VMEM((rows, half), BF),
             pltpu.VMEM((heads, rows, LANES), BF),
             pltpu.VMEM((heads, rows, LANES), F32),
             pltpu.VMEM((n_kv, seq_len, LANES), F32),
             pltpu.VMEM((n_kv, seq_len, LANES), F32),
+            pltpu.VMEM((contexts, 2 * n_kv, rows, LANES), BF),
+            pltpu.VMEM((lots, 2 * n_kv, rows, LANES), BF),
+        )
+
+        for item in (DOWN, GATE, UP):
+            for s in range(1, planes):
+                p = ring.plane(s)
+                there = strip_dst(item, p)
+                copy_to(there, there, grad_send.at[item, s], grad_recv.at[item, p], ring.at_k).wait_recv()
+                strip_copy(item, s).wait_send()
+            strip_keep(item).wait()
+        for reduction in (down, gate, up):
+            reduction.outer_done()
+        for i in range(max(planes - 2, 0), planes):
+            norm_x(i).wait_send()
+        for p in blocks:
+            mlp_x(p).wait_send()
+        for p in order:
+            norm_z(p).wait_send()
+            mlp_z(p).wait_send()
+
+    hbm = pl.BlockSpec(memory_space=pl.ANY)
+    vmem = pl.BlockSpec(memory_space=pltpu.VMEM)
+    dma = pltpu.SemaphoreType.DMA
+    shape = jax.ShapeDtypeStruct
+    acts = pltpu.VMEM((planes, rows, half), BF)
+    arrivals = pltpu.VMEM((planes - 1, rows, half), BF)
+    return pl.pallas_call(
+        kernel,
+        name="back",
+        out_shape=(
+            shape((rows, half), BF),
+            shape((rows, half), BF),
+            shape((strip, planes * units), BF),
+            shape((strip, planes * units), BF),
+            shape((planes, unit_strip, depth), BF),
+            shape((rows, width), BF),
+            shape((rows, qkv_cols), BF),
+            shape((8, half), F32),
+        ),
+        in_specs=[hbm] * 11 + [vmem] * 7,
+        out_specs=(vmem, vmem, hbm, hbm, hbm, vmem, vmem, vmem),
+        scratch_shapes=[acts, acts, arrivals, arrivals, pltpu.VMEM((2, rows, half), BF), acts, acts, acts]
+        + [
+            pltpu.VMEM((outers, planes, strip, units), BF),
+            pltpu.VMEM((outers, 1, unit_strip, width), BF),
+            pltpu.VMEM((2, lots, planes, strip, units), BF),
+            pltpu.VMEM((lots, 1, unit_strip, width), BF),
+            pltpu.VMEM((2, lots, planes, strip, units), BF),
+            pltpu.VMEM((lots, 1, unit_strip, width), BF),
+            pltpu.VMEM((2, planes, strip, units), BF),
+            pltpu.VMEM((1, unit_strip, width), BF),
+            pltpu.VMEM((outers, 2 * n_kv, rows, LANES), BF),
+            pltpu.VMEM((lots, 2 * n_kv, rows, LANES), BF),
+            pltpu.VMEM((2, rows, LANES), F32),
+            pltpu.VMEM((2, rows, LANES), F32),
+            pltpu.VMEM((rows, half), BF),
+            pltpu.VMEM((rows, half), BF),
+            dma((2 * planes + 4,)),
+            dma((2 * planes + 4,)),
+            dma((2, planes)),
+            dma((2, planes)),
+            dma((4, outers)),
+            dma((4, outers)),
+            dma((4, max(outers, 2))),
+            dma((4, max(outers, 2))),
+            dma((3, planes)),
+            dma((3, planes)),
+            dma((2 * planes + 3,)),
+            pltpu.SemaphoreType.REGULAR,
         ],
-        compiler_params=pltpu.CompilerParams(vmem_limit_bytes=VMEM_LIMIT),
-        cost_estimate=pl.CostEstimate(
-            flops=10 * heads * rows * seq_len * LANES, bytes_accessed=8 * 10**6,
-            transcendentals=heads * rows * seq_len,
+        compiler_params=pltpu.CompilerParams(
+            collective_id=1, has_side_effects=True, vmem_limit_bytes=VMEM_LIMIT
         ),
+        cost_estimate=pl.CostEstimate(flops=50 * 10**9, bytes_accessed=80 * 10**6, transcendentals=8 * 10**6),
+    )
+
+
+def build_grads(planes, contexts, rows, width, query_cols, kv_cols, units):
+    outers = contexts // 2
+    half = width // 2
+    depth = width // planes
+    strip = depth // contexts
+    out_strip = query_cols // contexts
+    unit_strip = units // contexts
+    qkv_cols = query_cols + 2 * kv_cols
+    lots = max(outers - 1, 1)
+    per_half = planes // 2
+    DOWN, GATE, UP, OUT, QKV = range(5)
+
+    def kernel(
+        attn, mid_full, normed_one, qkv_grad, gain_rows, gate_strip, up_strip, down_strip,
+        gate_out, up_out, down_out, out_out, qkv_out, gain_out,
+        out_part, qkv_part, out_core, qkv_core, out_outer_out, qkv_outer_out, out_outer_in, qkv_outer_in,
+        out_sum, qkv_sum, out_z, qkv_z, gain_z, gain_y, gain_k, gain_now,
+        k_send, k_recv, y_send, y_recv, z_send, z_recv, sk_send, sk_recv, sy_send, sy_recv, gain_send, gain_recv,
+        own_sem,
+    ):
+        ring = Ring(planes, contexts)
+        z, c, t, k, o = ring.z, ring.c, ring.t, ring.k, ring.o
+        order = ring.by_distance()
+        ring.greet()
+
+        def slot(item, q):
+            if item == DOWN:
+                return down_out.at[:, q]
+            if item == OUT:
+                return out_out.at[pl.ds(q * out_strip, out_strip), :]
+            whole = {GATE: gate_out, UP: up_out, QKV: qkv_out}[item]
+            return whole.at[pl.ds(q * strip, strip), :]
+
+        def own_strip(item):
+            return {DOWN: down_strip, GATE: gate_strip, UP: up_strip}.get(item, None)
+
+        def source(item):
+            found = own_strip(item)
+            return slot(item, c) if found is None else found
+
+        def y_copy(item, by):
+            return copy_to(
+                source(item), slot(item, c), sy_send.at[item, by], sy_recv.at[item, by], ring.at_o(ring.after(by))
+            )
+
+        def k_copy(item, by):
+            q = ring.before(by) * 2 + k
+            src = source(item) if by == 0 else slot(item, q)
+            return copy_to(src, slot(item, q), sk_send.at[item, by], sk_recv.at[item, by], ring.at_k)
+
+        def share(item):
+            for by in range(1, outers):
+                y_copy(item, by).start()
+            k_copy(item, 0).start()
+
+        def share_on(item):
+            for by in range(1, outers):
+                there = slot(item, ring.before(by) * 2 + k)
+                copy_to(there, there, sy_send.at[item, by], sy_recv.at[item, by], ring.at_k).wait_recv()
+                k_copy(item, by).start()
+
+        def shared(item):
+            for by in range(outers):
+                there = slot(item, ring.before(by) * 2 + 1 - k)
+                copy_to(there, there, sk_send.at[item, by], sk_recv.at[item, by], ring.at_k).wait_recv()
+            for by in range(1, outers):
+                y_copy(item, by).wait_send()
+            for by in range(outers):
+                k_copy(item, by).wait_send()
+
+        keeps = [
+            pltpu.make_async_copy(own_strip(item), slot(item, c), own_sem.at[item]) for item in (DOWN, GATE, UP)
+        ]
+        share(DOWN)
+        for one in keeps:
+            one.start()
+
+        takes_part = z // per_half == t
+
+        def gain_plane(j):
+            return t * per_half + j
+
+        def gain_copy(j):
+            return copy_to(
+                gain_rows.at[:, pl.ds(j * depth, depth)], gain_z.at[z], gain_send.at[j], gain_recv.at[z],
+                ring.at_z(gain_plane(j)),
+            )
+
+        for j in range(per_half):
+
+            @pl.when(gain_plane(j) != z)
+            def _(j=j):
+                gain_copy(j).start()
+
+        gain_x = copy_to(
+            gain_out, gain_out, gain_send.at[per_half], gain_recv.at[planes], ring.at_x
+        )
+
+        def gain_outer(by):
+            return copy_to(
+                gain_now.at[0], gain_y.at[by - 1], gain_send.at[per_half + by], gain_recv.at[planes + by],
+                ring.at_o(ring.after(by)),
+            )
+
+        gain_core = copy_to(
+            gain_now.at[1], gain_k, gain_send.at[per_half + outers], gain_recv.at[planes + outers], ring.at_k
+        )
+
+        def product(part, left, right):
+            @pl.loop(0, left.shape[1] // TILE)
+            def _(i):
+                cols = pl.ds(pl.multiple_of(i * TILE, TILE), TILE)
+                store_part(part, i, t_dot(left[:, cols], right[...]))
+
+        sems = (k_send, k_recv, y_send, y_recv)
+        out = Reduction(ring, 0, out_part, out_core, out_outer_out, out_outer_in, out_sum, sems)
+        qkv = Reduction(ring, 1, qkv_part, qkv_core, qkv_outer_out, qkv_outer_in, qkv_sum, sems)
+        product(out_part, attn, mid_full)
+        out.to_core()
+        product(qkv_part, normed_one, qkv_grad)
+        qkv.to_core()
+        out.from_core()
+
+        @pl.when(takes_part)
+        def _():
+            mine = lax.rem(z, per_half) * depth
+            total = gain_rows[:, pl.ds(pl.multiple_of(mine, depth), depth)]
+            for s in range(1, planes):
+                p = ring.plane(s)
+                copy_to(gain_z.at[p], gain_z.at[p], gain_send.at[0], gain_recv.at[p], ring.at_k).wait_recv()
+                total = total + gain_z[p]
+            gain_now[0] = total
+            for by in range(1, outers):
+                gain_outer(by).start()
+
+        qkv.from_core()
+        share(GATE)
+        share(UP)
+
+        @pl.when(takes_part)
+        def _():
+            total = gain_now[0]
+            for by in range(1, outers):
+                gain_outer(by).wait()
+                total = total + gain_y[by - 1]
+            gain_now[1] = total
+            gain_core.start()
+
+        def piece(item, p):
+            if item == OUT:
+                return out_sum.at[0, :, pl.ds(pl.multiple_of(p * depth, depth), depth)]
+            return qkv_sum.at[p]
+
+        def landing(item, p):
+            return (out_z if item == OUT else qkv_z).at[p]
+
+        def z_copy(item, s):
+            p = ring.plane(s)
+            return copy_to(
+                piece(item, p), landing(item, z), z_send.at[item - OUT, s], z_recv.at[item - OUT, z], ring.at_z(p)
+            )
+
+        def to_planes(item, reduction):
+            reduction.from_outer()
+            for s in range(1, planes):
+                z_copy(item, s).start()
+
+        def from_planes(item):
+            for p in order:
+                there = landing(item, p)
+                copy_to(there, there, z_send.at[item - OUT, 0], z_recv.at[item - OUT, p], ring.at_k).wait_recv()
+            size = out_strip if item == OUT else strip
+            whole = out_out if item == OUT else qkv_out
+            total = piece(item, z)[...].astype(F32)
+            for p in order:
+                total = total + landing(item, p)[...].astype(F32)
+            whole[pl.ds(pl.multiple_of(c * size, size), size), :] = total.astype(BF)
+            share(item)
+
+        to_planes(OUT, out)
+
+        @pl.when(takes_part)
+        def _():
+            gain_core.wait()
+            gain_out[...] = gain_now[1] + gain_k[...]
+            gain_x.start()
+
+        share_on(DOWN)
+        to_planes(QKV, qkv)
+        from_planes(OUT)
+        from_planes(QKV)
+        share_on(GATE)
+        share_on(UP)
+        share_on(OUT)
+        share_on(QKV)
+        for one in keeps:
+            one.wait()
+        for item in range(5):
+            shared(item)
+        for reduction in (out, qkv):
+            reduction.core_done()
+            reduction.outer_done()
+        for item in (OUT, QKV):
+            for s in range(1, planes):
+                z_copy(item, s).wait_send()
+        for j in range(per_half):
+
+            @pl.when(gain_plane(j) != z)
+            def _(j=j):
+                gain_copy(j).wait_send()
+
+        @pl.when(takes_part)
+        def _():
+            gain_x.wait_send()
+
+        @pl.when(jnp.logical_not(takes_part))
+        def _():
+            gain_x.wait_recv()
+
+    hbm = pl.BlockSpec(memory_space=pl.ANY)
+    vmem = pl.BlockSpec(memory_space=pltpu.VMEM)
+    dma = pltpu.SemaphoreType.DMA
+    shape = jax.ShapeDtypeStruct
+    return pl.pallas_call(
+        kernel,
+        name="grads",
+        out_shape=(
+            shape((depth, planes * units), BF),
+            shape((depth, planes * units), BF),
+            shape((planes, contexts, unit_strip, depth), BF),
+            shape((query_cols, depth), BF),
+            shape((depth, qkv_cols), BF),
+            shape((8, depth), F32),
+        ),
+        in_specs=[vmem] * 5 + [hbm] * 3,
+        out_specs=(hbm, hbm, hbm, vmem, vmem, vmem),
+        scratch_shapes=[
+            pltpu.VMEM((1, contexts, out_strip, width), BF),
+            pltpu.VMEM((planes, contexts, strip, qkv_cols), BF),
+            pltpu.VMEM((outers, 1, out_strip, width), BF),
+            pltpu.VMEM((outers, planes, strip, qkv_cols), BF),
+            pltpu.VMEM((lots, 1, out_strip, width), BF),
+            pltpu.VMEM((lots, planes, strip, qkv_cols), BF),
+            pltpu.VMEM((lots, 1, out_strip, width), BF),
+            pltpu.VMEM((lots, planes, strip, qkv_cols), BF),
+            pltpu.VMEM((1, out_strip, width), BF),
+            pltpu.VMEM((planes, strip, qkv_cols), BF),
+            pltpu.VMEM((planes, out_strip, depth), BF),
+            pltpu.VMEM((planes, strip, qkv_cols), BF),
+            pltpu.VMEM((planes, 8, depth), F32),
+            pltpu.VMEM((lots, 8, depth), F32),
+            pltpu.VMEM((8, depth), F32),
+            pltpu.VMEM((2, 8, depth), F32),
+            dma((2, outers)),
+            dma((2, outers)),
+            dma((2, max(outers, 2))),
+            dma((2, max(outers, 2))),
+            dma((2, planes)),
+            dma((2, planes)),
+            dma((5, outers)),
+            dma((5, outers)),
+            dma((5, max(outers, 2))),
+            dma((5, max(outers, 2))),
+            dma((per_half + outers + 1,)),
+            dma((planes + outers + 1,)),
+            dma((3,)),
+        ],
+        compiler_params=pltpu.CompilerParams(
+            collective_id=2, has_side_effects=True, vmem_limit_bytes=VMEM_LIMIT
+        ),
+        cost_estimate=pl.CostEstimate(flops=4 * 10**9, bytes_accessed=40 * 10**6, transcendentals=0),
     )
 
 
@@ -601,75 +1399,22 @@
 ):
     planes = lax.axis_size("fsdp")
     contexts = lax.axis_size("context")
-    z = lax.axis_index("fsdp")
     c = lax.axis_index("context")
-    t = lax.axis_index("tensor")
-    outers = contexts // 2
-    o, k = c // 2, c % 2
-
-    def swap_t(v):
-        return lax.ppermute(v, "tensor", [(0, 1), (1, 0)])
-
-    def swap_k(v):
-        return lax.ppermute(v, "context", [(i, i ^ 1) for i in range(contexts)])
-
-    def shift_o(v, by):
-        return lax.ppermute(
-            v,
-            "context",
-            [(i, ((i // 2 + by) % outers) * 2 + i % 2) for i in range(contexts)],
-        )
-
-    def shift_z(v, by):
-        return lax.ppermute(v, "fsdp", [(i, (i + by) % planes) for i in range(planes)])
-
-    def gather_context(piece):
-        column = [piece] + [shift_o(piece, by) for by in range(1, outers)]
-        other = swap_k(jnp.stack(column))
-        found = []
-        for by in range(outers):
-            home = (o - by + outers) % outers
-            found.append((home * 2 + k, column[by]))
-            found.append((home * 2 + 1 - k, other[by]))
-        return found
-
-    def sum_context(part):
-        shape = part.shape
-        part = part.reshape(shape[0], outers, 2, *shape[2:])
-        got = swap_k(pick(part, 1 - k, 2).astype(BF))
-        total = pick(part, k, 2) + got.astype(F32)
-        sums = pick(total, o, 1)
-        for by in range(1, outers):
-            sums = sums + shift_o(pick(total, (o + by) % outers, 1).astype(BF), by).astype(F32)
-        return sums
-
     tok_own, cot_own = tokens[0], out_grad[0]
     rows, own_cols = tok_own.shape
     width = own_cols * 2
     depth = width // planes
-    strip = depth // contexts
     units = w_gate.shape[1] // planes
-    unit_strip = units // contexts
-
-    def whole_cols(mine, theirs):
-        return jnp.concatenate(
-            [jnp.where(t == 0, mine, theirs), jnp.where(t == 0, theirs, mine)], -1
-        )
-
-    def own_half(v):
-        return lax.dynamic_slice_in_dim(v, t * own_cols, own_cols, v.ndim - 1)
-
-    def other_half(v):
-        return lax.dynamic_slice_in_dim(v, (1 - t) * own_cols, own_cols, v.ndim - 1)
-
     query_cols = w_query.shape[1]
     kv_cols = key_weight.shape[1]
+    sizes = (planes, contexts, rows, width, query_cols, kv_cols, units)
+
     half_rows = rows // 2
     slot = jnp.arange(rows, dtype=jnp.int32)
 
     def positions(index):
-        spans = pick(span_order, index)
-        return spans[slot // half_rows] * half_rows + slot % half_rows
+        spans = lax.dynamic_index_in_dim(span_order, index, 0, keepdims=False)
+        return jnp.where(slot < half_rows, spans[0], spans[1]) * half_rows + slot % half_rows
 
     pos_mine = positions(c)
     pos_q = jnp.broadcast_to(pos_mine[None, :], (8, rows))
@@ -679,165 +1424,36 @@
     cosine_table = jnp.concatenate([cosine] * 4, 1)
     sine_table = jnp.concatenate([-sine, sine] * 2, 1)
 
-    own_in = tok_own.astype(F32)
     qkv_own = jnp.concatenate([w_query, key_weight, value_weight], 1)
     gains_own = jnp.concatenate(
         [attn_gain[None], mlp_gain[None], jnp.zeros((GAIN_ROWS - 2, depth), BF)], 0
     )
-    front = build_front(planes, contexts, rows, width, query_cols, kv_cols, units)
     (
-        gate_w, up_w, down_w, cot_all, norm_all, qkv_w, out_w, gains, q_pad, kv_all, attn_low, log_sum,
-        mid_own, first_normalized, resid_low,
-    ) = front(
-        tok_own, cot_own, gains_own, qkv_own, w_out, w_gate, w_up, w_down, cosine_table, sine_table,
-        pos_q, pos_k,
+        gate_w, up_w, down_w, cot_all, norm_all, qkv_w, out_w, gains, q_pad, kv_all, attn, log_sum, mid_own,
+        normed_one, tok_all, scales,
+    ) = build_front(*sizes)(
+        tok_own, cot_own, gains_own, qkv_own, w_out, w_gate, w_up, w_down, cosine_table, sine_table, pos_q, pos_k
     )
-    gain_one, gain_two = gains[0].astype(F32), gains[1].astype(F32)
-    resid_in = resid_low.astype(F32)
-    scale_one = lax.rsqrt(jnp.mean(resid_in * resid_in, -1, keepdims=True) + EPS)
-
-    def row_total(v):
-        part = jnp.sum(v, -1)
-        return (part + swap_t(part))[:, None]
-
-    gain_one_own, gain_two_own = own_half(gain_one), own_half(gain_two)
-    scale_two = lax.rsqrt(row_total(mid_own * mid_own) / width + EPS)
-    normal_two = mid_own * scale_two
-
-    normed_blocks, cot_blocks, hidden_blocks, unit_grad_blocks = [], [], [], []
-    mlp_sum = None
-    normed_grad = None
-    for by in range(planes):
-        home = (z - by + planes) % planes
-        normed = pick(norm_all, home)
-        cot = pick(cot_all, home)
-        gate_val, up_val = dot(normed, gate_w), dot(normed, up_w)
-        sigmoid_gate = jax.nn.sigmoid(gate_val)
-        hidden = (gate_val * sigmoid_gate * up_val).astype(BF)
-        hidden_grad = dot_t(cot, down_w)
-        gate_grad = hidden_grad * up_val * sigmoid_gate * (1.0 + gate_val * (1.0 - sigmoid_gate))
-        up_grad = hidden_grad * gate_val * sigmoid_gate
-        gate_grad, up_grad = gate_grad.astype(BF), up_grad.astype(BF)
-        unit_grad = jnp.concatenate([gate_grad, up_grad], 1)
-        normed_part = dot_t(gate_grad, gate_w) + dot_t(up_grad, up_w)
-        mlp_part = dot(hidden, down_w)
-        grad_own = own_half(normed_part) + swap_t(other_half(normed_part).astype(BF)).astype(F32)
-        mlp_own = own_half(mlp_part) + swap_t(other_half(mlp_part).astype(BF)).astype(F32)
-        if by == 0:
-            normed_grad, mlp_sum = grad_own, mlp_own
-        else:
-            normed_grad = normed_grad + shift_z(grad_own.astype(BF), planes - by).astype(F32)
-            mlp_sum = mlp_sum + shift_z(mlp_own.astype(BF), planes - by).astype(F32)
-        normed_blocks.append(normed)
-        cot_blocks.append(cot)
-        hidden_blocks.append(hidden)
-        unit_grad_blocks.append(unit_grad)
-    result = (mid_own + mlp_sum).astype(BF)
-
-    normed_all = jnp.concatenate(normed_blocks, 0)
-    hidden_all = jnp.concatenate(hidden_blocks, 0)
-    unit_grad_all = jnp.concatenate(unit_grad_blocks, 0)
-    cot_all = jnp.concatenate(cot_blocks, 0)
-    gate_up_grad = t_dot(normed_all, unit_grad_all)
-    down_grad = t_dot(hidden_all, cot_all)
-
-    gate_up_sum = sum_context(gate_up_grad.reshape(planes, contexts, strip, 2 * units)).astype(BF)
-    gate_strips = jnp.zeros((2, strip, planes * units), BF)
-    for by in range(planes):
-        home = (z - by + planes) % planes
-        block = pick(gate_up_sum, (z + by) % planes)
-        piece = block if by == 0 else shift_z(block, by)
-        piece = jnp.stack([piece[:, :units], piece[:, units:]])
-        gate_strips = place(gate_strips, piece, (0, 0, home * units))
-    gate_out = jnp.zeros((depth, planes * units), F32)
-    up_out = jnp.zeros((depth, planes * units), F32)
-    for index, piece in gather_context(gate_strips):
-        gate_out = place(gate_out, piece[0].astype(F32), (index * strip, 0))
-        up_out = place(up_out, piece[1].astype(F32), (index * strip, 0))
-
-    down_parts = down_grad.reshape(1, contexts, unit_strip, width)
-    down_sum = sum_context(down_parts)[0].astype(BF)
-    down_strips = jnp.zeros((planes, unit_strip, depth), BF)
-    for by in range(planes):
-        home = (z - by + planes) % planes
-        block = lax.dynamic_slice_in_dim(down_sum, ((z + by) % planes) * depth, depth, 1)
-        piece = block if by == 0 else shift_z(block, by)
-        down_strips = place(down_strips, piece[None], (home, 0, 0))
-    down_out = jnp.zeros((planes, contexts, unit_strip, depth), F32)
-    for index, piece in gather_context(down_strips):
-        down_out = place(down_out, piece[:, None].astype(F32), (0, index, 0, 0))
-    down_out = down_out.reshape(planes * units, depth)
-
-    def norm_backward(grad_out, normal, scale_row, gain):
-        scaled = grad_out * gain
-        gain_grad = jnp.sum(grad_out * normal, 0)
-        inner = row_total(scaled * normal) / width
-        return (gain_grad, scale_row * (scaled - normal * inner))
-
-    gain_two_grad, mid_from_norm = norm_backward(normed_grad, normal_two, scale_two, gain_two_own)
-    mid_grad = cot_own.astype(F32) + mid_from_norm
-    mid_grad_own = mid_grad.astype(BF)
-    mid_grad_low = whole_cols(mid_grad_own, swap_t(mid_grad_own))
-
-    out_w_grad = t_dot(attn_low, mid_grad_low)
-    attn_grad = dot_t(mid_grad_low, out_w).astype(BF)
-    query_grad, kv_grad = build_attend_back(contexts, rows, query_cols, kv_cols)(
-        q_pad, kv_all, attn_grad, log_sum, cosine_table, sine_table, pos_q, pos_k
+    result, input_grad, gate_strip, up_strip, down_strip, mid_full, qkv_grad, gain_rows = build_back(*sizes)(
+        gate_w, up_w, down_w, norm_all, cot_all, qkv_w, out_w, q_pad, kv_all, mid_own, tok_all, gains,
+        cosine_table, sine_table, pos_q, pos_k, log_sum, scales,
     )
-    kv_sum = sum_context(kv_grad[None].astype(F32))[0]
-    n_kv = kv_cols // LANES
-    key_grad = apply_rotary(
-        kv_sum[:n_kv].reshape(n_kv, rows, 2, HEAD_WIDTH), cosine[:, None, :], -sine[:, None, :]
+    gate_out, up_out, down_out, out_out, qkv_out, gain_out = build_grads(*sizes)(
+        attn, mid_full, normed_one, qkv_grad, gain_rows, gate_strip, up_strip, down_strip
     )
-    kv_tiles = jnp.concatenate([key_grad.reshape(n_kv, rows, LANES), kv_sum[n_kv:]], 0)
-    qkv_grad = jnp.concatenate(
-        [query_grad, kv_tiles.transpose(1, 0, 2).reshape(rows, 2 * kv_cols).astype(BF)], 1
-    )
-    qkv_w_grad = t_dot(first_normalized, qkv_grad)
-    normed_one_part = dot_t(qkv_grad, qkv_w)
-    normed_one_grad = own_half(normed_one_part) + swap_t(
-        other_half(normed_one_part).astype(BF)
-    ).astype(F32)
-    gain_one_grad, in_from_norm = norm_backward(
-        normed_one_grad, own_in * scale_one, scale_one, gain_one_own
-    )
-    input_result = (mid_grad + in_from_norm).astype(BF)
-
-    def sum_planes(parts):
-        total = pick(parts, z)
-        for by in range(1, planes):
-            total = total + shift_z(pick(parts, (z + by) % planes).astype(BF), by).astype(F32)
-        return total
-
-    out_rows = w_out.shape[0]
-    out_strip_rows = out_rows // contexts
-    out_sum = sum_context(out_w_grad.reshape(1, contexts, out_strip_rows, width))[0]
-    out_sum = sum_planes(out_sum.reshape(out_strip_rows, planes, depth).transpose(1, 0, 2))
-    out_out = jnp.zeros((out_rows, depth), F32)
-    for index, piece in gather_context(out_sum.astype(BF)):
-        out_out = place(out_out, piece.astype(F32), (index * out_strip_rows, 0))
-
-    qkv_sum = sum_context(qkv_w_grad.reshape(planes, contexts, strip, -1))
-    qkv_sum = sum_planes(qkv_sum)
-    qkv_out = jnp.zeros((depth, qkv_own.shape[1]), F32)
-    for index, piece in gather_context(qkv_sum.astype(BF)):
-        qkv_out = place(qkv_out, piece.astype(F32), (index * strip, 0))
-
-    gain_grads = lax.psum(jnp.stack([gain_one_grad, gain_two_grad]), ("fsdp", "context"))
-    gain_all = whole_cols(gain_grads, swap_t(gain_grads))
-    gain_out = lax.dynamic_slice_in_dim(gain_all, z * depth, depth, 1)
+    qkv_out = qkv_out.astype(F32)
     return (
         result[None],
-        input_result[None],
+        input_grad[None],
         gain_out[0],
         qkv_out[:, :query_cols],
         qkv_out[:, query_cols : query_cols + kv_cols],
         qkv_out[:, query_cols + kv_cols :],
-        out_out,
+        out_out.astype(F32),
         gain_out[1],
-        gate_out,
-        up_out,
-        down_out,
+        gate_out.astype(F32),
+        up_out.astype(F32),
+        down_out.reshape(planes * units, depth).astype(F32),
     )
 
 

time: 842 us -> 639 us (0.76)
  Pallas kernels: 262 us -> 596 us
  waiting for transfers between devices: 200 us -> 0 us
  matrix products: 92.2 us -> 0 us
  local copies, waits for them, and re-layouts: 95.8 us -> 14 us
  starting transfers between devices: 62.6 us -> 0 us
  other arithmetic: 77.4 us -> 27.5 us
  blocking collectives: 43.5 us -> 0 us
    pallas_call x2 -> x3, Pallas kernels: 262 us -> 596 us  [the longest x1 241 us: shards(): build_front(*sizes)]
    ppermute x50 -> x0, waiting for transfers between devices: 200 us -> none  [the longest x18 86.4 us: shift_z(): lax.ppermute(v, 'fsdp', [(i, (i + by) % planes) for i in range(planes)])]
    dot_general x30 -> x0, matrix products: 92.2 us -> none  [the longest x4 33.9 us: t_dot(): lax.dot_general(left, right, (((0,), (0,)), ((), ())), preferred_element_...]
    ppermute x50 -> x0, starting transfers between devices: 62.6 us -> none  [the longest x18 40.4 us: shift_z(): lax.ppermute(v, 'fsdp', [(i, (i + by) % planes) for i in range(planes)])]
    psum x1 -> x0, blocking collectives: 43.5 us -> none  [shards(): lax.psum(jnp.stack([gain_one_grad, gain_two_grad]), ('fsdp', 'context'))]
    convert_element_type x24 -> x0, local copies, waits for them, and re-layouts: 33 us -> none  [the longest x3 11.9 us: sum_context(): got = swap_k(pick(part, 1 - k, 2).astype(BF))]
    unnamed x134 -> x14, local copies, waits for them, and re-layouts: 22.5 us -> 1.61 us
    dynamic_slice x8 -> x1, local copies, waits for them, and re-layouts: 17.1 us -> 0.75 us  [positions(): spans = lax.dynamic_index_in_dim(span_order, index, 0, keepdims=False)]
  transfers between devices with their start and end apart: 50 -> 0, of which waited for: 20 -> 0; matrix products, arithmetic and copies ran while one was open for 27% -> 0% of each run, Pallas kernels for 3% -> 0%
where the time goes in v3:
time: 639 us; the launch traced here: 638 us
  Pallas kernels  596 us (93%)
  other arithmetic  27.5 us (4%)
  local copies, waits for them, and re-layouts  14 us (2%)
    pallas_call x1, Pallas kernels, shards(): build_front(*sizes)  241 us
    pallas_call x1, Pallas kernels, shards(): build_back(*sizes)  205 us
    pallas_call x1, Pallas kernels, shards(): build_grads(*sizes)  150 us

profile of v3, /device:TPU:0, one launch (start us, length us, event | category | flops | bytes accessed | tf_op | source)
XLA Modules:
  0.0 638.4 jit_solution(12410339121603306496)
XLA Ops:
  0.6 0.8 constant_dynamic-slice_fusion
  1.4 0.5 fusion.5
  1.9 0.1 pad.17.clone
  2.0 1.3 multiply_add_fusion.4
  3.3 0.7 broadcast_in_dim.58
  4.0 0.7 broadcast_in_dim.59
  4.7 1.6 fusion.4
  6.3 2.6 multiply_add_fusion.2
  8.9 2.6 multiply_add_fusion
  11.5 0.6 broadcast_in_dim.63.pos_q
  12.1 0.7 maximum_maximum_fusion.gains_own
  12.8 0.5 fusion
  13.3 0.8 pad_maximum_fusion.2.sine
  14.1 0.8 pad_maximum_fusion.1.cosine
  15.0 1.0 copy.26.pos_k
  16.0 2.6 pad_maximum_fusion.qkv_own
  18.6 241.1 %front.1 = (bf16[2048,1024]{1,0:T(8,128)(2,1)}, bf16[2048,1024]{1,0:T(8,128)(2,1)}, bf16[1024,2048]{1,0:T(8,128)(2,1)}, bf16[4,256,2048]{2,1,0:T(8,128)(2,1)}, b...) custom-call(bf16[256,1024]{1,0:T(8,128)(2,1)} %bitcast.25, ...), custom_call_target="tpu_custom_call" | custom-call | flops 8000000000 | bytes 80000000 | tf_op jit(solution)/shard_map/front/pallas_call | solution.py:1434
  259.8 204.9 %back.1 = (bf16[256,1024]{1,0:T(8,128)(2,1)}, bf16[256,1024]{1,0:T(8,128)(2,1)}, bf16[128,4096]{1,0:T(8,128)(2,1)}, bf16[128,4096]{1,0:T(8,128)(2,1)}, bf16[4,25...) custom-call(bf16[2048,1024]{1,0:T(8,128)(2,1)} %get-tuple-element.41.gate_hbm, ...), custom_call_target="tpu_custom_call" | custom-call | flops 49999998976 | bytes 80000000 | tf_op jit(solution)/shard_map/back/pallas_call | solution.py:1437
  464.6 150.2 %grads.1 = (bf16[512,4096]{1,0:T(8,128)(2,1)}, bf16[512,4096]{1,0:T(8,128)(2,1)}, bf16[4,4,256,512]{3,2,1,0:T(8,128)(2,1)}, bf16[1024,512]{1,0:T(8,128)(2,1)}, b...) custom-call(bf16[256,1024]{1,0:T(8,128)(2,1)} %get-tuple-element.57.attn, bf16[256,2048]{1,0:T(8,128)(2,1)} %get-tuple-element.58.mid_full, ...), custom_call_target="tpu_custom_call" | custom-call | flops 4000000000 | bytes 40000000 | tf_op jit(solution)/shard_map/grads/pallas_call | solution.py:1441
  614.9 0.0 copy-start.3
  614.9 1.4 fusion.3
  616.3 2.1 fusion.2
  618.4 0.0 copy-start.2
  618.4 2.9 slice.82
  621.3 0.0 copy-done.3
  621.3 1.6 convert_element_type.27
  622.9 0.0 copy-done.2
  622.9 0.0 copy-start.1
  622.9 4.5 convert_element_type.28
  627.4 0.0 copy-done.1
  627.4 0.0 copy-start
  627.4 4.5 convert_element_type.29
  631.9 0.0 copy-done
  631.9 0.0 copy-start.5
  631.9 0.0 copy-start.4
  631.9 4.9 bitcast_convert_fusion
  636.8 0.0 copy-done.5
  636.8 0.8 copy.30
  637.6 0.0 copy-done.4
  637.6 0.8 copy.31
  (3 shorter events, 0.0 us)
Async XLA Ops:
  614.9 6.4 %copy-start.3 = (bf16[1024,512]{1,0:T(8,128)(2,1)S(1)}, bf16[1024,512]{1,0:T(8,128)(2,1)}, u32[]{:S(2)}) copy-start(bf16[1024,512]{1,0:T(8,128)(2,1)} %get-tuple-element.67) | copy-start | bytes 3145732
  618.4 4.6 copy-start.2
  622.9 4.5 copy-start.1
  627.4 4.5 copy-start
  631.9 4.9 copy-start.5
  631.9 5.7 copy-start.4

commit v4 on v3

--- a/solution.py
+++ b/solution.py
@@ -14,7 +14,7 @@
 F32 = jnp.float32
 LANES = 128
 TILE = 256
-GAIN_ROWS = 16
+WIDE = 512
 FACTOR = 1.0 / math.sqrt(HEAD_WIDTH)
 VMEM_LIMIT = 62 * 2**20
 MESH = pl.DeviceIdType.MESH
@@ -55,10 +55,11 @@
     QKV, OUT, GATE, UP, DOWN, COT, NORM, GAIN = range(8)
 
     def kernel(
-        tok, cot, gains_own, qkv_own, out_own, gate_own, up_own, down_own, cosine, sine, pos_q, pos_k,
-        gate_w, up_w, down_w, cot_all, norm_all, qkv_w, out_w, gains, q_pad, kv_all, attn, log_sum,
-        mid_own, normed_one, tok_all, scales,
-        lin, heads_out, send_half, recv_half, norm_own, sq_send, sq_recv,
+        tok, cot, gain_one_own, gain_two_own, query_own, key_own, value_own, out_own, gate_own, up_own, down_own,
+        spans, freqs,
+        gate_w, up_w, down_w, cot_all, norm_all, qkv_hbm, out_hbm, gains, q_pad, kv_all, attn, log_sum,
+        mid_own, normed_one, tok_all, scales, cosine, sine, pos_q, pos_k,
+        qkv_w, out_w, gains_own, lin, heads_out, send_half, recv_half, norm_own, sq_send, sq_recv,
         z_send, z_recv, y_send, y_recv, k_send, k_recv, x_send, x_recv, own_sem,
     ):
         z = lax.axis_index("fsdp")
@@ -190,6 +191,9 @@
         def x_copy(i, src, dst):
             return copy(src, dst, x_send.at[i], x_recv.at[i], at_x)
 
+        gains_own[...] = jnp.zeros_like(gains_own)
+        gains_own[0:1, :] = gain_one_own[...].astype(F32)
+        gains_own[1:2, :] = gain_two_own[...].astype(F32)
         tok_cols = pl.ds(t * half, half)
         tok_copy = x_copy(0, tok, tok_all.at[:, tok_cols])
         tok_copy.start()
@@ -202,11 +206,20 @@
         ]
         for one in gain_copies:
             one.start()
-        qkv_src = qkv_own.at[pl.ds(c * strip, strip), :]
+        home = pl.ds(z * depth, depth)
+        own_qkv = [
+            pltpu.make_async_copy(query_own, qkv_w.at[home, pl.ds(0, query_cols)], own_sem.at[0]),
+            pltpu.make_async_copy(key_own, qkv_w.at[home, pl.ds(query_cols, kv_cols)], own_sem.at[7]),
+            pltpu.make_async_copy(value_own, qkv_w.at[home, pl.ds(query_cols + kv_cols, kv_cols)], own_sem.at[8]),
+        ]
+        for one in own_qkv:
+            one.start()
+        for one in own_qkv:
+            one.wait()
+        qkv_src = slot(QKV, z, c)
         out_src = out_own.at[pl.ds(c * out_strip, out_strip), :]
         spread(QKV, qkv_src)
         own_copies = [
-            pltpu.make_async_copy(qkv_own, qkv_w.at[pl.ds(z * depth, depth), :], own_sem.at[0]),
             pltpu.make_async_copy(out_own, out_w.at[:, pl.ds(z * depth, depth)], own_sem.at[1]),
             pltpu.make_async_copy(
                 gate_own.at[:, pl.ds(z * units, units)], gate_w.at[pl.ds(z * depth, depth), :], own_sem.at[2]
@@ -224,6 +237,18 @@
         gains[:, pl.ds(z * depth, depth)] = gains_own[...]
         tok_all[:, tok_cols] = tok[...]
 
+        def positions(q, shape, axis):
+            r = lax.broadcasted_iota(jnp.int32, shape, axis)
+            return jnp.where(r < rows // 2, spans[q, 0], spans[q, 1]) * (rows // 2) + lax.rem(r, rows // 2)
+
+        for q in range(contexts):
+            pos_k[q * rows : (q + 1) * rows, :] = positions(q, (rows, 1), 0)
+        pos_q[...] = positions(c, (8, rows), 1)
+        angle = positions(c, (rows, LANES), 0).astype(F32) * freqs[...]
+        cosine[...] = jnp.cos(angle)
+        side_of = lax.rem(lax.broadcasted_iota(jnp.int32, (rows, LANES), 1), HEAD_WIDTH) < HEAD_WIDTH // 2
+        sine[...] = jnp.where(side_of, -jnp.sin(angle), jnp.sin(angle))
+
         tok_copy.wait()
         for s in range(1, planes):
             p = lax.rem(z + s, planes)
@@ -241,27 +266,37 @@
 
         spread(OUT, out_src)
         sends = []
-        for s in range(1, planes):
-            goal = lax.rem(z + s, planes)
-            cols = pl.ds(goal * units, units)
-            sends += [
-                z_copy(GATE, z, gate_own.at[pl.ds(c * strip, strip), cols], goal, s - 1),
-                z_copy(UP, z, up_own.at[pl.ds(c * strip, strip), cols], goal, s - 1),
-                z_copy(
-                    DOWN, z, down_own.at[pl.ds(goal * units + c * unit_strip, unit_strip), :], goal, s - 1
-                ),
-            ]
-        for one in sends:
-            one.start()
-        spread(COT, cot)
-        cot_copy = x_copy(1 + z, cot, slot(COT, z, c))
-        cot_copy.start()
-
+
+        def send_units(item):
+            for s in range(1, planes):
+                goal = lax.rem(z + s, planes)
+                if item == DOWN:
+                    src = down_own.at[pl.ds(goal * units + c * unit_strip, unit_strip), :]
+                else:
+                    own = gate_own if item == GATE else up_own
+                    src = own.at[pl.ds(c * strip, strip), pl.ds(goal * units, units)]
+                one = z_copy(item, z, src, goal, s - 1)
+                one.start()
+                sends.append(one)
+
+        def share_units(item):
+            for s in range(1, planes):
+                p = lax.rem(z + planes - s, planes)
+                z_wait(item, p)
+                share(item, p)
+
+        items = (GATE, UP, DOWN)
+        send_units(GATE)
         for p in order:
             share_on(QKV, p)
+            z_wait(OUT, p)
+            forward(OUT, p)
+            share(OUT, p)
+        send_units(UP)
         for p in order:
             shared(QKV, p)
-        own_copies[0].wait()
+        qkv_keep = pltpu.make_async_copy(qkv_w, qkv_hbm, own_sem.at[0])
+        qkv_keep.start()
 
         n_tile = 2 * LANES
 
@@ -316,10 +351,10 @@
             q = lax.rem(o - by + outers, outers) * 2 + 1 - k
             copy(kv_slot(q), kv_slot(q), k_send.at[COT, 0, by], k_recv.at[COT, 0, by], at_k).wait_recv()
 
-        for p in order:
-            z_wait(OUT, p)
-            forward(OUT, p)
-            share(OUT, p)
+        send_units(DOWN)
+        spread(COT, cot)
+        cot_copy = x_copy(1 + z, cot, slot(COT, z, c))
+        cot_copy.start()
 
         def attend(first_head, last_head):
             @pl.loop(first_head, last_head)
@@ -339,10 +374,7 @@
         attend(0, heads // 2)
         for p in order:
             share_on(OUT, p)
-        for p in order:
-            z_wait(COT, p)
-            forward(COT, p)
-            x_copy(1 + p, slot(COT, p, c), slot(COT, p, c)).start()
+        share_units(GATE)
         attend(heads // 2, heads)
 
         for j in range(n_q):
@@ -356,7 +388,9 @@
 
         for p in order:
             shared(OUT, p)
-        own_copies[1].wait()
+        own_copies[0].wait()
+        out_keep = pltpu.make_async_copy(out_w, out_hbm, own_sem.at[7])
+        out_keep.start()
 
         n_out = half // n_tile
 
@@ -376,6 +410,7 @@
             part = jnp.dot(attn[...], out_w[:, cols], preferred_element_type=F32)
             mid_own[:, here] = tok[:, here].astype(F32) + part
 
+        share_units(UP)
         half_copy.wait_recv()
         mid = mid_own[...] + recv_half[...].astype(F32)
         mid_own[...] = mid
@@ -394,16 +429,14 @@
         norm_copy.start()
         norm_keep = pltpu.make_async_copy(norm_own, slot(NORM, z, c), own_sem.at[6])
         norm_keep.start()
-        items = (GATE, UP, DOWN)
-        for s in range(1, planes):
-            p = lax.rem(z + planes - s, planes)
-            for item in items:
-                z_wait(item, p)
-                share(item, p)
+        share_units(DOWN)
         for i, p in enumerate(order):
             z_wait(NORM, p)
             forward(NORM, p)
             x_copy(3 + planes + p, slot(NORM, p, c), slot(NORM, p, c)).start()
+            z_wait(COT, p)
+            forward(COT, p)
+            x_copy(1 + p, slot(COT, p, c), slot(COT, p, c)).start()
             for item in items:
                 share_on(item, lax.rem(z + planes - 1 - i, planes))
 
@@ -415,7 +448,7 @@
             for base, item in ((1, COT), (3 + planes, NORM)):
                 there = (cot_all if item == COT else norm_all).at[p, :, pl.ds((1 - t) * half, half)]
                 copy(there, there, x_send.at[base + p], x_recv.at[base + p], at_x).wait_recv()
-        for one in own_copies[2:]:
+        for one in own_copies[1:] + [qkv_keep, out_keep]:
             one.wait()
         norm_keep.wait()
         tok_copy_out = [half_copy, sq_copy, cot_copy, norm_copy]
@@ -448,7 +481,7 @@
             shape((planes, rows, width), BF),
             shape((width, qkv_cols), BF),
             shape((query_cols, width), BF),
-            shape((GAIN_ROWS, width), BF),
+            shape((8, width), F32),
             shape((heads, rows, LANES), BF),
             shape((contexts, 2 * n_kv, rows, LANES), BF),
             shape((rows, query_cols), BF),
@@ -457,10 +490,17 @@
             shape((rows, width), BF),
             shape((rows, width), BF),
             shape((2, rows, LANES), F32),
+            shape((rows, LANES), F32),
+            shape((rows, LANES), F32),
+            shape((8, rows), jnp.int32),
+            shape((seq_len, 1), jnp.int32),
         ),
-        in_specs=[vmem, hbm, vmem, hbm, hbm, hbm, hbm, hbm, vmem, vmem, vmem, vmem],
-        out_specs=(hbm,) * 5 + (vmem,) * 11,
+        in_specs=[vmem, hbm, vmem, vmem] + [hbm] * 7 + [pl.BlockSpec(memory_space=pltpu.SMEM), vmem],
+        out_specs=(hbm,) * 7 + (vmem,) * 13,
         scratch_shapes=[
+            pltpu.VMEM((width, qkv_cols), BF),
+            pltpu.VMEM((query_cols, width), BF),
+            pltpu.VMEM((8, depth), F32),
             pltpu.VMEM((qkv_cols // LANES, rows, LANES), F32),
             pltpu.VMEM((heads, rows, LANES), F32),
             pltpu.VMEM((rows, half), BF),
@@ -476,7 +516,7 @@
             dma((6, planes, max(outers, 2))),
             dma((3 + 2 * planes,)),
             dma((3 + 2 * planes,)),
-            dma((8,)),
+            dma((9,)),
         ],
         compiler_params=pltpu.CompilerParams(
             collective_id=0, has_side_effects=True, vmem_limit_bytes=VMEM_LIMIT
@@ -600,6 +640,50 @@
     def outer_done(self):
         for by in range(1, self.ring.outers):
             self.outer_copy(by).wait_send()
+
+
+class Share:
+    def __init__(self, ring, item, slot, sems, source=None):
+        self.ring, self.item, self.slot = ring, item, slot
+        self.source = slot(ring.c) if source is None else source
+        self.y_send, self.y_recv, self.k_send, self.k_recv = sems
+
+    def outer_copy(self, by):
+        g = self.ring
+        return copy_to(
+            self.source, self.slot(g.c), self.y_send.at[self.item, by], self.y_recv.at[self.item, by],
+            g.at_o(g.after(by)),
+        )
+
+    def core_copy(self, by):
+        g = self.ring
+        there = self.slot(g.before(by) * 2 + g.k)
+        return copy_to(
+            self.source if by == 0 else there, there, self.k_send.at[self.item, by], self.k_recv.at[self.item, by],
+            g.at_k,
+        )
+
+    def start(self):
+        for by in range(1, self.ring.outers):
+            self.outer_copy(by).start()
+        self.core_copy(0).start()
+
+    def pass_on(self):
+        g = self.ring
+        for by in range(1, g.outers):
+            there = self.slot(g.before(by) * 2 + g.k)
+            copy_to(there, there, self.y_send.at[self.item, by], self.y_recv.at[self.item, by], g.at_k).wait_recv()
+            self.core_copy(by).start()
+
+    def finish(self):
+        g = self.ring
+        for by in range(g.outers):
+            there = self.slot(g.before(by) * 2 + 1 - g.k)
+            copy_to(there, there, self.k_send.at[self.item, by], self.k_recv.at[self.item, by], g.at_k).wait_recv()
+        for by in range(1, g.outers):
+            self.outer_copy(by).wait_send()
+        for by in range(g.outers):
+            self.core_copy(by).wait_send()
 
 
 def rotate_tile(u, cosine, sine, first):
@@ -633,11 +717,12 @@
     def kernel(
         gate_hbm, up_hbm, down_hbm, norm_hbm, cot_hbm, qkv_hbm, out_hbm, q_hbm, kv_hbm, mid_hbm, tok_hbm,
         gains, cosine, sine, pos_q, pos_k, log_sum, scales,
-        result, input_grad, gate_strip, up_strip, down_strip, mid_full, qkv_grad, gain_rows,
-        norm_x_in, mlp_x_in, norm_z_in, mlp_z_in, norm_x_out, mlp_x_out, norm_sum, mlp_sum,
+        input_grad, gate_out, up_strip, down_out, mid_full, qkv_grad, gain_rows, mlp_part,
+        norm_x_in, norm_z_in, norm_x_out, norm_sum, mlp_stage,
         row_core_in, col_core_in, row_outer_in, col_outer_in, row_outer_out, col_outer_out, row_sum, col_sum,
         kv_core_in, kv_outer_in, sq_out, sq_in, first_x_out, first_x_in,
-        x_send, x_recv, z_send, z_recv, k_send, k_recv, y_send, y_recv, grad_send, grad_recv, load_sem, credit,
+        x_send, x_recv, z_send, z_recv, k_send, k_recv, y_send, y_recv, grad_send, grad_recv, sy_send, sy_recv, sk_send,
+        sk_recv, load_sem, stage_sem, credit,
     ):
         ring = Ring(planes, contexts)
         z, c, t, k, o = ring.z, ring.c, ring.t, ring.k, ring.o
@@ -646,18 +731,15 @@
         ring.greet()
         own_cols = pl.multiple_of(t * half, half)
         other_cols = pl.multiple_of((1 - t) * half, half)
-        n_half = half // TILE
+        n_half = half // WIDE
 
         def x_copy(i, src, dst):
             return copy_to(src, dst, x_send.at[i], x_recv.at[i], ring.at_x)
 
-        NORM, MLP, MID, SQ_TWO, FIRST, SQ_ONE = 0, planes, 2 * planes, 2 * planes + 1, 2 * planes + 2, 2 * planes + 3
+        NORM, MID, SQ_TWO, FIRST, SQ_ONE = 0, planes, planes + 1, planes + 2, planes + 3
 
         def norm_x(i):
             return x_copy(NORM + i, norm_x_out.at[i % 2], norm_x_in.at[blocks[i]])
-
-        def mlp_x(p):
-            return x_copy(MLP + p, mlp_x_out.at[p], mlp_x_in.at[p])
 
         def back_from(p, here):
             return lax.rem(p - here + planes, planes) - 1
@@ -667,14 +749,9 @@
                 norm_sum.at[p], norm_z_in.at[back_from(z, p)], z_send.at[0, p], z_recv.at[0, z], ring.at_z(p)
             )
 
-        def mlp_z(p):
-            return copy_to(
-                mlp_sum.at[p], mlp_z_in.at[back_from(z, p)], z_send.at[1, p], z_recv.at[1, z], ring.at_z(p)
-            )
-
-        def z_wait(i, dst, p):
-            there = dst.at[back_from(p, z)]
-            copy_to(there, there, z_send.at[i, p], z_recv.at[i, p], ring.at_k).wait_recv()
+        def norm_z_wait(p):
+            there = norm_z_in.at[back_from(p, z)]
+            copy_to(there, there, z_send.at[0, p], z_recv.at[0, p], ring.at_k).wait_recv()
 
         def add_block(total, other, p):
             n = rows // 64
@@ -687,10 +764,6 @@
         def norm_on(i):
             norm_x(i).wait_recv()
             add_block(norm_sum, norm_x_in, blocks[i])
-
-        def mlp_on(p):
-            mlp_x(p).wait_recv()
-            add_block(mlp_sum, mlp_x_in, p)
 
         sems = (k_send, k_recv, y_send, y_recv)
 
@@ -705,7 +778,16 @@
                 for i, p in enumerate(blocks)
             ]
 
-            def with_weights(gate_w, up_w, down_w):
+            def product(part, left, right):
+                total = planes * rows
+
+                @pl.loop(0, left.shape[2] // TILE)
+                def _(i):
+                    cols = pl.ds(pl.multiple_of(i * TILE, TILE), TILE)
+                    tile = t_dot(left[:, :, cols].reshape(total, TILE), right[...].reshape(total, right.shape[2]))
+                    store_part(part, i, tile)
+
+            def with_weights(gate_w, up_w, down_w, col_part):
                 weights = [
                     load(2 * planes, gate_hbm, gate_w),
                     load(2 * planes + 1, up_hbm, up_w),
@@ -713,7 +795,8 @@
                 ]
                 for one in weights:
                     one.wait()
-                for i, p in enumerate(blocks):
+                def forward_block(i):
+                    p = blocks[i]
                     loads[i][0].wait()
                     loads[i][1].wait()
 
@@ -729,66 +812,76 @@
                         gate_grad[p, :, cols] = (grad * up * sig * (1.0 + gate * (1.0 - sig))).astype(BF)
                         up_grad[p, :, cols] = (grad * act).astype(BF)
 
-                    def norm_tile(at):
-                        r = pl.ds(pl.multiple_of(at, TILE), TILE)
+                def norm_block(i):
+                    p = blocks[i]
+
+                    def tile_of(at):
+                        r = pl.ds(pl.multiple_of(at, WIDE), WIDE)
                         return dot_t(gate_grad[p], gate_w[r, :]) + dot_t(up_grad[p], up_w[r, :])
-
-                    def mlp_tile(at):
-                        r = pl.ds(pl.multiple_of(at, TILE), TILE)
-                        return jnp.dot(hid[p], down_w[:, r], preferred_element_type=F32)
-
-                    def halves(tile_of, out, total, start):
-                        @pl.loop(0, n_half)
-                        def _(j):
-                            here = pl.ds(pl.multiple_of(j * TILE, TILE), TILE)
-                            out[:, here] = tile_of(other_cols + j * TILE).astype(BF)
-
-                        start()
-
-                        @pl.loop(0, n_half)
-                        def _(j):
-                            here = pl.ds(pl.multiple_of(j * TILE, TILE), TILE)
-                            total[p, :, here] = tile_of(own_cols + j * TILE).astype(BF)
 
                     if i > 1:
                         norm_x(i - 2).wait_send()
-                    halves(norm_tile, norm_x_out.at[i % 2], norm_sum, lambda: norm_x(i).start())
+
+                    @pl.loop(0, n_half)
+                    def _(j):
+                        here = pl.ds(pl.multiple_of(j * WIDE, WIDE), WIDE)
+                        norm_x_out[i % 2, :, here] = tile_of(other_cols + j * WIDE).astype(BF)
+
+                    norm_x(i).start()
+
+                    @pl.loop(0, n_half)
+                    def _(j):
+                        here = pl.ds(pl.multiple_of(j * WIDE, WIDE), WIDE)
+                        norm_sum[p, :, here] = tile_of(own_cols + j * WIDE).astype(BF)
+
                     if i > 0:
                         norm_on(i - 1)
                         norm_z(blocks[i - 1]).start()
-                    halves(mlp_tile, mlp_x_out.at[p], mlp_sum, lambda: None)
+
+                down = Reduction(
+                    ring, DOWN, col_part, col_core_in, col_outer_out, col_outer_in, col_sum, sems
+                )
+                for i in range(planes):
+                    forward_block(i)
+                    norm_block(i)
+                product(col_part, hid, cot)
+                down.to_core()
+
+                def stage_copy(i):
+                    return pltpu.make_async_copy(mlp_stage.at[i % 2], mlp_part.at[blocks[i]], stage_sem.at[i % 2])
+
+                for i, p in enumerate(blocks):
+                    if i > 1:
+                        stage_copy(i - 2).wait()
+
+                    @pl.loop(0, width // WIDE)
+                    def _(j):
+                        r = pl.ds(pl.multiple_of(j * WIDE, WIDE), WIDE)
+                        mlp_stage[i % 2, :, r] = jnp.dot(hid[p], down_w[:, r], preferred_element_type=F32).astype(BF)
+
+                    stage_copy(i).start()
+                    if i == 0:
+                        down.from_core()
+                for i in range(max(planes - 2, 0), planes):
+                    stage_copy(i).wait()
+                down.core_done()
 
             pl.run_scoped(
                 with_weights,
                 pltpu.VMEM((width, units), BF), pltpu.VMEM((width, units), BF), pltpu.VMEM((units, width), BF),
+                pltpu.VMEM((1, contexts, unit_strip, width), BF),
             )
 
-            def with_parts(row_part, col_part):
-                down = Reduction(
-                    ring, DOWN, col_part, col_core_in, col_outer_out, col_outer_in, col_sum, sems
-                )
+            def with_parts(row_part):
                 gate = Reduction(
                     ring, GATE, row_part, row_core_in, row_outer_out.at[0], row_outer_in.at[0], row_sum.at[0], sems
                 )
                 up = Reduction(
                     ring, UP, row_part, row_core_in, row_outer_out.at[1], row_outer_in.at[1], row_sum.at[1], sems
                 )
-
-                def product(part, left, right):
-                    total = planes * rows
-
-                    @pl.loop(0, left.shape[2] // TILE)
-                    def _(i):
-                        cols = pl.ds(pl.multiple_of(i * TILE, TILE), TILE)
-                        tile = t_dot(left[:, :, cols].reshape(total, TILE), right[...].reshape(total, right.shape[2]))
-                        store_part(part, i, tile)
-
-                product(col_part, hid, cot)
-                down.to_core()
-                norm_on(planes - 1)
                 product(row_part, norm, gate_grad)
                 gate.to_core()
-                down.from_core()
+                norm_on(planes - 1)
                 gate.from_core()
                 gate.core_done()
                 pl.semaphore_signal(credit, inc=1, device_id=ring.at_k, device_id_type=MESH)
@@ -797,12 +890,8 @@
                 up.to_core()
                 up.from_core()
                 up.core_done()
-                down.core_done()
-
-            pl.run_scoped(
-                with_parts,
-                pltpu.VMEM((planes, contexts, strip, units), BF), pltpu.VMEM((1, contexts, unit_strip, width), BF),
-            )
+
+            pl.run_scoped(with_parts, pltpu.VMEM((planes, contexts, strip, units), BF))
 
         block_bf = pltpu.VMEM((planes, rows, width), BF)
         unit_bf = pltpu.VMEM((planes, rows, units), BF)
@@ -819,8 +908,11 @@
 
         def strip_dst(item, home):
             if item == DOWN:
-                return down_strip.at[home]
-            return (gate_strip if item == GATE else up_strip).at[:, pl.ds(pl.multiple_of(home * units, units), units)]
+                return down_out.at[home, c]
+            cols = pl.ds(pl.multiple_of(home * units, units), units)
+            if item == GATE:
+                return gate_out.at[pl.ds(pl.multiple_of(c * strip, strip), strip), cols]
+            return up_strip.at[:, cols]
 
         def strip_copy(item, s):
             goal = ring.plane(s)
@@ -837,9 +929,20 @@
                 strip_copy(item, s).start()
             strip_keep(item).start()
 
-        def attention(mid, mid_grad, q_pad, kv_all, tok, grad_pad, query_out, key_sum, value_sum, kv_grad, kv_out):
+        def from_planes(item):
+            for s in range(1, planes):
+                p = ring.plane(s)
+                there = strip_dst(item, p)
+                copy_to(there, there, grad_send.at[item, s], grad_recv.at[item, p], ring.at_k).wait_recv()
+            strip_keep(item).wait()
+
+        share_sems = (sy_send, sy_recv, sk_send, sk_recv)
+        down_share = Share(ring, 0, lambda q: down_out.at[:, q], share_sems)
+        gate_share = Share(ring, 1, lambda q: gate_out.at[pl.ds(pl.multiple_of(q * strip, strip), strip), :], share_sems)
+
+        def attention(mid_grad, q_pad, kv_all, tok, grad_pad, query_out, key_sum, value_sum, kv_grad, kv_out):
             loads = [
-                pltpu.make_async_copy(mid_hbm, mid, load_sem.at[0]),
+                pltpu.make_async_copy(mid_hbm, mid_grad, load_sem.at[0]),
                 pltpu.make_async_copy(tok_hbm.at[:, pl.ds(own_cols, half)], tok, load_sem.at[1]),
                 pltpu.make_async_copy(q_hbm, q_pad, load_sem.at[2]),
                 pltpu.make_async_copy(kv_hbm, kv_all, load_sem.at[3]),
@@ -865,20 +968,18 @@
                 return scale * (scaled - normal * inner)
 
             for p in order:
-                z_wait(0, norm_z_in, p)
+                norm_z_wait(p)
             grad = norm_sum[z].astype(F32)
             for p in order:
                 grad = grad + norm_z_in[back_from(p, z)].astype(F32)
             scale_two = scales[1][:, 0:1]
             gain_two = gains[1:2, pl.ds(own_cols, half)].astype(F32)
-            back = norm_back(grad, mid[...] * scale_two, scale_two, gain_two, 1, 0)
+            back = norm_back(grad, mid_grad[...] * scale_two, scale_two, gain_two, 1, 0)
             mid_grad[...] = first_x_out[...].astype(F32) + back
             mine = mid_full.at[:, pl.ds(own_cols, half)]
             mid_full[:, pl.ds(own_cols, half)] = mid_grad[...].astype(BF)
             mid_swap = x_copy(MID, mine, mine)
             mid_swap.start()
-            for p in blocks:
-                mlp_x(p).start()
             to_planes(DOWN, down)
             mid_swap.wait_recv()
 
@@ -924,8 +1025,9 @@
                     query_out[h] = t_dot(keys, score_grad).T
 
             attend_back(0, heads // 2)
-            mlp_on(blocks[0])
-            mlp_z(blocks[0]).start()
+            to_planes(GATE, gate)
+            from_planes(DOWN)
+            down_share.start()
             attend_back(heads // 2, heads)
             for i in range(n_kv):
                 kv_grad[:, i] = key_sum[i].astype(BF).reshape(contexts, rows, LANES)
@@ -945,7 +1047,6 @@
 
             for other in range(outers):
                 kv_core(other).start()
-            to_planes(GATE, gate)
             for j in range(n_q):
                 side = (2 * j) // group % 2
                 lo, hi = query_out[2 * j], query_out[2 * j + 1]
@@ -955,6 +1056,7 @@
                     lo = pltpu.roll(lo, HEAD_WIDTH, 1)
                 u = jnp.where(low, lo, hi) * FACTOR
                 qkv_grad[:, j * LANES : (j + 1) * LANES] = rotate_tile(u, cosine[...], -sine[...], first).astype(BF)
+            to_planes(UP, up)
             for other in range(outers):
                 kv_core(other).wait_recv()
             for by in range(1, outers):
@@ -984,24 +1086,22 @@
                 one.wait()
 
                 def tile_of(at):
-                    return dot_t(qkv_grad[...], qkv_w[pl.ds(pl.multiple_of(at, TILE), TILE), :])
+                    return dot_t(qkv_grad[...], qkv_w[pl.ds(pl.multiple_of(at, WIDE), WIDE), :])
 
                 @pl.loop(0, n_half)
                 def _(j):
-                    here = pl.ds(pl.multiple_of(j * TILE, TILE), TILE)
-                    first_x_out[:, here] = tile_of(other_cols + j * TILE).astype(BF)
+                    here = pl.ds(pl.multiple_of(j * WIDE, WIDE), WIDE)
+                    first_x_out[:, here] = tile_of(other_cols + j * WIDE).astype(BF)
 
                 first_swap.start()
 
                 @pl.loop(0, n_half)
                 def _(j):
-                    here = pl.ds(pl.multiple_of(j * TILE, TILE), TILE)
-                    own[:, here] = tile_of(own_cols + j * TILE)
-
-                for p in blocks[1:]:
-                    mlp_on(p)
-                    if p is not z:
-                        mlp_z(p).start()
+                    here = pl.ds(pl.multiple_of(j * WIDE, WIDE), WIDE)
+                    own[:, here] = tile_of(own_cols + j * WIDE)
+
+                from_planes(GATE)
+                gate_share.start()
                 first_swap.wait()
                 scale_one = scales[0][:, 0:1]
                 gain_one = gains[0:1, pl.ds(own_cols, half)].astype(F32)
@@ -1011,18 +1111,11 @@
                 input_grad[...] = (mid_grad[...] + back).astype(BF)
 
             pl.run_scoped(with_qkv, pltpu.VMEM((width, qkv_cols), BF), pltpu.VMEM((rows, half), F32))
-            to_planes(UP, up)
             mid_swap.wait_send()
-            total = mid[...] + mlp_sum[z].astype(F32)
-            for p in order:
-                z_wait(1, mlp_z_in, p)
-                total = total + mlp_z_in[back_from(p, z)].astype(F32)
-            result[...] = total.astype(BF)
 
         tile_f32 = pltpu.VMEM((rows, half), F32)
         pl.run_scoped(
             attention,
-            tile_f32,
             tile_f32,
             pltpu.VMEM((heads, rows, LANES), BF),
             pltpu.VMEM((contexts, 2 * n_kv, rows, LANES), BF),
@@ -1035,22 +1128,20 @@
             pltpu.VMEM((lots, 2 * n_kv, rows, LANES), BF),
         )
 
+        down_share.pass_on()
+        gate_share.pass_on()
+        from_planes(UP)
+        down_share.finish()
+        gate_share.finish()
         for item in (DOWN, GATE, UP):
             for s in range(1, planes):
-                p = ring.plane(s)
-                there = strip_dst(item, p)
-                copy_to(there, there, grad_send.at[item, s], grad_recv.at[item, p], ring.at_k).wait_recv()
                 strip_copy(item, s).wait_send()
-            strip_keep(item).wait()
         for reduction in (down, gate, up):
             reduction.outer_done()
         for i in range(max(planes - 2, 0), planes):
             norm_x(i).wait_send()
-        for p in blocks:
-            mlp_x(p).wait_send()
         for p in order:
             norm_z(p).wait_send()
-            mlp_z(p).wait_send()
 
     hbm = pl.BlockSpec(memory_space=pl.ANY)
     vmem = pl.BlockSpec(memory_space=pltpu.VMEM)
@@ -1063,17 +1154,17 @@
         name="back",
         out_shape=(
             shape((rows, half), BF),
-            shape((rows, half), BF),
+            shape((depth, planes * units), BF),
             shape((strip, planes * units), BF),
-            shape((strip, planes * units), BF),
-            shape((planes, unit_strip, depth), BF),
+            shape((planes, contexts, unit_strip, depth), BF),
             shape((rows, width), BF),
             shape((rows, qkv_cols), BF),
             shape((8, half), F32),
+            shape((planes, rows, width), BF),
         ),
         in_specs=[hbm] * 11 + [vmem] * 7,
-        out_specs=(vmem, vmem, hbm, hbm, hbm, vmem, vmem, vmem),
-        scratch_shapes=[acts, acts, arrivals, arrivals, pltpu.VMEM((2, rows, half), BF), acts, acts, acts]
+        out_specs=(vmem, hbm, hbm, hbm, vmem, vmem, vmem, hbm),
+        scratch_shapes=[acts, arrivals, pltpu.VMEM((2, rows, half), BF), acts, pltpu.VMEM((2, rows, width), BF)]
         + [
             pltpu.VMEM((outers, planes, strip, units), BF),
             pltpu.VMEM((outers, 1, unit_strip, width), BF),
@@ -1089,17 +1180,22 @@
             pltpu.VMEM((2, rows, LANES), F32),
             pltpu.VMEM((rows, half), BF),
             pltpu.VMEM((rows, half), BF),
-            dma((2 * planes + 4,)),
-            dma((2 * planes + 4,)),
-            dma((2, planes)),
-            dma((2, planes)),
+            dma((planes + 4,)),
+            dma((planes + 4,)),
+            dma((1, planes)),
+            dma((1, planes)),
             dma((4, outers)),
             dma((4, outers)),
             dma((4, max(outers, 2))),
             dma((4, max(outers, 2))),
             dma((3, planes)),
             dma((3, planes)),
+            dma((2, max(outers, 2))),
+            dma((2, max(outers, 2))),
+            dma((2, outers)),
+            dma((2, outers)),
             dma((2 * planes + 3,)),
+            dma((2,)),
             pltpu.SemaphoreType.REGULAR,
         ],
         compiler_params=pltpu.CompilerParams(
@@ -1119,72 +1215,58 @@
     qkv_cols = query_cols + 2 * kv_cols
     lots = max(outers - 1, 1)
     per_half = planes // 2
-    DOWN, GATE, UP, OUT, QKV = range(5)
+    OUT, QKV, UP = range(3)
 
     def kernel(
-        attn, mid_full, normed_one, qkv_grad, gain_rows, gate_strip, up_strip, down_strip,
-        gate_out, up_out, down_out, out_out, qkv_out, gain_out,
+        attn, mid_full, normed_one, qkv_grad, gain_rows, mid_own, up_strip, mlp_part,
+        up_out, out_out, qkv_out, gain_out, result,
         out_part, qkv_part, out_core, qkv_core, out_outer_out, qkv_outer_out, out_outer_in, qkv_outer_in,
-        out_sum, qkv_sum, out_z, qkv_z, gain_z, gain_y, gain_k, gain_now,
+        out_sum, qkv_sum, out_z, qkv_z, gain_z, gain_y, gain_k, gain_now, mlp_x_in, mlp_z_in, mlp_sum,
         k_send, k_recv, y_send, y_recv, z_send, z_recv, sk_send, sk_recv, sy_send, sy_recv, gain_send, gain_recv,
-        own_sem,
+        mx_send, mx_recv, mz_send, mz_recv, own_sem,
     ):
         ring = Ring(planes, contexts)
         z, c, t, k, o = ring.z, ring.c, ring.t, ring.k, ring.o
         order = ring.by_distance()
         ring.greet()
 
-        def slot(item, q):
-            if item == DOWN:
-                return down_out.at[:, q]
-            if item == OUT:
-                return out_out.at[pl.ds(q * out_strip, out_strip), :]
-            whole = {GATE: gate_out, UP: up_out, QKV: qkv_out}[item]
-            return whole.at[pl.ds(q * strip, strip), :]
-
-        def own_strip(item):
-            return {DOWN: down_strip, GATE: gate_strip, UP: up_strip}.get(item, None)
-
-        def source(item):
-            found = own_strip(item)
-            return slot(item, c) if found is None else found
-
-        def y_copy(item, by):
+        def rows_of(whole, size):
+            return lambda q: whole.at[pl.ds(pl.multiple_of(q * size, size), size), :]
+
+        share_sems = (sy_send, sy_recv, sk_send, sk_recv)
+        up_share = Share(ring, UP, rows_of(up_out, strip), share_sems, up_strip)
+        out_share = Share(ring, OUT, rows_of(out_out, out_strip), share_sems)
+        qkv_share = Share(ring, QKV, rows_of(qkv_out, strip), share_sems)
+        keep = pltpu.make_async_copy(up_strip, rows_of(up_out, strip)(c), own_sem.at[0])
+        keep.start()
+
+        own_cols = pl.multiple_of(t * half, half)
+        other_cols = pl.multiple_of((1 - t) * half, half)
+        blocks = order[::-1] + [z]
+
+        def mlp_x(p):
             return copy_to(
-                source(item), slot(item, c), sy_send.at[item, by], sy_recv.at[item, by], ring.at_o(ring.after(by))
+                mlp_part.at[p, :, pl.ds(other_cols, half)], mlp_x_in.at[p], mx_send.at[p], mx_recv.at[p], ring.at_x
             )
 
-        def k_copy(item, by):
-            q = ring.before(by) * 2 + k
-            src = source(item) if by == 0 else slot(item, q)
-            return copy_to(src, slot(item, q), sk_send.at[item, by], sk_recv.at[item, by], ring.at_k)
-
-        def share(item):
-            for by in range(1, outers):
-                y_copy(item, by).start()
-            k_copy(item, 0).start()
-
-        def share_on(item):
-            for by in range(1, outers):
-                there = slot(item, ring.before(by) * 2 + k)
-                copy_to(there, there, sy_send.at[item, by], sy_recv.at[item, by], ring.at_k).wait_recv()
-                k_copy(item, by).start()
-
-        def shared(item):
-            for by in range(outers):
-                there = slot(item, ring.before(by) * 2 + 1 - k)
-                copy_to(there, there, sk_send.at[item, by], sk_recv.at[item, by], ring.at_k).wait_recv()
-            for by in range(1, outers):
-                y_copy(item, by).wait_send()
-            for by in range(outers):
-                k_copy(item, by).wait_send()
-
-        keeps = [
-            pltpu.make_async_copy(own_strip(item), slot(item, c), own_sem.at[item]) for item in (DOWN, GATE, UP)
-        ]
-        share(DOWN)
-        for one in keeps:
-            one.start()
+        def mlp_z(p):
+            return copy_to(
+                mlp_sum.at[p], mlp_z_in.at[lax.rem(z - p + planes, planes) - 1], mz_send.at[p], mz_recv.at[z],
+                ring.at_z(p),
+            )
+
+        mlp_load = pltpu.make_async_copy(mlp_part.at[:, :, pl.ds(own_cols, half)], mlp_sum, own_sem.at[1])
+        for p in blocks:
+            mlp_x(p).start()
+        mlp_load.start()
+
+        def mlp_on(p):
+            mlp_x(p).wait_recv()
+
+            @pl.loop(0, rows // 64)
+            def _(i):
+                r = pl.ds(pl.multiple_of(i * 64, 64), 64)
+                mlp_sum[p, r, :] = (mlp_sum[p, r, :].astype(F32) + mlp_x_in[p, r, :].astype(F32)).astype(BF)
 
         takes_part = z // per_half == t
 
@@ -1226,11 +1308,11 @@
         sems = (k_send, k_recv, y_send, y_recv)
         out = Reduction(ring, 0, out_part, out_core, out_outer_out, out_outer_in, out_sum, sems)
         qkv = Reduction(ring, 1, qkv_part, qkv_core, qkv_outer_out, qkv_outer_in, qkv_sum, sems)
-        product(out_part, attn, mid_full)
-        out.to_core()
         product(qkv_part, normed_one, qkv_grad)
         qkv.to_core()
-        out.from_core()
+        product(out_part, attn, mid_full)
+        qkv.from_core()
+        out.to_core()
 
         @pl.when(takes_part)
         def _():
@@ -1244,9 +1326,11 @@
             for by in range(1, outers):
                 gain_outer(by).start()
 
-        qkv.from_core()
-        share(GATE)
-        share(UP)
+        out.from_core()
+        mlp_load.wait()
+        for p in blocks[:-1]:
+            mlp_on(p)
+            mlp_z(p).start()
 
         @pl.when(takes_part)
         def _():
@@ -1268,7 +1352,7 @@
         def z_copy(item, s):
             p = ring.plane(s)
             return copy_to(
-                piece(item, p), landing(item, z), z_send.at[item - OUT, s], z_recv.at[item - OUT, z], ring.at_z(p)
+                piece(item, p), landing(item, z), z_send.at[item, s], z_recv.at[item, z], ring.at_z(p)
             )
 
         def to_planes(item, reduction):
@@ -1279,16 +1363,16 @@
         def from_planes(item):
             for p in order:
                 there = landing(item, p)
-                copy_to(there, there, z_send.at[item - OUT, 0], z_recv.at[item - OUT, p], ring.at_k).wait_recv()
+                copy_to(there, there, z_send.at[item, 0], z_recv.at[item, p], ring.at_k).wait_recv()
             size = out_strip if item == OUT else strip
             whole = out_out if item == OUT else qkv_out
             total = piece(item, z)[...].astype(F32)
             for p in order:
                 total = total + landing(item, p)[...].astype(F32)
             whole[pl.ds(pl.multiple_of(c * size, size), size), :] = total.astype(BF)
-            share(item)
-
-        to_planes(OUT, out)
+            (out_share if item == OUT else qkv_share).start()
+
+        to_planes(QKV, qkv)
 
         @pl.when(takes_part)
         def _():
@@ -1296,18 +1380,26 @@
             gain_out[...] = gain_now[1] + gain_k[...]
             gain_x.start()
 
-        share_on(DOWN)
-        to_planes(QKV, qkv)
+        to_planes(OUT, out)
+        up_share.start()
+        from_planes(QKV)
+        mlp_on(z)
         from_planes(OUT)
-        from_planes(QKV)
-        share_on(GATE)
-        share_on(UP)
-        share_on(OUT)
-        share_on(QKV)
-        for one in keeps:
-            one.wait()
-        for item in range(5):
-            shared(item)
+        total = mid_own[...] + mlp_sum[z].astype(F32)
+        for p in order:
+            there = mlp_z_in.at[lax.rem(p - z + planes, planes) - 1]
+            copy_to(there, there, mz_send.at[p], mz_recv.at[p], ring.at_k).wait_recv()
+            total = total + there[...].astype(F32)
+        result[...] = total.astype(BF)
+        for one in (up_share, out_share, qkv_share):
+            one.pass_on()
+        keep.wait()
+        for one in (up_share, out_share, qkv_share):
+            one.finish()
+        for p in blocks:
+            mlp_x(p).wait_send()
+        for p in order:
+            mlp_z(p).wait_send()
         for reduction in (out, qkv):
             reduction.core_done()
             reduction.outer_done()
@@ -1337,14 +1429,13 @@
         name="grads",
         out_shape=(
             shape((depth, planes * units), BF),
-            shape((depth, planes * units), BF),
-            shape((planes, contexts, unit_strip, depth), BF),
             shape((query_cols, depth), BF),
             shape((depth, qkv_cols), BF),
             shape((8, depth), F32),
+            shape((rows, half), BF),
         ),
-        in_specs=[vmem] * 5 + [hbm] * 3,
-        out_specs=(hbm, hbm, hbm, vmem, vmem, vmem),
+        in_specs=[vmem] * 6 + [hbm] * 2,
+        out_specs=(hbm, vmem, vmem, vmem, vmem),
         scratch_shapes=[
             pltpu.VMEM((1, contexts, out_strip, width), BF),
             pltpu.VMEM((planes, contexts, strip, qkv_cols), BF),
@@ -1362,19 +1453,26 @@
             pltpu.VMEM((lots, 8, depth), F32),
             pltpu.VMEM((8, depth), F32),
             pltpu.VMEM((2, 8, depth), F32),
+            pltpu.VMEM((planes, rows, half), BF),
+            pltpu.VMEM((planes - 1, rows, half), BF),
+            pltpu.VMEM((planes, rows, half), BF),
             dma((2, outers)),
             dma((2, outers)),
             dma((2, max(outers, 2))),
             dma((2, max(outers, 2))),
             dma((2, planes)),
             dma((2, planes)),
-            dma((5, outers)),
-            dma((5, outers)),
-            dma((5, max(outers, 2))),
-            dma((5, max(outers, 2))),
+            dma((3, outers)),
+            dma((3, outers)),
+            dma((3, max(outers, 2))),
+            dma((3, max(outers, 2))),
             dma((per_half + outers + 1,)),
             dma((planes + outers + 1,)),
-            dma((3,)),
+            dma((planes,)),
+            dma((planes,)),
+            dma((planes,)),
+            dma((planes,)),
+            dma((2,)),
         ],
         compiler_params=pltpu.CompilerParams(
             collective_id=2, has_side_effects=True, vmem_limit_bytes=VMEM_LIMIT
@@ -1399,7 +1497,6 @@
 ):
     planes = lax.axis_size("fsdp")
     contexts = lax.axis_size("context")
-    c = lax.axis_index("context")
     tok_own, cot_own = tokens[0], out_grad[0]
     rows, own_cols = tok_own.shape
     width = own_cols * 2
@@ -1409,37 +1506,20 @@
     kv_cols = key_weight.shape[1]
     sizes = (planes, contexts, rows, width, query_cols, kv_cols, units)
 
-    half_rows = rows // 2
-    slot = jnp.arange(rows, dtype=jnp.int32)
-
-    def positions(index):
-        spans = lax.dynamic_index_in_dim(span_order, index, 0, keepdims=False)
-        return jnp.where(slot < half_rows, spans[0], spans[1]) * half_rows + slot % half_rows
-
-    pos_mine = positions(c)
-    pos_q = jnp.broadcast_to(pos_mine[None, :], (8, rows))
-    pos_k = jnp.concatenate([positions(i) for i in range(contexts)])[:, None]
-    angles = pos_mine.astype(F32)[:, None] * rope_freqs(HEAD_WIDTH)[None, :]
-    cosine, sine = jnp.cos(angles), jnp.sin(angles)
-    cosine_table = jnp.concatenate([cosine] * 4, 1)
-    sine_table = jnp.concatenate([-sine, sine] * 2, 1)
-
-    qkv_own = jnp.concatenate([w_query, key_weight, value_weight], 1)
-    gains_own = jnp.concatenate(
-        [attn_gain[None], mlp_gain[None], jnp.zeros((GAIN_ROWS - 2, depth), BF)], 0
-    )
+    freqs = jnp.tile(rope_freqs(HEAD_WIDTH), LANES // (HEAD_WIDTH // 2))[None]
     (
         gate_w, up_w, down_w, cot_all, norm_all, qkv_w, out_w, gains, q_pad, kv_all, attn, log_sum, mid_own,
-        normed_one, tok_all, scales,
+        normed_one, tok_all, scales, cosine_table, sine_table, pos_q, pos_k,
     ) = build_front(*sizes)(
-        tok_own, cot_own, gains_own, qkv_own, w_out, w_gate, w_up, w_down, cosine_table, sine_table, pos_q, pos_k
+        tok_own, cot_own, attn_gain[None], mlp_gain[None], w_query, key_weight, value_weight, w_out, w_gate, w_up,
+        w_down, span_order, freqs,
     )
-    result, input_grad, gate_strip, up_strip, down_strip, mid_full, qkv_grad, gain_rows = build_back(*sizes)(
+    input_grad, gate_out, up_strip, down_out, mid_full, qkv_grad, gain_rows, mlp_part = build_back(*sizes)(
         gate_w, up_w, down_w, norm_all, cot_all, qkv_w, out_w, q_pad, kv_all, mid_own, tok_all, gains,
         cosine_table, sine_table, pos_q, pos_k, log_sum, scales,
     )
-    gate_out, up_out, down_out, out_out, qkv_out, gain_out = build_grads(*sizes)(
-        attn, mid_full, normed_one, qkv_grad, gain_rows, gate_strip, up_strip, down_strip
+    up_out, out_out, qkv_out, gain_out, result = build_grads(*sizes)(
+        attn, mid_full, normed_one, qkv_grad, gain_rows, mid_own, up_strip, mlp_part
     )
     qkv_out = qkv_out.astype(F32)
     return (

time: 639 us -> 570 us (0.89)
  Pallas kernels: 596 us -> 538 us
  other arithmetic: 27.5 us -> 15.5 us
    pallas_call x1, Pallas kernels: 241 us -> 216 us  [shards(): build_front(*sizes)]
    pallas_call x1, Pallas kernels: 150 us -> 127 us  [shards(): build_grads(*sizes)]
    pallas_call x1, Pallas kernels: 205 us -> 195 us  [shards(): build_back(*sizes)]
    add x3 -> x0, other arithmetic: 6.48 us -> none  [positions(): jnp.where(slot < half_rows, spans[0], spans[1]) * half_rows]
where the time goes in v4:
time: 570 us; the launch traced here: 566 us
  Pallas kernels  538 us (94%)
  other arithmetic  15.5 us (3%)
  local copies, waits for them, and re-layouts  12.5 us (2%)
    pallas_call x1, Pallas kernels, shards(): build_front(*sizes)  216 us
    pallas_call x1, Pallas kernels, shards(): build_back(*sizes)  195 us
    pallas_call x1, Pallas kernels, shards(): build_grads(*sizes)  127 us

profile of v4, /device:TPU:0, one launch (start us, length us, event | category | flops | bytes accessed | tf_op | source)
XLA Modules:
  0.0 566.4 jit_solution(15375264752030845414)
XLA Ops:
  0.7 0.6 broadcast_in_dim_tile.3.freqs
  1.3 1.3 copy.23.spans
  2.6 1.3 broadcast_in_dim.12.gain_one_own
  3.9 1.3 broadcast_in_dim.13.gain_two_own
  5.1 215.6 %front.1 = (bf16[2048,1024]{1,0:T(8,128)(2,1)}, bf16[2048,1024]{1,0:T(8,128)(2,1)}, bf16[1024,2048]{1,0:T(8,128)(2,1)}, bf16[4,256,2048]{2,1,0:T(8,128)(2,1)}, b...) custom-call(bf16[256,1024]{1,0:T(8,128)(2,1)} %bitcast.13, ...), custom_call_target="tpu_custom_call" | custom-call | flops 8000000000 | bytes 80000000 | tf_op jit(solution)/shard_map/front/pallas_call | solution.py:1513
  220.7 195.3 %back.1 = (bf16[256,1024]{1,0:T(8,128)(2,1)}, bf16[512,4096]{1,0:T(8,128)(2,1)}, bf16[128,4096]{1,0:T(8,128)(2,1)}, bf16[4,4,256,512]{3,2,1,0:T(8,128)(2,1)}, bf...) custom-call(bf16[2048,1024]{1,0:T(8,128)(2,1)} %get-tuple-element.45.gat, ...), custom_call_target="tpu_custom_call" | custom-call | flops 49999998976 | bytes 80000000 | tf_op jit(solution)/shard_map/back/pallas_call | solution.py:1517
  416.0 126.9 %grads.1 = (bf16[512,4096]{1,0:T(8,128)(2,1)}, bf16[1024,512]{1,0:T(8,128)(2,1)}, bf16[512,1536]{1,0:T(8,128)(2,1)}, f32[8,512]{1,0:T(8,128)}, bf16[256,1024]{1,0:T(8,128)(2,1)}) custom-call(bf16[256,1024]{1,0:T(8,128)(2,1)} %get-tuple-element.44.attn, bf16[256,2048]{1,0:T(8,128)(2,1)} %get-tuple-element.63.mid_full, ...), custom_call_target="tpu_custom_call" | custom-call | flops 4000000000 | bytes 40000000 | tf_op jit(solution)/shard_map/grads/pallas_call | solution.py:1521
  542.9 0.0 copy-start.3
  542.9 1.4 fusion.1
  544.3 2.1 fusion
  546.4 0.0 copy-start.2
  546.4 2.9 slice.20
  549.3 0.0 copy-done.3
  549.3 1.6 convert_element_type.19
  551.0 0.0 copy-done.2
  551.0 0.0 copy-start.1
  551.0 4.5 convert_element_type.21
  555.4 0.0 copy-done.1
  555.4 0.0 copy-start
  555.4 4.5 convert_element_type.20
  559.9 0.0 copy-done
  559.9 0.0 copy-start.5
  559.9 0.0 copy-start.4
  559.9 4.9 bitcast_convert_fusion
  564.8 0.0 copy-done.5
  564.8 0.8 copy.26
  565.6 0.0 copy-done.4
  565.6 0.8 copy.27
  (2 shorter events, 0.0 us)
Async XLA Ops:
  542.9 6.4 %copy-start.3 = (bf16[1024,512]{1,0:T(8,128)(2,1)S(1)}, bf16[1024,512]{1,0:T(8,128)(2,1)}, u32[]{:S(2)}) copy-start(bf16[1024,512]{1,0:T(8,128)(2,1)} %get-tuple-element.73) | copy-start | bytes 3145732
  546.4 4.6 copy-start.2
  551.0 4.5 copy-start.1
  555.4 4.5 copy-start
  559.9 4.9 copy-start.5
  559.9 5.7 %copy-start.4 = (bf16[256,1024]{1,0:T(8,128)(2,1)S(1)}, bf16[256,1024]{1,0:T(8,128)(2,1)}, u32[]{:S(2)}) copy-start(bf16[256,1024]{1,0:T(8,128)(2,1)} %get-tuple-element.70) | copy-start | bytes 1572868

commit v5 on v4

--- a/solution.py
+++ b/solution.py
@@ -285,14 +285,24 @@
                 z_wait(item, p)
                 share(item, p)
 
+        def step(item, i):
+            p = order[i]
+            z_wait(item, p)
+            forward(item, p)
+            if item == OUT:
+                share(OUT, p)
+            else:
+                base = 1 if item == COT else 3 + planes
+                x_copy(base + p, slot(item, p, c), slot(item, p, c)).start()
+
         items = (GATE, UP, DOWN)
-        send_units(GATE)
+        last = planes - 1
+        step(OUT, 0)
+        spread(COT, cot)
+        cot_copy = x_copy(1 + z, cot, slot(COT, z, c))
+        cot_copy.start()
         for p in order:
             share_on(QKV, p)
-            z_wait(OUT, p)
-            forward(OUT, p)
-            share(OUT, p)
-        send_units(UP)
         for p in order:
             shared(QKV, p)
         qkv_keep = pltpu.make_async_copy(qkv_w, qkv_hbm, own_sem.at[0])
@@ -331,6 +341,10 @@
         kv_sends.append(copy(kv_slot(c), kv_slot(c), k_send.at[COT, 0, 0], k_recv.at[COT, 0, 0], at_k))
         for one in kv_sends:
             one.start()
+        for i in range(1, last - 1):
+            step(OUT, i)
+        step(COT, 0)
+        send_units(GATE)
 
         @pl.loop(0, n_q)
         def _(j):
@@ -350,11 +364,6 @@
         for by in range(outers):
             q = lax.rem(o - by + outers, outers) * 2 + 1 - k
             copy(kv_slot(q), kv_slot(q), k_send.at[COT, 0, by], k_recv.at[COT, 0, by], at_k).wait_recv()
-
-        send_units(DOWN)
-        spread(COT, cot)
-        cot_copy = x_copy(1 + z, cot, slot(COT, z, c))
-        cot_copy.start()
 
         def attend(first_head, last_head):
             @pl.loop(first_head, last_head)
@@ -372,9 +381,12 @@
                 log_sum[pl.ds(h, 1), :] = top + jnp.log(total)
 
         attend(0, heads // 2)
+        step(OUT, last - 1)
+        for i in range(1, last - 1):
+            step(COT, i)
+        send_units(UP)
         for p in order:
             share_on(OUT, p)
-        share_units(GATE)
         attend(heads // 2, heads)
 
         for j in range(n_q):
@@ -410,7 +422,6 @@
             part = jnp.dot(attn[...], out_w[:, cols], preferred_element_type=F32)
             mid_own[:, here] = tok[:, here].astype(F32) + part
 
-        share_units(UP)
         half_copy.wait_recv()
         mid = mid_own[...] + recv_half[...].astype(F32)
         mid_own[...] = mid
@@ -429,16 +440,21 @@
         norm_copy.start()
         norm_keep = pltpu.make_async_copy(norm_own, slot(NORM, z, c), own_sem.at[6])
         norm_keep.start()
+        step(COT, last - 1)
+        step(NORM, 0)
+        send_units(DOWN)
+        share_units(GATE)
+        step(NORM, 1)
+        share_units(UP)
+        for i in range(2, last):
+            step(NORM, i)
+        for s in range(1, planes):
+            share_on(GATE, lax.rem(z + planes - s, planes))
         share_units(DOWN)
-        for i, p in enumerate(order):
-            z_wait(NORM, p)
-            forward(NORM, p)
-            x_copy(3 + planes + p, slot(NORM, p, c), slot(NORM, p, c)).start()
-            z_wait(COT, p)
-            forward(COT, p)
-            x_copy(1 + p, slot(COT, p, c), slot(COT, p, c)).start()
-            for item in items:
-                share_on(item, lax.rem(z + planes - 1 - i, planes))
+        for s in range(1, planes):
+            share_on(UP, lax.rem(z + planes - s, planes))
+        for s in range(1, planes):
+            share_on(DOWN, lax.rem(z + planes - s, planes))
 
         for s in range(1, planes):
             p = lax.rem(z + s, planes)
@@ -694,10 +710,10 @@
 
 
 def store_part(part, i, tile):
-    size = part.shape[2]
-    per = part.shape[1] * size // TILE
-    for r in range(TILE // size):
-        part[i // per, lax.rem(i, per) * (TILE // size) + r] = tile[r * size : (r + 1) * size].astype(BF)
+    size, taken = part.shape[2], tile.shape[0]
+    per = part.shape[1] * size // taken
+    for r in range(taken // size):
+        part[i // per, lax.rem(i, per) * (taken // size) + r] = tile[r * size : (r + 1) * size].astype(BF)
 
 
 def build_back(planes, contexts, rows, width, query_cols, kv_cols, units):
@@ -717,7 +733,7 @@
     def kernel(
         gate_hbm, up_hbm, down_hbm, norm_hbm, cot_hbm, qkv_hbm, out_hbm, q_hbm, kv_hbm, mid_hbm, tok_hbm,
         gains, cosine, sine, pos_q, pos_k, log_sum, scales,
-        input_grad, gate_out, up_strip, down_out, mid_full, qkv_grad, gain_rows, mlp_part,
+        input_grad, gate_strip, up_strip, down_out, mid_full, qkv_grad, gain_rows, mlp_part,
         norm_x_in, norm_z_in, norm_x_out, norm_sum, mlp_stage,
         row_core_in, col_core_in, row_outer_in, col_outer_in, row_outer_out, col_outer_out, row_sum, col_sum,
         kv_core_in, kv_outer_in, sq_out, sq_in, first_x_out, first_x_in,
@@ -778,13 +794,13 @@
                 for i, p in enumerate(blocks)
             ]
 
-            def product(part, left, right):
+            def product(part, left, right, size):
                 total = planes * rows
 
-                @pl.loop(0, left.shape[2] // TILE)
+                @pl.loop(0, left.shape[2] // size)
                 def _(i):
-                    cols = pl.ds(pl.multiple_of(i * TILE, TILE), TILE)
-                    tile = t_dot(left[:, :, cols].reshape(total, TILE), right[...].reshape(total, right.shape[2]))
+                    cols = pl.ds(pl.multiple_of(i * size, size), size)
+                    tile = t_dot(left[:, :, cols].reshape(total, size), right[...].reshape(total, right.shape[2]))
                     store_part(part, i, tile)
 
             def with_weights(gate_w, up_w, down_w, col_part):
@@ -834,9 +850,9 @@
                         here = pl.ds(pl.multiple_of(j * WIDE, WIDE), WIDE)
                         norm_sum[p, :, here] = tile_of(own_cols + j * WIDE).astype(BF)
 
-                    if i > 0:
-                        norm_on(i - 1)
-                        norm_z(blocks[i - 1]).start()
+                    if i > 1:
+                        norm_on(i - 2)
+                        norm_z(blocks[i - 2]).start()
 
                 down = Reduction(
                     ring, DOWN, col_part, col_core_in, col_outer_out, col_outer_in, col_sum, sems
@@ -844,8 +860,10 @@
                 for i in range(planes):
                     forward_block(i)
                     norm_block(i)
-                product(col_part, hid, cot)
+                product(col_part, hid, cot, TILE)
                 down.to_core()
+                norm_on(planes - 2)
+                norm_z(blocks[planes - 2]).start()
 
                 def stage_copy(i):
                     return pltpu.make_async_copy(mlp_stage.at[i % 2], mlp_part.at[blocks[i]], stage_sem.at[i % 2])
@@ -879,13 +897,13 @@
                 up = Reduction(
                     ring, UP, row_part, row_core_in, row_outer_out.at[1], row_outer_in.at[1], row_sum.at[1], sems
                 )
-                product(row_part, norm, gate_grad)
+                product(row_part, norm, gate_grad, WIDE)
                 gate.to_core()
                 norm_on(planes - 1)
                 gate.from_core()
                 gate.core_done()
                 pl.semaphore_signal(credit, inc=1, device_id=ring.at_k, device_id_type=MESH)
-                product(row_part, norm, up_grad)
+                product(row_part, norm, up_grad, WIDE)
                 pl.semaphore_wait(credit, 1)
                 up.to_core()
                 up.from_core()
@@ -910,9 +928,7 @@
             if item == DOWN:
                 return down_out.at[home, c]
             cols = pl.ds(pl.multiple_of(home * units, units), units)
-            if item == GATE:
-                return gate_out.at[pl.ds(pl.multiple_of(c * strip, strip), strip), cols]
-            return up_strip.at[:, cols]
+            return (gate_strip if item == GATE else up_strip).at[:, cols]
 
         def strip_copy(item, s):
             goal = ring.plane(s)
@@ -938,7 +954,6 @@
 
         share_sems = (sy_send, sy_recv, sk_send, sk_recv)
         down_share = Share(ring, 0, lambda q: down_out.at[:, q], share_sems)
-        gate_share = Share(ring, 1, lambda q: gate_out.at[pl.ds(pl.multiple_of(q * strip, strip), strip), :], share_sems)
 
         def attention(mid_grad, q_pad, kv_all, tok, grad_pad, query_out, key_sum, value_sum, kv_grad, kv_out):
             loads = [
@@ -1026,8 +1041,6 @@
 
             attend_back(0, heads // 2)
             to_planes(GATE, gate)
-            from_planes(DOWN)
-            down_share.start()
             attend_back(heads // 2, heads)
             for i in range(n_kv):
                 kv_grad[:, i] = key_sum[i].astype(BF).reshape(contexts, rows, LANES)
@@ -1056,7 +1069,6 @@
                     lo = pltpu.roll(lo, HEAD_WIDTH, 1)
                 u = jnp.where(low, lo, hi) * FACTOR
                 qkv_grad[:, j * LANES : (j + 1) * LANES] = rotate_tile(u, cosine[...], -sine[...], first).astype(BF)
-            to_planes(UP, up)
             for other in range(outers):
                 kv_core(other).wait_recv()
             for by in range(1, outers):
@@ -1065,6 +1077,9 @@
                     kv_grad[goal * 2 + k].astype(F32) + kv_core_in[goal].astype(F32)
                 ).astype(BF)
                 kv_outer(by).start()
+            to_planes(UP, up)
+            from_planes(DOWN)
+            down_share.start()
             kv_sum = kv_grad[c].astype(F32) + kv_core_in[o].astype(F32)
             for by in range(1, outers):
                 kv_outer(by).wait_recv()
@@ -1100,8 +1115,6 @@
                     here = pl.ds(pl.multiple_of(j * WIDE, WIDE), WIDE)
                     own[:, here] = tile_of(own_cols + j * WIDE)
 
-                from_planes(GATE)
-                gate_share.start()
                 first_swap.wait()
                 scale_one = scales[0][:, 0:1]
                 gain_one = gains[0:1, pl.ds(own_cols, half)].astype(F32)
@@ -1129,10 +1142,9 @@
         )
 
         down_share.pass_on()
-        gate_share.pass_on()
+        from_planes(GATE)
         from_planes(UP)
         down_share.finish()
-        gate_share.finish()
         for item in (DOWN, GATE, UP):
             for s in range(1, planes):
                 strip_copy(item, s).wait_send()
@@ -1154,7 +1166,7 @@
         name="back",
         out_shape=(
             shape((rows, half), BF),
-            shape((depth, planes * units), BF),
+            shape((strip, planes * units), BF),
             shape((strip, planes * units), BF),
             shape((planes, contexts, unit_strip, depth), BF),
             shape((rows, width), BF),
@@ -1215,11 +1227,11 @@
     qkv_cols = query_cols + 2 * kv_cols
     lots = max(outers - 1, 1)
     per_half = planes // 2
-    OUT, QKV, UP = range(3)
+    OUT, QKV, UP, GATE = range(4)
 
     def kernel(
-        attn, mid_full, normed_one, qkv_grad, gain_rows, mid_own, up_strip, mlp_part,
-        up_out, out_out, qkv_out, gain_out, result,
+        attn, mid_full, normed_one, qkv_grad, gain_rows, mid_own, gate_strip, up_strip, mlp_part,
+        gate_out, up_out, out_out, qkv_out, gain_out, result,
         out_part, qkv_part, out_core, qkv_core, out_outer_out, qkv_outer_out, out_outer_in, qkv_outer_in,
         out_sum, qkv_sum, out_z, qkv_z, gain_z, gain_y, gain_k, gain_now, mlp_x_in, mlp_z_in, mlp_sum,
         k_send, k_recv, y_send, y_recv, z_send, z_recv, sk_send, sk_recv, sy_send, sy_recv, gain_send, gain_recv,
@@ -1237,8 +1249,14 @@
         up_share = Share(ring, UP, rows_of(up_out, strip), share_sems, up_strip)
         out_share = Share(ring, OUT, rows_of(out_out, out_strip), share_sems)
         qkv_share = Share(ring, QKV, rows_of(qkv_out, strip), share_sems)
-        keep = pltpu.make_async_copy(up_strip, rows_of(up_out, strip)(c), own_sem.at[0])
-        keep.start()
+        gate_share = Share(ring, GATE, rows_of(gate_out, strip), share_sems, gate_strip)
+        gate_share.start()
+        keeps = [
+            pltpu.make_async_copy(gate_strip, rows_of(gate_out, strip)(c), own_sem.at[0]),
+            pltpu.make_async_copy(up_strip, rows_of(up_out, strip)(c), own_sem.at[2]),
+        ]
+        for one in keeps:
+            one.start()
 
         own_cols = pl.multiple_of(t * half, half)
         other_cols = pl.multiple_of((1 - t) * half, half)
@@ -1391,10 +1409,11 @@
             copy_to(there, there, mz_send.at[p], mz_recv.at[p], ring.at_k).wait_recv()
             total = total + there[...].astype(F32)
         result[...] = total.astype(BF)
-        for one in (up_share, out_share, qkv_share):
+        for one in (gate_share, up_share, qkv_share, out_share):
             one.pass_on()
-        keep.wait()
-        for one in (up_share, out_share, qkv_share):
+        for one in keeps:
+            one.wait()
+        for one in (gate_share, up_share, qkv_share, out_share):
             one.finish()
         for p in blocks:
             mlp_x(p).wait_send()
@@ -1429,13 +1448,14 @@
         name="grads",
         out_shape=(
             shape((depth, planes * units), BF),
+            shape((depth, planes * units), BF),
             shape((query_cols, depth), BF),
             shape((depth, qkv_cols), BF),
             shape((8, depth), F32),
             shape((rows, half), BF),
         ),
-        in_specs=[vmem] * 6 + [hbm] * 2,
-        out_specs=(hbm, vmem, vmem, vmem, vmem),
+        in_specs=[vmem] * 6 + [hbm] * 3,
+        out_specs=(hbm, hbm, vmem, vmem, vmem, vmem),
         scratch_shapes=[
             pltpu.VMEM((1, contexts, out_strip, width), BF),
             pltpu.VMEM((planes, contexts, strip, qkv_cols), BF),
@@ -1462,17 +1482,17 @@
             dma((2, max(outers, 2))),
             dma((2, planes)),
             dma((2, planes)),
-            dma((3, outers)),
-            dma((3, outers)),
-            dma((3, max(outers, 2))),
-            dma((3, max(outers, 2))),
+            dma((4, outers)),
+            dma((4, outers)),
+            dma((4, max(outers, 2))),
+            dma((4, max(outers, 2))),
             dma((per_half + outers + 1,)),
             dma((planes + outers + 1,)),
             dma((planes,)),
             dma((planes,)),
             dma((planes,)),
             dma((planes,)),
-            dma((2,)),
+            dma((3,)),
         ],
         compiler_params=pltpu.CompilerParams(
             collective_id=2, has_side_effects=True, vmem_limit_bytes=VMEM_LIMIT
@@ -1514,12 +1534,12 @@
         tok_own, cot_own, attn_gain[None], mlp_gain[None], w_query, key_weight, value_weight, w_out, w_gate, w_up,
         w_down, span_order, freqs,
     )
-    input_grad, gate_out, up_strip, down_out, mid_full, qkv_grad, gain_rows, mlp_part = build_back(*sizes)(
+    input_grad, gate_strip, up_strip, down_out, mid_full, qkv_grad, gain_rows, mlp_part = build_back(*sizes)(
         gate_w, up_w, down_w, norm_all, cot_all, qkv_w, out_w, q_pad, kv_all, mid_own, tok_all, gains,
         cosine_table, sine_table, pos_q, pos_k, log_sum, scales,
     )
-    up_out, out_out, qkv_out, gain_out, result = build_grads(*sizes)(
-        attn, mid_full, normed_one, qkv_grad, gain_rows, mid_own, up_strip, mlp_part
+    gate_out, up_out, out_out, qkv_out, gain_out, result = build_grads(*sizes)(
+        attn, mid_full, normed_one, qkv_grad, gain_rows, mid_own, gate_strip, up_strip, mlp_part
     )
     qkv_out = qkv_out.astype(F32)
     return (

time: 570 us -> 523 us (0.918)
  Pallas kernels: 538 us -> 491 us
    pallas_call x1, Pallas kernels: 195 us -> 158 us  [shards(): build_back(*sizes)]
    pallas_call x1, Pallas kernels: 216 us -> 206 us  [shards(): build_front(*sizes)]
where the time goes in v5:
time: 523 us; the launch traced here: 519 us
  Pallas kernels  491 us (94%)
  other arithmetic  15.5 us (3%)
  local copies, waits for them, and re-layouts  12.5 us (2%)
    pallas_call x1, Pallas kernels, shards(): build_front(*sizes)  206 us
    pallas_call x1, Pallas kernels, shards(): build_back(*sizes)  158 us
    pallas_call x1, Pallas kernels, shards(): build_grads(*sizes)  127 us

profile of v5, /device:TPU:0, one launch (start us, length us, event | category | flops | bytes accessed | tf_op | source)
XLA Modules:
  0.0 519.2 jit_solution(18097929298177680549)
XLA Ops:
  0.7 0.6 broadcast_in_dim_tile.3.freqs
  1.3 1.3 copy.23.spans
  2.6 1.3 broadcast_in_dim.12.gain_one_own
  3.9 1.3 broadcast_in_dim.13.gain_two_own
  5.1 205.7 %front.1 = (bf16[2048,1024]{1,0:T(8,128)(2,1)}, bf16[2048,1024]{1,0:T(8,128)(2,1)}, bf16[1024,2048]{1,0:T(8,128)(2,1)}, bf16[4,256,2048]{2,1,0:T(8,128)(2,1)}, b...) custom-call(bf16[256,1024]{1,0:T(8,128)(2,1)} %bitcast.13, ...), custom_call_target="tpu_custom_call" | custom-call | flops 8000000000 | bytes 80000000 | tf_op jit(solution)/shard_map/front/pallas_call | solution.py:1533
  210.8 157.9 %back.1 = (bf16[256,1024]{1,0:T(8,128)(2,1)}, bf16[128,4096]{1,0:T(8,128)(2,1)}, bf16[128,4096]{1,0:T(8,128)(2,1)}, bf16[4,4,256,512]{3,2,1,0:T(8,128)(2,1)}, bf...) custom-call(bf16[2048,1024]{1,0:T(8,128)(2,1)} %get-tuple-element.46.gat, ...), custom_call_target="tpu_custom_call" | custom-call | flops 49999998976 | bytes 80000000 | tf_op jit(solution)/shard_map/back/pallas_call | solution.py:1537
  368.7 127.0 %grads.1 = (bf16[512,4096]{1,0:T(8,128)(2,1)}, bf16[512,4096]{1,0:T(8,128)(2,1)}, bf16[1024,512]{1,0:T(8,128)(2,1)}, bf16[512,1536]{1,0:T(8,128)(2,1)}, f32[8,512]{1,0:T(8,128)}, /*index=5*/bf16[256,1024]{1,0:T(8,128)(2,1)}) custom-call(bf16[256,1024]{1,0:T(8,128)(2,1)} %get-tuple-element.45.attn, bf16[256,2048]{1,0:T(8,128)(2,1)} %get-tuple-element.64.mid_full, ...), custom_call_target="tpu_custom_call" | custom-call | flops 4000000000 | bytes 40000000 | tf_op jit(solution)/shard_map/grads/pallas_call | solution.py:1541
  495.7 0.0 copy-start.3
  495.7 1.4 fusion.1
  497.1 2.1 fusion
  499.2 0.0 copy-start.2
  499.2 2.9 slice.20
  502.1 0.0 copy-done.3
  502.1 1.6 convert_element_type.19
  503.8 0.0 copy-done.2
  503.8 0.0 copy-start.1
  503.8 4.5 convert_element_type.20
  508.2 0.0 copy-done.1
  508.2 0.0 copy-start
  508.3 4.5 convert_element_type.21
  512.7 0.0 copy-done
  512.7 0.0 copy-start.5
  512.7 0.0 copy-start.4
  512.7 4.9 bitcast_convert_fusion
  517.6 0.0 copy-done.5
  517.6 0.8 copy.26
  518.4 0.0 copy-done.4
  518.4 0.8 copy.27
  (2 shorter events, 0.0 us)
Async XLA Ops:
  495.7 6.4 %copy-start.3 = (bf16[1024,512]{1,0:T(8,128)(2,1)S(1)}, bf16[1024,512]{1,0:T(8,128)(2,1)}, u32[]{:S(2)}) copy-start(bf16[1024,512]{1,0:T(8,128)(2,1)} %get-tuple-element.75) | copy-start | bytes 3145732
  499.2 4.6 copy-start.2
  503.8 4.5 copy-start.1
  508.2 4.5 copy-start
  512.7 4.9 copy-start.5
  512.7 5.7 %copy-start.4 = (bf16[256,1024]{1,0:T(8,128)(2,1)S(1)}, bf16[256,1024]{1,0:T(8,128)(2,1)}, u32[]{:S(2)}) copy-start(bf16[256,1024]{1,0:T(8,128)(2,1)} %get-tuple-element.72) | copy-start | bytes 1572868

commit v6 on v5

--- a/solution.py
+++ b/solution.py
@@ -15,6 +15,7 @@
 LANES = 128
 TILE = 256
 WIDE = 512
+STEP = 32
 FACTOR = 1.0 / math.sqrt(HEAD_WIDTH)
 VMEM_LIMIT = 62 * 2**20
 MESH = pl.DeviceIdType.MESH
@@ -52,15 +53,18 @@
     heads = query_cols // HEAD_WIDTH
     group = query_cols // kv_cols
     qkv_cols = query_cols + 2 * kv_cols
-    QKV, OUT, GATE, UP, DOWN, COT, NORM, GAIN = range(8)
+    QKV, OUT, GATE, UP, DOWN, COT, NORM, GAIN, LATE = range(9)
+    half_rows = rows // 2
+    base_of = {COT: 1, NORM: 3 + planes, LATE: 3 + 2 * planes}
 
     def kernel(
         tok, cot, gain_one_own, gain_two_own, query_own, key_own, value_own, out_own, gate_own, up_own, down_own,
         spans, freqs,
-        gate_w, up_w, down_w, cot_all, norm_all, qkv_hbm, out_hbm, gains, q_pad, kv_all, attn, log_sum,
-        mid_own, normed_one, tok_all, scales, cosine, sine, pos_q, pos_k,
-        qkv_w, out_w, gains_own, lin, heads_out, send_half, recv_half, norm_own, sq_send, sq_recv,
-        z_send, z_recv, y_send, y_recv, k_send, k_recv, x_send, x_recv, own_sem,
+        gate_hbm, up_hbm, down_hbm, cot_hbm, norm_hbm, qkv_hbm, out_hbm, hid_hbm, gate_grad_hbm, up_grad_hbm, gains, q_hbm, kv_hbm, attn_hbm,
+        log_sum, mid_hbm, normed_hbm, tok_hbm, scales, cosine, sine, pos_q, pos_k,
+        q_pad, kv_all, attn, mid_own, normed_one, tok_all,
+        gate_w, up_w, down_w, cot_all, norm_all, acts, qkv_w, out_w, gains_own, lin, heads_out, send_half, recv_half, norm_own, sq_send, sq_recv,
+        z_send, z_recv, y_send, y_recv, k_send, k_recv, x_send, x_recv, own_sem, act_sem,
     ):
         z = lax.axis_index("fsdp")
         c = lax.axis_index("context")
@@ -110,7 +114,7 @@
                 return down_w.at[pl.ds(q * unit_strip, unit_strip), pl.ds(p * depth, depth)]
             if item == COT:
                 return cot_all.at[p, :, pl.ds(t * half, half)]
-            return norm_all.at[p, :, pl.ds(t * half, half)]
+            return norm_all.at[p, pl.ds(0 if item == NORM else half_rows, half_rows), pl.ds(t * half, half)]
 
         def z_copy(item, p, src, goal, way):
             return copy(src, slot(item, p, c), z_send.at[item, p, way], z_recv.at[item, p], at_z(goal))
@@ -237,6 +241,23 @@
         gains[:, pl.ds(z * depth, depth)] = gains_own[...]
         tok_all[:, tok_cols] = tok[...]
 
+        def at_distance(i, act):
+            for p in (z - (i + 1), z + (i + 1)):
+
+                @pl.when((p >= 0) & (p < planes))
+                def _(p=p):
+                    act(p)
+
+        def qkv_step(i):
+            def act(p):
+                z_wait(QKV, p)
+                forward(QKV, p)
+                share(QKV, p)
+
+            at_distance(i, act)
+
+        qkv_step(0)
+
         def positions(q, shape, axis):
             r = lax.broadcasted_iota(jnp.int32, shape, axis)
             return jnp.where(r < rows // 2, spans[q, 0], spans[q, 1]) * (rows // 2) + lax.rem(r, rows // 2)
@@ -244,56 +265,63 @@
         for q in range(contexts):
             pos_k[q * rows : (q + 1) * rows, :] = positions(q, (rows, 1), 0)
         pos_q[...] = positions(c, (8, rows), 1)
+        side_of = lax.rem(lax.broadcasted_iota(jnp.int32, (rows, LANES), 1), HEAD_WIDTH) < HEAD_WIDTH // 2
         angle = positions(c, (rows, LANES), 0).astype(F32) * freqs[...]
         cosine[...] = jnp.cos(angle)
-        side_of = lax.rem(lax.broadcasted_iota(jnp.int32, (rows, LANES), 1), HEAD_WIDTH) < HEAD_WIDTH // 2
-        sine[...] = jnp.where(side_of, -jnp.sin(angle), jnp.sin(angle))
+        turned = jnp.sin(angle)
+        sine[...] = jnp.where(side_of, -turned, turned)
+        qkv_step(1)
 
         tok_copy.wait()
         for s in range(1, planes):
             p = lax.rem(z + s, planes)
             there = gains.at[:, pl.ds(p * depth, depth)]
             copy(there, there, z_send.at[GAIN, p, 0], z_recv.at[GAIN, p], at_k).wait_recv()
-        x = tok_all[...].astype(F32)
-        scale = lax.rsqrt(jnp.mean(x * x, -1, keepdims=True) + EPS)
-        scales[0] = jnp.broadcast_to(scale, (rows, LANES))
-        normed_one[...] = (x * scale * gains[0:1, :].astype(F32)).astype(BF)
-
-        for p in order:
-            z_wait(QKV, p)
-            forward(QKV, p)
-            share(QKV, p)
+
+        @pl.loop(0, rows // STEP)
+        def _(i):
+            r = pl.ds(pl.multiple_of(i * STEP, STEP), STEP)
+            x = tok_all[r, :].astype(F32)
+            scale = lax.rsqrt(jnp.mean(x * x, -1, keepdims=True) + EPS)
+            scales[0, r, :] = jnp.broadcast_to(scale, (STEP, LANES))
+            normed_one[r, :] = (x * scale * gains[0:1, :]).astype(BF)
+
+        for i in range(2, planes - 1):
+            qkv_step(i)
 
         spread(OUT, out_src)
         sends = []
 
         def send_units(item):
-            for s in range(1, planes):
-                goal = lax.rem(z + s, planes)
+            for i, goal in enumerate(order):
                 if item == DOWN:
                     src = down_own.at[pl.ds(goal * units + c * unit_strip, unit_strip), :]
                 else:
                     own = gate_own if item == GATE else up_own
                     src = own.at[pl.ds(c * strip, strip), pl.ds(goal * units, units)]
-                one = z_copy(item, z, src, goal, s - 1)
+                one = z_copy(item, z, src, goal, i)
                 one.start()
                 sends.append(one)
 
         def share_units(item):
-            for s in range(1, planes):
-                p = lax.rem(z + planes - s, planes)
+            for p in order:
                 z_wait(item, p)
                 share(item, p)
 
-        def step(item, i):
-            p = order[i]
-            z_wait(item, p)
-            forward(item, p)
-            if item == OUT:
-                share(OUT, p)
-            else:
-                base = 1 if item == COT else 3 + planes
-                x_copy(base + p, slot(item, p, c), slot(item, p, c)).start()
+        def cross(item, i):
+            base = base_of[item]
+            at_distance(i, lambda p: x_copy(base + p, slot(item, p, c), slot(item, p, c)).start())
+
+        def step(item, i, crosses=True):
+            def act(p):
+                z_wait(item, p)
+                forward(item, p)
+                if item == OUT:
+                    share(OUT, p)
+
+            at_distance(i, act)
+            if item != OUT and crosses:
+                cross(item, i)
 
         items = (GATE, UP, DOWN)
         last = planes - 1
@@ -383,8 +411,9 @@
         attend(0, heads // 2)
         step(OUT, last - 1)
         for i in range(1, last - 1):
-            step(COT, i)
+            step(COT, i, False)
         send_units(UP)
+        send_units(DOWN)
         for p in order:
             share_on(OUT, p)
         attend(heads // 2, heads)
@@ -414,6 +443,8 @@
 
         half_copy = x_copy(1 + planes, send_half, recv_half)
         half_copy.start()
+        for i in range(1, last - 1):
+            cross(COT, i)
 
         @pl.loop(0, n_out)
         def _(i):
@@ -423,64 +454,136 @@
             mid_own[:, here] = tok[:, here].astype(F32) + part
 
         half_copy.wait_recv()
-        mid = mid_own[...] + recv_half[...].astype(F32)
-        mid_own[...] = mid
-        squares = jnp.sum(mid * mid, -1, keepdims=True)
-        sq_send[...] = jnp.broadcast_to(squares, (rows, LANES))
+
+        @pl.loop(0, rows // STEP)
+        def _(i):
+            r = pl.ds(pl.multiple_of(i * STEP, STEP), STEP)
+            mid = mid_own[r, :] + recv_half[r, :].astype(F32)
+            mid_own[r, :] = mid
+            sq_send[r, :] = jnp.broadcast_to(jnp.sum(mid * mid, -1, keepdims=True), (STEP, LANES))
+
         sq_copy = x_copy(2 + planes, sq_send, sq_recv)
         sq_copy.start()
         sq_copy.wait_recv()
-        scale_two = lax.rsqrt((squares + sq_recv[:, 0:1]) * (1.0 / width) + EPS)
-        scales[1] = jnp.broadcast_to(scale_two, (rows, LANES))
-        gain_two = gains[1:2, pl.ds(pl.multiple_of(t * half, half), half)].astype(F32)
-        norm_own[...] = (mid_own[...] * scale_two * gain_two).astype(BF)
-
-        spread(NORM, norm_own)
-        norm_copy = x_copy(3 + planes + z, norm_own, slot(NORM, z, c))
-        norm_copy.start()
-        norm_keep = pltpu.make_async_copy(norm_own, slot(NORM, z, c), own_sem.at[6])
+        gain_two = gains[1:2, pl.ds(pl.multiple_of(t * half, half), half)]
+
+        @pl.loop(0, rows // STEP)
+        def _(i):
+            r = pl.ds(pl.multiple_of(i * STEP, STEP), STEP)
+            squares = sq_send[r, 0:1] + sq_recv[r, 0:1]
+            scale = lax.rsqrt(squares * (1.0 / width) + EPS)
+            scales[1, r, :] = jnp.broadcast_to(scale, (STEP, LANES))
+            norm_own[r, :] = (mid_own[r, :] * scale * gain_two).astype(BF)
+
+        norm_src = {
+            NORM: norm_own.at[pl.ds(0, half_rows), :], LATE: norm_own.at[pl.ds(half_rows, half_rows), :]
+        }
+        norm_copies = []
+        for item, src in norm_src.items():
+            spread(item, src)
+            one = x_copy(base_of[item] + z, src, slot(item, z, c))
+            one.start()
+            norm_copies.append(one)
+        norm_keep = pltpu.make_async_copy(norm_own, norm_all.at[z, :, pl.ds(t * half, half)], own_sem.at[6])
         norm_keep.start()
+        moved = (
+            (q_pad, q_hbm), (kv_all, kv_hbm), (attn, attn_hbm), (mid_own, mid_hbm), (normed_one, normed_hbm),
+            (tok_all, tok_hbm),
+        )
+        moves = [
+            pltpu.make_async_copy(src, dst, act_sem.at[3 + 5 * planes + i]) for i, (src, dst) in enumerate(moved)
+        ]
+        for one in moves:
+            one.start()
+        share_units(GATE)
+        share_units(UP)
         step(COT, last - 1)
-        step(NORM, 0)
-        send_units(DOWN)
-        share_units(GATE)
-        step(NORM, 1)
-        share_units(UP)
-        for i in range(2, last):
+        for item in (GATE, UP):
+            for p in order:
+                share_on(item, p)
+        share_units(DOWN)
+        for i in range(last - 1):
             step(NORM, i)
-        for s in range(1, planes):
-            share_on(GATE, lax.rem(z + planes - s, planes))
-        share_units(DOWN)
-        for s in range(1, planes):
-            share_on(UP, lax.rem(z + planes - s, planes))
-        for s in range(1, planes):
-            share_on(DOWN, lax.rem(z + planes - s, planes))
-
-        for s in range(1, planes):
-            p = lax.rem(z + s, planes)
-            for item in items:
-                shared(item, p)
-        for p in [z] + order:
-            for base, item in ((1, COT), (3 + planes, NORM)):
-                there = (cot_all if item == COT else norm_all).at[p, :, pl.ds((1 - t) * half, half)]
-                copy(there, there, x_send.at[base + p], x_recv.at[base + p], at_x).wait_recv()
-        for one in own_copies[1:] + [qkv_keep, out_keep]:
+            step(LATE, i)
+        for p in order:
+            share_on(DOWN, p)
+        for item in items:
+            for s in range(1, planes):
+                shared(item, lax.rem(z + s, planes))
+        for one in own_copies[1:]:
             one.wait()
         norm_keep.wait()
-        tok_copy_out = [half_copy, sq_copy, cot_copy, norm_copy]
+        unit_keeps = [
+            pltpu.make_async_copy(src, dst, act_sem.at[i])
+            for i, (src, dst) in enumerate(((gate_w, gate_hbm), (up_w, up_hbm), (down_w, down_hbm)))
+        ]
+        for one in unit_keeps:
+            one.start()
+
+        def forward_block(p):
+            other = pl.ds((1 - t) * half, half)
+            for item, there in (
+                (COT, cot_all.at[p, :, other]),
+                (NORM, norm_all.at[p, pl.ds(0, half_rows), other]),
+                (LATE, norm_all.at[p, pl.ds(half_rows, half_rows), other]),
+            ):
+                base = base_of[item]
+                copy(there, there, x_send.at[base + p], x_recv.at[base + p], at_x).wait_recv()
+
+            @pl.loop(0, units // TILE)
+            def _(j):
+                cols = pl.ds(pl.multiple_of(j * TILE, TILE), TILE)
+                gate = jnp.dot(norm_all[p], gate_w[:, cols], preferred_element_type=F32)
+                up = jnp.dot(norm_all[p], up_w[:, cols], preferred_element_type=F32)
+                grad = dot_t(cot_all[p], down_w[cols, :])
+                sig = jax.nn.sigmoid(gate)
+                act = gate * sig
+                acts[0, p, :, cols] = (act * up).astype(BF)
+                acts[1, p, :, cols] = (grad * up * sig * (1.0 + gate * (1.0 - sig))).astype(BF)
+                acts[2, p, :, cols] = (grad * act).astype(BF)
+
+            kinds = (
+                (acts.at[0, p], hid_hbm), (acts.at[1, p], gate_grad_hbm), (acts.at[2, p], up_grad_hbm),
+                (norm_all.at[p], norm_hbm), (cot_all.at[p], cot_hbm),
+            )
+            found = [
+                pltpu.make_async_copy(src, whole.at[p], act_sem.at[3 + i + 5 * len(kept)])
+                for i, (src, whole) in enumerate(kinds)
+            ]
+            for one in found:
+                one.start()
+            kept.append(found)
+
+        kept = []
+        forward_block(z)
+        forward_block(order[0])
+        step(NORM, last - 1)
+        step(LATE, last - 1)
+        for p in order[1:]:
+            forward_block(p)
+
+        for found in kept:
+            for one in found:
+                one.wait()
+        for one in unit_keeps + moves:
+            one.wait()
+        for one in [qkv_keep, out_keep]:
+            one.wait()
+        tok_copy_out = [half_copy, sq_copy, cot_copy] + norm_copies
         for one in gain_copies + sends + kv_sends + tok_copy_out:
             one.wait_send()
         spread_done(QKV, qkv_src)
         spread_done(OUT, out_src)
         spread_done(COT, cot)
-        spread_done(NORM, norm_own)
+        for item, src in norm_src.items():
+            spread_done(item, src)
         for p in order:
-            for item in (QKV, OUT, COT, NORM):
+            for item in (QKV, OUT, COT, NORM, LATE):
                 forward_done(item, p)
             for item in (QKV, OUT, GATE, UP, DOWN):
                 share_done(item, p)
-            x_copy(1 + p, slot(COT, p, c), slot(COT, p, c)).wait_send()
-            x_copy(3 + planes + p, slot(NORM, p, c), slot(NORM, p, c)).wait_send()
+            for item, base in base_of.items():
+                x_copy(base + p, slot(item, p, c), slot(item, p, c)).wait_send()
 
     hbm = pl.BlockSpec(memory_space=pl.ANY)
     vmem = pl.BlockSpec(memory_space=pltpu.VMEM)
@@ -497,6 +600,9 @@
             shape((planes, rows, width), BF),
             shape((width, qkv_cols), BF),
             shape((query_cols, width), BF),
+            shape((planes, rows, units), BF),
+            shape((planes, rows, units), BF),
+            shape((planes, rows, units), BF),
             shape((8, width), F32),
             shape((heads, rows, LANES), BF),
             shape((contexts, 2 * n_kv, rows, LANES), BF),
@@ -512,8 +618,20 @@
             shape((seq_len, 1), jnp.int32),
         ),
         in_specs=[vmem, hbm, vmem, vmem] + [hbm] * 7 + [pl.BlockSpec(memory_space=pltpu.SMEM), vmem],
-        out_specs=(hbm,) * 7 + (vmem,) * 13,
+        out_specs=(hbm,) * 10 + (vmem, hbm, hbm, hbm, vmem, hbm, hbm, hbm) + (vmem,) * 5,
         scratch_shapes=[
+            pltpu.VMEM((heads, rows, LANES), BF),
+            pltpu.VMEM((contexts, 2 * n_kv, rows, LANES), BF),
+            pltpu.VMEM((rows, query_cols), BF),
+            pltpu.VMEM((rows, half), F32),
+            pltpu.VMEM((rows, width), BF),
+            pltpu.VMEM((rows, width), BF),
+            pltpu.VMEM((width, units), BF),
+            pltpu.VMEM((width, units), BF),
+            pltpu.VMEM((units, width), BF),
+            pltpu.VMEM((planes, rows, width), BF),
+            pltpu.VMEM((planes, rows, width), BF),
+            pltpu.VMEM((3, planes, rows, units), BF),
             pltpu.VMEM((width, qkv_cols), BF),
             pltpu.VMEM((query_cols, width), BF),
             pltpu.VMEM((8, depth), F32),
@@ -524,15 +642,16 @@
             pltpu.VMEM((rows, half), BF),
             pltpu.VMEM((rows, LANES), F32),
             pltpu.VMEM((rows, LANES), F32),
-            dma((8, planes, planes)),
-            dma((8, planes)),
+            dma((9, planes, planes)),
+            dma((9, planes)),
             dma((6, planes, max(outers, 2))),
             dma((6, planes, max(outers, 2))),
             dma((6, planes, max(outers, 2))),
             dma((6, planes, max(outers, 2))),
-            dma((3 + 2 * planes,)),
-            dma((3 + 2 * planes,)),
+            dma((3 + 3 * planes,)),
+            dma((3 + 3 * planes,)),
             dma((9,)),
+            dma((9 + 5 * planes,)),
         ],
         compiler_params=pltpu.CompilerParams(
             collective_id=0, has_side_effects=True, vmem_limit_bytes=VMEM_LIMIT
@@ -731,10 +850,10 @@
     lots = max(outers - 1, 1)
 
     def kernel(
-        gate_hbm, up_hbm, down_hbm, norm_hbm, cot_hbm, qkv_hbm, out_hbm, q_hbm, kv_hbm, mid_hbm, tok_hbm,
+        gate_hbm, up_hbm, down_hbm, norm_hbm, cot_hbm, hid_hbm, gate_grad_hbm, up_grad_hbm, qkv_hbm, out_hbm, q_hbm, kv_hbm, mid_hbm, tok_hbm,
         gains, cosine, sine, pos_q, pos_k, log_sum, scales,
         input_grad, gate_strip, up_strip, down_out, mid_full, qkv_grad, gain_rows, mlp_part,
-        norm_x_in, norm_z_in, norm_x_out, norm_sum, mlp_stage,
+        norm_x_in, norm_z_in, norm_x_out, norm_sum, mlp_stage, hid, down_w,
         row_core_in, col_core_in, row_outer_in, col_outer_in, row_outer_out, col_outer_out, row_sum, col_sum,
         kv_core_in, kv_outer_in, sq_out, sq_in, first_x_out, first_x_in,
         x_send, x_recv, z_send, z_recv, k_send, k_recv, y_send, y_recv, grad_send, grad_recv, sy_send, sy_recv, sk_send,
@@ -783,16 +902,11 @@
 
         sems = (k_send, k_recv, y_send, y_recv)
 
-        def feed_forward(norm, cot, hid, gate_grad, up_grad):
+        def feed_forward(norm, cot, gate_grad, up_grad):
             def load(i, src, dst):
                 one = pltpu.make_async_copy(src, dst, load_sem.at[i])
                 one.start()
                 return one
-
-            loads = [
-                (load(2 * i, norm_hbm.at[p], norm.at[p]), load(2 * i + 1, cot_hbm.at[p], cot.at[p]))
-                for i, p in enumerate(blocks)
-            ]
 
             def product(part, left, right, size):
                 total = planes * rows
@@ -803,33 +917,23 @@
                     tile = t_dot(left[:, :, cols].reshape(total, size), right[...].reshape(total, right.shape[2]))
                     store_part(part, i, tile)
 
-            def with_weights(gate_w, up_w, down_w, col_part):
-                weights = [
-                    load(2 * planes, gate_hbm, gate_w),
-                    load(2 * planes + 1, up_hbm, up_w),
-                    load(2 * planes + 2, down_hbm, down_w),
+            def with_weights(gate_w, up_w, col_part):
+                weights = [load(0, gate_hbm, gate_w), load(1, up_hbm, up_w)]
+                loads = [
+                    (load(2 + 2 * i, gate_grad_hbm.at[p], gate_grad.at[p]), load(3 + 2 * i, up_grad_hbm.at[p], up_grad.at[p]))
+                    for i, p in enumerate(blocks)
+                ]
+                later = [
+                    load(2 + 2 * planes, hid_hbm, hid), load(3 + 2 * planes, cot_hbm, cot),
+                    load(4 + 2 * planes, norm_hbm, norm), load(5 + 2 * planes, down_hbm, down_w),
                 ]
                 for one in weights:
                     one.wait()
-                def forward_block(i):
-                    p = blocks[i]
-                    loads[i][0].wait()
-                    loads[i][1].wait()
-
-                    @pl.loop(0, units // TILE)
-                    def _(j):
-                        cols = pl.ds(pl.multiple_of(j * TILE, TILE), TILE)
-                        gate = jnp.dot(norm[p], gate_w[:, cols], preferred_element_type=F32)
-                        up = jnp.dot(norm[p], up_w[:, cols], preferred_element_type=F32)
-                        grad = dot_t(cot[p], down_w[cols, :])
-                        sig = jax.nn.sigmoid(gate)
-                        act = gate * sig
-                        hid[p, :, cols] = (act * up).astype(BF)
-                        gate_grad[p, :, cols] = (grad * up * sig * (1.0 + gate * (1.0 - sig))).astype(BF)
-                        up_grad[p, :, cols] = (grad * act).astype(BF)
 
                 def norm_block(i):
                     p = blocks[i]
+                    for one in loads[i]:
+                        one.wait()
 
                     def tile_of(at):
                         r = pl.ds(pl.multiple_of(at, WIDE), WIDE)
@@ -857,37 +961,22 @@
                 down = Reduction(
                     ring, DOWN, col_part, col_core_in, col_outer_out, col_outer_in, col_sum, sems
                 )
-                for i in range(planes):
-                    forward_block(i)
+                for i in range(planes - 2):
                     norm_block(i)
+                later[0].wait()
+                later[1].wait()
                 product(col_part, hid, cot, TILE)
                 down.to_core()
-                norm_on(planes - 2)
-                norm_z(blocks[planes - 2]).start()
-
-                def stage_copy(i):
-                    return pltpu.make_async_copy(mlp_stage.at[i % 2], mlp_part.at[blocks[i]], stage_sem.at[i % 2])
-
-                for i, p in enumerate(blocks):
-                    if i > 1:
-                        stage_copy(i - 2).wait()
-
-                    @pl.loop(0, width // WIDE)
-                    def _(j):
-                        r = pl.ds(pl.multiple_of(j * WIDE, WIDE), WIDE)
-                        mlp_stage[i % 2, :, r] = jnp.dot(hid[p], down_w[:, r], preferred_element_type=F32).astype(BF)
-
-                    stage_copy(i).start()
-                    if i == 0:
-                        down.from_core()
-                for i in range(max(planes - 2, 0), planes):
-                    stage_copy(i).wait()
+                norm_block(planes - 2)
+                down.from_core()
+                norm_block(planes - 1)
+                later[2].wait()
+                later[3].wait()
                 down.core_done()
 
             pl.run_scoped(
                 with_weights,
-                pltpu.VMEM((width, units), BF), pltpu.VMEM((width, units), BF), pltpu.VMEM((units, width), BF),
-                pltpu.VMEM((1, contexts, unit_strip, width), BF),
+                pltpu.VMEM((width, units), BF), pltpu.VMEM((width, units), BF), pltpu.VMEM((1, contexts, unit_strip, width), BF),
             )
 
             def with_parts(row_part):
@@ -899,13 +988,15 @@
                 )
                 product(row_part, norm, gate_grad, WIDE)
                 gate.to_core()
-                norm_on(planes - 1)
+                norm_on(planes - 2)
+                norm_z(blocks[planes - 2]).start()
                 gate.from_core()
                 gate.core_done()
                 pl.semaphore_signal(credit, inc=1, device_id=ring.at_k, device_id_type=MESH)
                 product(row_part, norm, up_grad, WIDE)
                 pl.semaphore_wait(credit, 1)
                 up.to_core()
+                norm_on(planes - 1)
                 up.from_core()
                 up.core_done()
 
@@ -913,7 +1004,7 @@
 
         block_bf = pltpu.VMEM((planes, rows, width), BF)
         unit_bf = pltpu.VMEM((planes, rows, units), BF)
-        pl.run_scoped(feed_forward, block_bf, block_bf, unit_bf, unit_bf, unit_bf)
+        pl.run_scoped(feed_forward, block_bf, block_bf, unit_bf, unit_bf)
 
         down = Reduction(ring, DOWN, None, None, col_outer_out, col_outer_in, col_sum, sems)
         gate = Reduction(ring, GATE, None, None, row_outer_out.at[0], row_outer_in.at[0], row_sum.at[0], sems)
@@ -955,7 +1046,10 @@
         share_sems = (sy_send, sy_recv, sk_send, sk_recv)
         down_share = Share(ring, 0, lambda q: down_out.at[:, q], share_sems)
 
-        def attention(mid_grad, q_pad, kv_all, tok, grad_pad, query_out, key_sum, value_sum, kv_grad, kv_out):
+        def stage_copy(i):
+            return pltpu.make_async_copy(mlp_stage.at[i % 2], mlp_part.at[blocks[i]], stage_sem.at[i % 2])
+
+        def attention(out_w, mid_keep, mid_grad, q_pad, kv_all, tok, grad_pad, query_out, key_sum, value_sum, kv_grad, kv_out):
             loads = [
                 pltpu.make_async_copy(mid_hbm, mid_grad, load_sem.at[0]),
                 pltpu.make_async_copy(tok_hbm.at[:, pl.ds(own_cols, half)], tok, load_sem.at[1]),
@@ -965,63 +1059,90 @@
             ]
             for one in loads:
                 one.start()
+            out_load = pltpu.make_async_copy(out_hbm, out_w, load_sem.at[5])
+            out_load.start()
             for one in loads:
                 one.wait()
             key_sum[...] = jnp.zeros_like(key_sum)
             value_sum[...] = jnp.zeros_like(value_sum)
             gain_rows[...] = jnp.zeros_like(gain_rows)
 
-            def norm_back(grad, normal, scale, gain, gain_row, i):
-                scaled = grad * gain
-                gain_rows[gain_row : gain_row + 1, :] = jnp.sum(grad * normal, 0, keepdims=True)
-                mine = jnp.sum(scaled * normal, -1, keepdims=True)
-                sq_out[i] = jnp.broadcast_to(mine, (rows, LANES))
+            def norm_back(grad_of, normal_of, finish, row, i):
+                gain = gains[row : row + 1, pl.ds(own_cols, half)]
+
+                def chunk(j):
+                    return pl.ds(pl.multiple_of(j * STEP, STEP), STEP)
+
+                @pl.loop(0, rows // STEP)
+                def _(j):
+                    r = chunk(j)
+                    grad, normal = grad_of(r), normal_of(r)
+                    both = grad * normal
+                    gain_rows[row : row + 1, :] += jnp.sum(both, 0, keepdims=True)
+                    sq_out[i, r, :] = jnp.broadcast_to(jnp.sum(both * gain, -1, keepdims=True), (STEP, LANES))
+
                 swap = x_copy(SQ_TWO if i == 0 else SQ_ONE, sq_out.at[i], sq_in.at[i])
                 swap.start()
                 swap.wait()
-                inner = (mine + sq_in[i][:, 0:1]) * (1.0 / width)
-                return scale * (scaled - normal * inner)
+
+                @pl.loop(0, rows // STEP)
+                def _(j):
+                    r = chunk(j)
+                    inner = (sq_out[i, r, 0:1] + sq_in[i, r, 0:1]) * (1.0 / width)
+                    finish(r, scales[row, r, 0:1] * (grad_of(r) * gain - normal_of(r) * inner))
 
             for p in order:
                 norm_z_wait(p)
-            grad = norm_sum[z].astype(F32)
-            for p in order:
-                grad = grad + norm_z_in[back_from(p, z)].astype(F32)
-            scale_two = scales[1][:, 0:1]
-            gain_two = gains[1:2, pl.ds(own_cols, half)].astype(F32)
-            back = norm_back(grad, mid_grad[...] * scale_two, scale_two, gain_two, 1, 0)
-            mid_grad[...] = first_x_out[...].astype(F32) + back
+
+            def norm_grad_of(r):
+                grad = norm_sum[z, r, :].astype(F32)
+                for i in range(planes - 1):
+                    grad = grad + norm_z_in[i, r, :].astype(F32)
+                return grad
+
+            def mid_finish(r, back):
+                found = first_x_out[r, :].astype(F32) + back
+                mid_keep[r, :] = found
+                mid_full[r, pl.ds(own_cols, half)] = found.astype(BF)
+
+            norm_back(norm_grad_of, lambda r: mid_grad[r, :] * scales[1, r, 0:1], mid_finish, 1, 0)
             mine = mid_full.at[:, pl.ds(own_cols, half)]
-            mid_full[:, pl.ds(own_cols, half)] = mid_grad[...].astype(BF)
             mid_swap = x_copy(MID, mine, mine)
             mid_swap.start()
+            for i, p in enumerate(blocks):
+                if i > 1:
+                    stage_copy(i - 2).wait()
+
+                @pl.loop(0, width // WIDE)
+                def _(j):
+                    r = pl.ds(pl.multiple_of(j * WIDE, WIDE), WIDE)
+                    mlp_stage[i % 2, :, r] = jnp.dot(hid[p], down_w[:, r], preferred_element_type=F32).astype(BF)
+
+                stage_copy(i).start()
             to_planes(DOWN, down)
             mid_swap.wait_recv()
+            out_load.wait()
 
             lane = lax.broadcasted_iota(jnp.int32, (rows, LANES), 1)
             first = lax.rem(lane, HEAD_WIDTH) < HEAD_WIDTH // 2
             low = lane < HEAD_WIDTH
 
-            def with_out(out_w):
-                one = pltpu.make_async_copy(out_hbm, out_w, load_sem.at[0])
-                one.start()
-                one.wait()
-
-                @pl.loop(0, query_cols // TILE)
-                def _(i):
-                    r = pl.ds(pl.multiple_of(i * TILE, TILE), TILE)
-                    found = dot_t(mid_full[...], out_w[r, :])
-                    for half_tile in range(TILE // LANES):
-                        j = i * (TILE // LANES) + half_tile
-                        u = found[:, half_tile * LANES : (half_tile + 1) * LANES]
-                        u = u.astype(BF).astype(F32)
-                        side = lax.rem((2 * j) // group, 2)
-                        lo = jnp.where(low, u, 0.0)
-                        hi = jnp.where(low, 0.0, u)
-                        grad_pad[2 * j] = jnp.where(side == 0, lo, pltpu.roll(lo, HEAD_WIDTH, 1)).astype(BF)
-                        grad_pad[2 * j + 1] = jnp.where(side == 1, hi, pltpu.roll(hi, HEAD_WIDTH, 1)).astype(BF)
-
-            pl.run_scoped(with_out, pltpu.VMEM((query_cols, width), BF))
+            @pl.loop(0, query_cols // TILE)
+            def _(i):
+                r = pl.ds(pl.multiple_of(i * TILE, TILE), TILE)
+                found = dot_t(mid_full[...], out_w[r, :])
+                for half_tile in range(TILE // LANES):
+                    j = i * (TILE // LANES) + half_tile
+                    u = found[:, half_tile * LANES : (half_tile + 1) * LANES]
+                    u = u.astype(BF).astype(F32)
+                    side = lax.rem((2 * j) // group, 2)
+                    lo = jnp.where(low, u, 0.0)
+                    hi = jnp.where(low, 0.0, u)
+                    grad_pad[2 * j] = jnp.where(side == 0, lo, pltpu.roll(lo, HEAD_WIDTH, 1)).astype(BF)
+                    grad_pad[2 * j + 1] = jnp.where(side == 1, hi, pltpu.roll(hi, HEAD_WIDTH, 1)).astype(BF)
+
+            for i in range(max(planes - 2, 0), planes):
+                stage_copy(i).wait()
 
             def attend_back(first_head, last_head):
                 @pl.loop(first_head, last_head)
@@ -1046,59 +1167,60 @@
                 kv_grad[:, i] = key_sum[i].astype(BF).reshape(contexts, rows, LANES)
                 kv_grad[:, n_kv + i] = value_sum[i].astype(BF).reshape(contexts, rows, LANES)
 
-            def kv_core(other):
-                return copy_to(
-                    kv_grad.at[other * 2 + 1 - k], kv_core_in.at[other], k_send.at[KV, other], k_recv.at[KV, other],
-                    ring.at_k,
-                )
-
-            def kv_outer(by):
-                return copy_to(
-                    kv_out.at[by - 1], kv_outer_in.at[by - 1], y_send.at[KV, by], y_recv.at[KV, by],
-                    ring.at_o(ring.after(by)),
-                )
-
-            for other in range(outers):
-                kv_core(other).start()
-            for j in range(n_q):
-                side = (2 * j) // group % 2
-                lo, hi = query_out[2 * j], query_out[2 * j + 1]
-                if side == 0:
-                    hi = pltpu.roll(hi, HEAD_WIDTH, 1)
-                else:
-                    lo = pltpu.roll(lo, HEAD_WIDTH, 1)
-                u = jnp.where(low, lo, hi) * FACTOR
-                qkv_grad[:, j * LANES : (j + 1) * LANES] = rotate_tile(u, cosine[...], -sine[...], first).astype(BF)
-            for other in range(outers):
-                kv_core(other).wait_recv()
-            for by in range(1, outers):
-                goal = ring.after(by)
-                kv_out[by - 1] = (
-                    kv_grad[goal * 2 + k].astype(F32) + kv_core_in[goal].astype(F32)
-                ).astype(BF)
-                kv_outer(by).start()
-            to_planes(UP, up)
-            from_planes(DOWN)
-            down_share.start()
-            kv_sum = kv_grad[c].astype(F32) + kv_core_in[o].astype(F32)
-            for by in range(1, outers):
-                kv_outer(by).wait_recv()
-                kv_sum = kv_sum + kv_outer_in[by - 1].astype(F32)
-            for i in range(n_kv):
-                at = query_cols + i * LANES
-                qkv_grad[:, at : at + LANES] = rotate_tile(kv_sum[i], cosine[...], -sine[...], first).astype(BF)
-                qkv_grad[:, at + kv_cols : at + kv_cols + LANES] = kv_sum[n_kv + i].astype(BF)
-            for other in range(outers):
-                kv_core(other).wait_send()
-            for by in range(1, outers):
-                kv_outer(by).wait_send()
-
             first_swap = x_copy(FIRST, first_x_out, first_x_in)
 
             def with_qkv(qkv_w, own):
-                one = pltpu.make_async_copy(qkv_hbm, qkv_w, load_sem.at[0])
-                one.start()
-                one.wait()
+                qkv_load = pltpu.make_async_copy(qkv_hbm, qkv_w, load_sem.at[0])
+                qkv_load.start()
+
+                def kv_core(other):
+                    return copy_to(
+                        kv_grad.at[other * 2 + 1 - k], kv_core_in.at[other], k_send.at[KV, other], k_recv.at[KV, other],
+                        ring.at_k,
+                    )
+
+                def kv_outer(by):
+                    return copy_to(
+                        kv_out.at[by - 1], kv_outer_in.at[by - 1], y_send.at[KV, by], y_recv.at[KV, by],
+                        ring.at_o(ring.after(by)),
+                    )
+
+                for other in range(outers):
+                    kv_core(other).start()
+                for j in range(n_q):
+                    side = (2 * j) // group % 2
+                    lo, hi = query_out[2 * j], query_out[2 * j + 1]
+                    if side == 0:
+                        hi = pltpu.roll(hi, HEAD_WIDTH, 1)
+                    else:
+                        lo = pltpu.roll(lo, HEAD_WIDTH, 1)
+                    u = jnp.where(low, lo, hi) * FACTOR
+                    qkv_grad[:, j * LANES : (j + 1) * LANES] = rotate_tile(u, cosine[...], -sine[...], first).astype(BF)
+                for other in range(outers):
+                    kv_core(other).wait_recv()
+                for by in range(1, outers):
+                    goal = ring.after(by)
+                    kv_out[by - 1] = (
+                        kv_grad[goal * 2 + k].astype(F32) + kv_core_in[goal].astype(F32)
+                    ).astype(BF)
+                    kv_outer(by).start()
+                to_planes(UP, up)
+                from_planes(DOWN)
+                down_share.start()
+                kv_sum = kv_grad[c].astype(F32) + kv_core_in[o].astype(F32)
+                for by in range(1, outers):
+                    kv_outer(by).wait_recv()
+                    kv_sum = kv_sum + kv_outer_in[by - 1].astype(F32)
+                for i in range(n_kv):
+                    at = query_cols + i * LANES
+                    qkv_grad[:, at : at + LANES] = rotate_tile(kv_sum[i], cosine[...], -sine[...], first).astype(BF)
+                    qkv_grad[:, at + kv_cols : at + kv_cols + LANES] = kv_sum[n_kv + i].astype(BF)
+                for other in range(outers):
+                    kv_core(other).wait_send()
+                for by in range(1, outers):
+                    kv_outer(by).wait_send()
+
+                qkv_load.wait()
 
                 def tile_of(at):
                     return dot_t(qkv_grad[...], qkv_w[pl.ds(pl.multiple_of(at, WIDE), WIDE), :])
@@ -1116,12 +1238,15 @@
                     own[:, here] = tile_of(own_cols + j * WIDE)
 
                 first_swap.wait()
-                scale_one = scales[0][:, 0:1]
-                gain_one = gains[0:1, pl.ds(own_cols, half)].astype(F32)
-                back = norm_back(
-                    own[...] + first_x_in[...].astype(F32), tok[...].astype(F32) * scale_one, scale_one, gain_one, 0, 1
+
+                def input_finish(r, back):
+                    input_grad[r, :] = (mid_keep[r, :] + back).astype(BF)
+
+                norm_back(
+                    lambda r: own[r, :] + first_x_in[r, :].astype(F32),
+                    lambda r: tok[r, :].astype(F32) * scales[0, r, 0:1],
+                    input_finish, 0, 1,
                 )
-                input_grad[...] = (mid_grad[...] + back).astype(BF)
 
             pl.run_scoped(with_qkv, pltpu.VMEM((width, qkv_cols), BF), pltpu.VMEM((rows, half), F32))
             mid_swap.wait_send()
@@ -1129,6 +1254,8 @@
         tile_f32 = pltpu.VMEM((rows, half), F32)
         pl.run_scoped(
             attention,
+            pltpu.VMEM((query_cols, width), BF),
+            tile_f32,
             tile_f32,
             pltpu.VMEM((heads, rows, LANES), BF),
             pltpu.VMEM((contexts, 2 * n_kv, rows, LANES), BF),
@@ -1161,6 +1288,7 @@
     shape = jax.ShapeDtypeStruct
     acts = pltpu.VMEM((planes, rows, half), BF)
     arrivals = pltpu.VMEM((planes - 1, rows, half), BF)
+    unit_acts = pltpu.VMEM((planes, rows, units), BF)
     return pl.pallas_call(
         kernel,
         name="back",
@@ -1174,9 +1302,9 @@
             shape((8, half), F32),
             shape((planes, rows, width), BF),
         ),
-        in_specs=[hbm] * 11 + [vmem] * 7,
+        in_specs=[hbm] * 14 + [vmem] * 7,
         out_specs=(vmem, hbm, hbm, hbm, vmem, vmem, vmem, hbm),
-        scratch_shapes=[acts, arrivals, pltpu.VMEM((2, rows, half), BF), acts, pltpu.VMEM((2, rows, width), BF)]
+        scratch_shapes=[acts, arrivals, pltpu.VMEM((2, rows, half), BF), acts, pltpu.VMEM((2, rows, width), BF), unit_acts, pltpu.VMEM((units, width), BF)]
         + [
             pltpu.VMEM((outers, planes, strip, units), BF),
             pltpu.VMEM((outers, 1, unit_strip, width), BF),
@@ -1206,7 +1334,7 @@
             dma((2, max(outers, 2))),
             dma((2, outers)),
             dma((2, outers)),
-            dma((2 * planes + 3,)),
+            dma((2 * planes + 6,)),
             dma((2,)),
             pltpu.SemaphoreType.REGULAR,
         ],
@@ -1528,14 +1656,14 @@
 
     freqs = jnp.tile(rope_freqs(HEAD_WIDTH), LANES // (HEAD_WIDTH // 2))[None]
     (
-        gate_w, up_w, down_w, cot_all, norm_all, qkv_w, out_w, gains, q_pad, kv_all, attn, log_sum, mid_own,
+        gate_w, up_w, down_w, cot_all, norm_all, qkv_w, out_w, hid, gate_grad, up_grad, gains, q_pad, kv_all, attn, log_sum, mid_own,
         normed_one, tok_all, scales, cosine_table, sine_table, pos_q, pos_k,
     ) = build_front(*sizes)(
         tok_own, cot_own, attn_gain[None], mlp_gain[None], w_query, key_weight, value_weight, w_out, w_gate, w_up,
         w_down, span_order, freqs,
     )
     input_grad, gate_strip, up_strip, down_out, mid_full, qkv_grad, gain_rows, mlp_part = build_back(*sizes)(
-        gate_w, up_w, down_w, norm_all, cot_all, qkv_w, out_w, q_pad, kv_all, mid_own, tok_all, gains,
+        gate_w, up_w, down_w, norm_all, cot_all, hid, gate_grad, up_grad, qkv_w, out_w, q_pad, kv_all, mid_own, tok_all, gains,
         cosine_table, sine_table, pos_q, pos_k, log_sum, scales,
     )
     gate_out, up_out, out_out, qkv_out, gain_out, result = build_grads(*sizes)(

time: 523 us -> 518 us (level)
  Pallas kernels: 491 us -> 485 us
    pallas_call x1, Pallas kernels: 158 us -> 143 us  [shards(): build_back(*sizes)]
    pallas_call x1, Pallas kernels: 127 us -> 138 us  [shards(): build_grads(*sizes)]
where the time goes in v6:
time: 518 us; the launch traced here: 514 us
  Pallas kernels  485 us (94%)
  other arithmetic  15.5 us (3%)
  local copies, waits for them, and re-layouts  12.5 us (2%)
    pallas_call x1, Pallas kernels, shards(): build_front(*sizes)  205 us
    pallas_call x1, Pallas kernels, shards(): build_back(*sizes)  143 us
    pallas_call x1, Pallas kernels, shards(): build_grads(*sizes)  138 us

profile of v6, /device:TPU:0, one launch (start us, length us, event | category | flops | bytes accessed | tf_op | source)
XLA Modules:
  0.0 513.9 jit_solution(4982670532476099221)
XLA Ops:
  0.7 0.6 broadcast_in_dim_tile.3.freqs
  1.3 1.3 copy.23.spans
  2.6 1.3 broadcast_in_dim.12.gain_one_own
  3.9 1.3 broadcast_in_dim.13.gain_two_own
  5.1 204.6 %front.1 = (bf16[2048,1024]{1,0:T(8,128)(2,1)}, bf16[2048,1024]{1,0:T(8,128)(2,1)}, bf16[1024,2048]{1,0:T(8,128)(2,1)}, bf16[4,256,2048]{2,1,0:T(8,128)(2,1)}, b...) custom-call(bf16[256,1024]{1,0:T(8,128)(2,1)} %bitcast.13, ...), custom_call_target="tpu_custom_call" | custom-call | flops 8000000000 | bytes 80000000 | tf_op jit(solution)/shard_map/front/pallas_call | solution.py:1661
  209.8 142.7 %back.1 = (bf16[256,1024]{1,0:T(8,128)(2,1)}, bf16[128,4096]{1,0:T(8,128)(2,1)}, bf16[128,4096]{1,0:T(8,128)(2,1)}, bf16[4,4,256,512]{3,2,1,0:T(8,128)(2,1)}, bf...) custom-call(bf16[2048,1024]{1,0:T(8,128)(2,1)} %get-tuple-element.49.gat, ...), custom_call_target="tpu_custom_call" | custom-call | flops 49999998976 | bytes 80000000 | tf_op jit(solution)/shard_map/back/pallas_call | solution.py:1665
  352.5 137.9 %grads.1 = (bf16[512,4096]{1,0:T(8,128)(2,1)}, bf16[512,4096]{1,0:T(8,128)(2,1)}, bf16[1024,512]{1,0:T(8,128)(2,1)}, bf16[512,1536]{1,0:T(8,128)(2,1)}, f32[8,512]{1,0:T(8,128)}, /*index=5*/bf16[256,1024]{1,0:T(8,128)(2,1)}) custom-call(bf16[256,1024]{1,0:T(8,128)(2,1)} %get-tuple-element.48.attn, bf16[256,2048]{1,0:T(8,128)(2,1)} %get-tuple-element.70.mid_full, ...), custom_call_target="tpu_custom_call" | custom-call | flops 4000000000 | bytes 40000000 | tf_op jit(solution)/shard_map/grads/pallas_call | solution.py:1669
  490.4 0.0 copy-start.3
  490.4 1.4 fusion.1
  491.8 2.1 fusion
  493.9 0.0 copy-start.2
  493.9 2.9 slice.20
  496.8 0.0 copy-done.3
  496.8 1.6 convert_element_type.19
  498.4 0.0 copy-done.2
  498.4 0.0 copy-start.1
  498.4 4.5 convert_element_type.20
  502.9 0.0 copy-done.1
  502.9 0.0 copy-start
  502.9 4.5 convert_element_type.21
  507.4 0.0 copy-done
  507.4 0.0 copy-start.5
  507.4 0.0 copy-start.4
  507.4 4.9 bitcast_convert_fusion
  512.3 0.0 copy-done.5
  512.3 0.8 copy.26
  513.1 0.0 copy-done.4
  513.1 0.8 copy.27
  (2 shorter events, 0.0 us)
Async XLA Ops:
  490.4 6.4 %copy-start.3 = (bf16[1024,512]{1,0:T(8,128)(2,1)S(1)}, bf16[1024,512]{1,0:T(8,128)(2,1)}, u32[]{:S(2)}) copy-start(bf16[1024,512]{1,0:T(8,128)(2,1)} %get-tuple-element.81) | copy-start | bytes 3145732
  493.9 4.6 copy-start.2
  498.4 4.5 copy-start.1
  502.9 4.5 copy-start
  507.4 4.9 copy-start.5
  507.4 5.7 %copy-start.4 = (bf16[256,1024]{1,0:T(8,128)(2,1)S(1)}, bf16[256,1024]{1,0:T(8,128)(2,1)}, u32[]{:S(2)}) copy-start(bf16[256,1024]{1,0:T(8,128)(2,1)} %get-tuple-element.78) | copy-start | bytes 1572868

commit v7 on v6

--- a/solution.py
+++ b/solution.py
@@ -53,7 +53,8 @@
     heads = query_cols // HEAD_WIDTH
     group = query_cols // kv_cols
     qkv_cols = query_cols + 2 * kv_cols
-    QKV, OUT, GATE, UP, DOWN, COT, NORM, GAIN, LATE = range(9)
+    QKV, OUT, GATE, UP, DOWN, COT, NORM, GAIN, LATE, MORE = range(10)
+    half_strip = strip // 2
     half_rows = rows // 2
     base_of = {COT: 1, NORM: 3 + planes, LATE: 3 + 2 * planes}
 
@@ -102,8 +103,9 @@
             order.append(p)
 
         def slot(item, p, q):
-            if item == QKV:
-                return qkv_w.at[pl.ds(p * depth + q * strip, strip), :]
+            if item in (QKV, MORE):
+                skip = 0 if item == QKV else half_strip
+                return qkv_w.at[pl.ds(p * depth + q * strip + skip, half_strip), :]
             if item == OUT:
                 return out_w.at[pl.ds(q * out_strip, out_strip), pl.ds(p * depth, depth)]
             if item == GATE:
@@ -220,9 +222,9 @@
             one.start()
         for one in own_qkv:
             one.wait()
-        qkv_src = slot(QKV, z, c)
         out_src = out_own.at[pl.ds(c * out_strip, out_strip), :]
-        spread(QKV, qkv_src)
+        for item in (QKV, MORE):
+            spread(item, slot(item, z, c))
         own_copies = [
             pltpu.make_async_copy(out_own, out_w.at[:, pl.ds(z * depth, depth)], own_sem.at[1]),
             pltpu.make_async_copy(
@@ -242,19 +244,23 @@
         tok_all[:, tok_cols] = tok[...]
 
         def at_distance(i, act):
-            for p in (z - (i + 1), z + (i + 1)):
+            lower, upper = z - (i + 1), z + (i + 1)
+            inner = z < planes // 2
+            for p in (jnp.where(inner, upper, lower), jnp.where(inner, lower, upper)):
 
                 @pl.when((p >= 0) & (p < planes))
                 def _(p=p):
                     act(p)
 
         def qkv_step(i):
-            def act(p):
-                z_wait(QKV, p)
-                forward(QKV, p)
-                share(QKV, p)
-
-            at_distance(i, act)
+            for item in (QKV, MORE):
+
+                def act(p, item=item):
+                    z_wait(item, p)
+                    forward(item, p)
+                    share(item, p)
+
+                at_distance(i, act)
 
         qkv_step(0)
 
@@ -330,9 +336,11 @@
         cot_copy = x_copy(1 + z, cot, slot(COT, z, c))
         cot_copy.start()
         for p in order:
-            share_on(QKV, p)
+            for item in (QKV, MORE):
+                share_on(item, p)
         for p in order:
-            shared(QKV, p)
+            for item in (QKV, MORE):
+                shared(item, p)
         qkv_keep = pltpu.make_async_copy(qkv_w, qkv_hbm, own_sem.at[0])
         qkv_keep.start()
 
@@ -572,15 +580,16 @@
         tok_copy_out = [half_copy, sq_copy, cot_copy] + norm_copies
         for one in gain_copies + sends + kv_sends + tok_copy_out:
             one.wait_send()
-        spread_done(QKV, qkv_src)
+        for item in (QKV, MORE):
+            spread_done(item, slot(item, z, c))
         spread_done(OUT, out_src)
         spread_done(COT, cot)
         for item, src in norm_src.items():
             spread_done(item, src)
         for p in order:
-            for item in (QKV, OUT, COT, NORM, LATE):
+            for item in (QKV, MORE, OUT, COT, NORM, LATE):
                 forward_done(item, p)
-            for item in (QKV, OUT, GATE, UP, DOWN):
+            for item in (QKV, MORE, OUT, GATE, UP, DOWN):
                 share_done(item, p)
             for item, base in base_of.items():
                 x_copy(base + p, slot(item, p, c), slot(item, p, c)).wait_send()
@@ -642,12 +651,12 @@
             pltpu.VMEM((rows, half), BF),
             pltpu.VMEM((rows, LANES), F32),
             pltpu.VMEM((rows, LANES), F32),
-            dma((9, planes, planes)),
-            dma((9, planes)),
-            dma((6, planes, max(outers, 2))),
-            dma((6, planes, max(outers, 2))),
-            dma((6, planes, max(outers, 2))),
-            dma((6, planes, max(outers, 2))),
+            dma((10, planes, planes)),
+            dma((10, planes)),
+            dma((10, planes, max(outers, 2))),
+            dma((10, planes, max(outers, 2))),
+            dma((10, planes, max(outers, 2))),
+            dma((10, planes, max(outers, 2))),
             dma((3 + 3 * planes,)),
             dma((3 + 3 * planes,)),
             dma((9,)),

time: 518 us -> 511 us (0.986)
  Pallas kernels: 485 us -> 479 us
where the time goes in v7:
time: 511 us; the launch traced here: 508 us
  Pallas kernels  479 us (94%)
  other arithmetic  15.5 us (3%)
  local copies, waits for them, and re-layouts  12.5 us (2%)
    pallas_call x1, Pallas kernels, shards(): build_front(*sizes)  200 us
    pallas_call x1, Pallas kernels, shards(): build_back(*sizes)  141 us
    pallas_call x1, Pallas kernels, shards(): build_grads(*sizes)  138 us

profile of v7, /device:TPU:0, one launch (start us, length us, event | category | flops | bytes accessed | tf_op | source)
XLA Modules:
  0.0 507.9 jit_solution(4895968180639246632)
XLA Ops:
  0.7 0.6 broadcast_in_dim_tile.3.freqs
  1.3 1.3 copy.23.spans
  2.6 1.3 broadcast_in_dim.12.gain_one_own
  3.9 1.3 broadcast_in_dim.13.gain_two_own
  5.1 200.1 %front.1 = (bf16[2048,1024]{1,0:T(8,128)(2,1)}, bf16[2048,1024]{1,0:T(8,128)(2,1)}, bf16[1024,2048]{1,0:T(8,128)(2,1)}, bf16[4,256,2048]{2,1,0:T(8,128)(2,1)}, b...) custom-call(bf16[256,1024]{1,0:T(8,128)(2,1)} %bitcast.13, ...), custom_call_target="tpu_custom_call" | custom-call | flops 8000000000 | bytes 80000000 | tf_op jit(solution)/shard_map/front/pallas_call | solution.py:1670
  205.2 141.3 %back.1 = (bf16[256,1024]{1,0:T(8,128)(2,1)}, bf16[128,4096]{1,0:T(8,128)(2,1)}, bf16[128,4096]{1,0:T(8,128)(2,1)}, bf16[4,4,256,512]{3,2,1,0:T(8,128)(2,1)}, bf...) custom-call(bf16[2048,1024]{1,0:T(8,128)(2,1)} %get-tuple-element.49.gat, ...), custom_call_target="tpu_custom_call" | custom-call | flops 49999998976 | bytes 80000000 | tf_op jit(solution)/shard_map/back/pallas_call | solution.py:1674
  346.5 138.0 %grads.1 = (bf16[512,4096]{1,0:T(8,128)(2,1)}, bf16[512,4096]{1,0:T(8,128)(2,1)}, bf16[1024,512]{1,0:T(8,128)(2,1)}, bf16[512,1536]{1,0:T(8,128)(2,1)}, f32[8,512]{1,0:T(8,128)}, /*index=5*/bf16[256,1024]{1,0:T(8,128)(2,1)}) custom-call(bf16[256,1024]{1,0:T(8,128)(2,1)} %get-tuple-element.48.attn, bf16[256,2048]{1,0:T(8,128)(2,1)} %get-tuple-element.70.mid_full, ...), custom_call_target="tpu_custom_call" | custom-call | flops 4000000000 | bytes 40000000 | tf_op jit(solution)/shard_map/grads/pallas_call | solution.py:1678
  484.4 0.0 copy-start.3
  484.4 1.4 fusion.1
  485.8 2.1 fusion
  487.9 0.0 copy-start.2
  487.9 2.9 slice.20
  490.9 0.0 copy-done.3
  490.9 1.6 convert_element_type.19
  492.5 0.0 copy-done.2
  492.5 0.0 copy-start.1
  492.5 4.5 convert_element_type.20
  497.0 0.0 copy-done.1
  497.0 0.0 copy-start
  497.0 4.5 convert_element_type.21
  501.5 0.0 copy-done
  501.5 0.0 copy-start.5
  501.5 0.0 copy-start.4
  501.5 4.9 bitcast_convert_fusion
  506.3 0.0 copy-done.5
  506.3 0.8 copy.26
  507.1 0.0 copy-done.4
  507.1 0.8 copy.27
  (2 shorter events, 0.0 us)
Async XLA Ops:
  484.4 6.4 %copy-start.3 = (bf16[1024,512]{1,0:T(8,128)(2,1)S(1)}, bf16[1024,512]{1,0:T(8,128)(2,1)}, u32[]{:S(2)}) copy-start(bf16[1024,512]{1,0:T(8,128)(2,1)} %get-tuple-element.81) | copy-start | bytes 3145732
  487.9 4.6 copy-start.2
  492.5 4.5 copy-start.1
  497.0 4.5 copy-start
  501.5 4.9 copy-start.5
  501.5 5.7 %copy-start.4 = (bf16[256,1024]{1,0:T(8,128)(2,1)S(1)}, bf16[256,1024]{1,0:T(8,128)(2,1)}, u32[]{:S(2)}) copy-start(bf16[256,1024]{1,0:T(8,128)(2,1)} %get-tuple-element.78) | copy-start | bytes 1572868
